TPU v7x, 32 devices: a whole 2x2x4 slice. The times are simulated.
32 devices in a mesh: fsdp: 16 (over z, y, x), seq: 2 (over core).
Axes of the slice: x: 2, y: 2, z: 4, core: 2. Of those that a mesh axis runs over, the one named last changes fastest.
Arguments:
- latents: bfloat16 [16, 256, 768], P('fsdp', 'seq'), may hold values from -6 to 6
- time_ids: int32 [16], P('fsdp'), may hold values from 0 to 1023
- class_ids: int32 [16], P('fsdp'), may hold values from 0 to 1023
- time_table: bfloat16 [1024, 768], P(('fsdp', 'seq')), may hold values from -6 to 6
- class_table: bfloat16 [1024, 768], P(('fsdp', 'seq')), may hold values from -6 to 6
- ada_w: bfloat16 [768, 4608], P(('fsdp', 'seq')), may hold values from -0.21875 to 0.21875
- ada_b: bfloat16 [4608], P(('fsdp', 'seq')), may hold values from -3 to 3
- qkv_w: bfloat16 [768, 2304], P(('fsdp', 'seq')), may hold values from -0.21875 to 0.21875
- qv_b: bfloat16 [1536], P(('fsdp', 'seq')), may hold values from -3 to 3
- proj_w: bfloat16 [768, 768], P(('fsdp', 'seq')), may hold values from -0.625 to 0.625
- proj_b: bfloat16 [768], P(('fsdp', 'seq')), may hold values from -3 to 3
- first_feedforward_weight: bfloat16 [768, 3072], P(('fsdp', 'seq')), may hold values from -0.21875 to 0.21875
- first_feedforward_bias: bfloat16 [3072], P(('fsdp', 'seq')), may hold values from -3 to 3
- second_feedforward_weight: bfloat16 [3072, 768], P(('fsdp', 'seq')), may hold values from -0.109375 to 0.109375
- second_feedforward_bias: bfloat16 [768], P(('fsdp', 'seq')), may hold values from -3 to 3
- cotangent: bfloat16 [16, 256, 768], P('fsdp', 'seq'), may hold values from -6 to 6
Outputs:
- output: bfloat16 [16, 256, 768], P('fsdp', 'seq')
- latents_grad: float32 [16, 256, 768], P('fsdp', 'seq')
- time_table_grad: float32 [1024, 768], P(('fsdp', 'seq'))
- class_table_grad: float32 [1024, 768], P(('fsdp', 'seq'))
- ada_w_grad: float32 [768, 4608], P(('fsdp', 'seq'))
- ada_b_grad: float32 [4608], P(('fsdp', 'seq'))
- qkv_w_grad: float32 [768, 2304], P(('fsdp', 'seq'))
- qv_b_grad: float32 [1536], P(('fsdp', 'seq'))
- proj_w_grad: float32 [768, 768], P(('fsdp', 'seq'))
- proj_b_grad: float32 [768], P(('fsdp', 'seq'))
- fc1_w_grad: float32 [768, 3072], P(('fsdp', 'seq'))
- fc1_b_grad: float32 [3072], P(('fsdp', 'seq'))
- fc2_w_grad: float32 [3072, 768], P(('fsdp', 'seq'))
- fc2_b_grad: float32 [768], P(('fsdp', 'seq'))
All inputs are finite; a program needn't handle non-finite values.
Results may differ from a plain program's by a relative error of at most 0.028.
Values may be sent and summed in bfloat16 or wider, within the bound.
No kernel may reach another device: no remote copies, remote signals or barrier semaphores. Data moves between devices by JAX's collectives and lax.ppermute only.
A program may use at most 192 MiB of HBM per device.

v0:
```python
import jax
import jax.numpy as jnp
from jax import lax
from jax.sharding import PartitionSpec as P

HD = 64


norm_eps = 1e-06
highest = lax.Precision.HIGHEST


def layer_norm(stream):
    center = stream - jnp.mean(stream, -1, keepdims=True)
    spread = jnp.mean(center * center, -1, keepdims=True)
    return center * lax.rsqrt(spread + norm_eps)


def modulate(stream, shift_part, scale_part):
    return layer_norm(stream) * (1.0 + scale_part) + shift_part


def gelu_tanh(preactivation_values):
    return jax.nn.gelu(preactivation_values, approximate=True)


def split_heads(tensor):
    return tensor.reshape(tensor.shape[0], tensor.shape[1], tensor.shape[2] // HD, HD)


def scores_of(q_heads, k_heads):
    return jnp.einsum(
        "lqhd,lkhd->lhqk", q_heads, k_heads, preferred_element_type=jnp.float32
    ) * HD ** (-0.5)


def one_hot(ids, rows):
    columns = lax.broadcasted_iota(jnp.int32, (ids.shape[0], rows), 1)
    return (ids[:, None] == columns).astype(jnp.bfloat16)


def shards(
    latents,
    time_ids,
    class_ids,
    time_table,
    class_table,
    ada_w,
    ada_b,
    qkv_w,
    qv_b,
    proj_w,
    proj_b,
    first_feedforward_weight,
    first_feedforward_bias,
    second_feedforward_weight,
    second_feedforward_bias,
    cotangent,
):
    gathered = (
        lax.all_gather(time_table, ("fsdp", "seq"), axis=0, tiled=True),
        lax.all_gather(class_table, ("fsdp", "seq"), axis=0, tiled=True),
        lax.all_gather(ada_w, ("fsdp", "seq"), axis=0, tiled=True),
        lax.all_gather(ada_b, ("fsdp", "seq"), axis=0, tiled=True),
        lax.all_gather(qkv_w, ("fsdp", "seq"), axis=0, tiled=True),
        lax.all_gather(qv_b, ("fsdp", "seq"), axis=0, tiled=True),
        lax.all_gather(proj_w, ("fsdp", "seq"), axis=0, tiled=True),
        lax.all_gather(proj_b, ("fsdp", "seq"), axis=0, tiled=True),
        lax.all_gather(first_feedforward_weight, ("fsdp", "seq"), axis=0, tiled=True),
        lax.all_gather(first_feedforward_bias, ("fsdp", "seq"), axis=0, tiled=True),
        lax.all_gather(second_feedforward_weight, ("fsdp", "seq"), axis=0, tiled=True),
        lax.all_gather(second_feedforward_bias, ("fsdp", "seq"), axis=0, tiled=True),
    )
    (
        time_full,
        class_full,
        ada_full,
        ada_bias,
        qkv_full,
        qv_bias,
        proj_full,
        proj_bias,
        first_feedforward_gathered,
        fc1_bias,
        second_feedforward_gathered,
        fc2_bias,
    ) = gathered
    features = latents.shape[2]
    root_inv = HD ** (-0.5)
    time_hot = one_hot(time_ids, time_full.shape[0])
    class_hot = one_hot(class_ids, class_full.shape[0])
    embedded = jnp.dot(time_hot, time_full, preferred_element_type=jnp.float32) + jnp.dot(
        class_hot, class_full, preferred_element_type=jnp.float32
    )
    condition = jax.nn.silu(embedded).astype(jnp.bfloat16)
    modulation = jnp.dot(condition, ada_full, preferred_element_type=jnp.float32) + ada_bias.astype(
        jnp.float32
    )
    blocks = [modulation[:, None, index * features : (index + 1) * features] for index in range(6)]
    shift_first, scale_first, gate_first, shift_second, scale_second, gate_second = blocks
    stream = latents.astype(jnp.float32)
    normed_first = modulate(stream, shift_first, scale_first).astype(jnp.bfloat16)
    qkv_out = jnp.einsum("lsd,de->lse", normed_first, qkv_full, preferred_element_type=jnp.float32)
    queries = (qkv_out[..., :features] + qv_bias[:features].astype(jnp.float32)).astype(
        jnp.bfloat16
    )
    keys_local = qkv_out[..., features : 2 * features].astype(jnp.bfloat16)
    values_local = (qkv_out[..., 2 * features :] + qv_bias[features:].astype(jnp.float32)).astype(
        jnp.bfloat16
    )
    keys_all, values_all = (
        lax.all_gather(keys_local, "seq", axis=1, tiled=True),
        lax.all_gather(values_local, "seq", axis=1, tiled=True),
    )
    q_heads = split_heads(queries)
    scores = scores_of(q_heads, split_heads(keys_all))
    row_max = jnp.max(scores, -1, keepdims=True)
    log_total = row_max + jnp.log(jnp.sum(jnp.exp(scores - row_max), -1, keepdims=True))
    probs = jnp.exp(scores - log_total).astype(jnp.bfloat16)
    attended = (
        jnp.einsum(
            "lhqk,lkhd->lqhd", probs, split_heads(values_all), preferred_element_type=jnp.float32
        )
        .reshape(latents.shape)
        .astype(jnp.bfloat16)
    )
    branch = jnp.einsum(
        "lsd,de->lse", attended, proj_full, preferred_element_type=jnp.float32
    ) + proj_bias.astype(jnp.float32)
    residual = stream + gate_first * branch
    second_normed_input = modulate(residual, shift_second, scale_second).astype(jnp.bfloat16)
    preactivation_values = jnp.einsum(
        "zxw,wh->zxh",
        second_normed_input,
        first_feedforward_gathered,
        preferred_element_type=jnp.float32,
    ) + fc1_bias.astype(jnp.float32)
    gelu_activation = gelu_tanh(preactivation_values).astype(jnp.bfloat16)
    feedforward_output = jnp.einsum(
        "yxt,ti->yxi",
        gelu_activation,
        second_feedforward_gathered,
        preferred_element_type=jnp.float32,
    ) + fc2_bias.astype(jnp.float32)
    output = (residual + gate_second * feedforward_output).astype(jnp.bfloat16)
    ada_back, qkv_back, proj_back, first_feedforward_backward, second_feedforward_backward = (
        lax.all_gather(ada_w, ("fsdp", "seq"), axis=0, tiled=True),
        lax.all_gather(qkv_w, ("fsdp", "seq"), axis=0, tiled=True),
        lax.all_gather(proj_w, ("fsdp", "seq"), axis=0, tiled=True),
        lax.all_gather(first_feedforward_weight, ("fsdp", "seq"), axis=0, tiled=True),
        lax.all_gather(second_feedforward_weight, ("fsdp", "seq"), axis=0, tiled=True),
    )
    keys_back, values_back = (
        lax.all_gather(keys_local, "seq", axis=1, tiled=True),
        lax.all_gather(values_local, "seq", axis=1, tiled=True),
    )
    upstream = cotangent.astype(jnp.float32)
    d_gate_second = jnp.sum(upstream * feedforward_output, 1)
    feedforward_gradient = (upstream * gate_second).astype(jnp.bfloat16)
    second_feedforward_gradient = jnp.einsum(
        "avr,avm->rm", gelu_activation, feedforward_gradient, preferred_element_type=jnp.float32
    )
    fc2_bias_grad = jnp.sum(feedforward_gradient.astype(jnp.float32), (0, 1))
    activation_gradient = jnp.einsum(
        "pqh,ah->pqa",
        feedforward_gradient,
        second_feedforward_backward,
        preferred_element_type=jnp.float32,
    )
    preactivation_gradient = jax.vjp(gelu_tanh, preactivation_values)[1](activation_gradient)[
        0
    ].astype(jnp.bfloat16)
    first_feedforward_gradient = jnp.einsum(
        "ryk,ryt->kt",
        second_normed_input,
        preactivation_gradient,
        preferred_element_type=jnp.float32,
    )
    fc1_bias_grad = jnp.sum(preactivation_gradient.astype(jnp.float32), (0, 1))
    second_normed_gradient = jnp.einsum(
        "jmv,yv->jmy",
        preactivation_gradient,
        first_feedforward_backward,
        preferred_element_type=jnp.float32,
    )
    back_second = jax.vjp(modulate, residual, shift_second, scale_second)[1](second_normed_gradient)
    d_residual = upstream + back_second[0]
    d_gate_first = jnp.sum(d_residual * branch, 1)
    d_branch = (d_residual * gate_first).astype(jnp.bfloat16)
    proj_grad = jnp.einsum("lsd,lse->de", attended, d_branch, preferred_element_type=jnp.float32)
    proj_bias_grad = jnp.sum(d_branch.astype(jnp.float32), (0, 1))
    d_attended = jnp.einsum(
        "lse,de->lsd", d_branch, proj_back, preferred_element_type=jnp.float32
    ).astype(jnp.bfloat16)
    k_heads = split_heads(keys_back)
    v_heads = split_heads(values_back)
    exact = jnp.exp(scores_of(q_heads, k_heads) - log_total)
    probs_back = exact.astype(jnp.bfloat16)
    do_heads = split_heads(d_attended)
    d_values = jnp.einsum(
        "lhqk,lqhd->lkhd", probs_back, do_heads, preferred_element_type=jnp.float32
    )
    d_probs = jnp.einsum("lqhd,lkhd->lhqk", do_heads, v_heads, preferred_element_type=jnp.float32)
    delta = jnp.einsum(
        "lqhd,lqhd->lhq", do_heads, split_heads(attended), preferred_element_type=jnp.float32
    )
    d_scores = (exact * (d_probs - delta[..., None]) * root_inv).astype(jnp.bfloat16)
    d_queries = jnp.einsum(
        "lhqk,lkhd->lqhd", d_scores, k_heads, preferred_element_type=jnp.float32
    ).reshape(latents.shape)
    d_keys = jnp.einsum(
        "lhqk,lqhd->lkhd", d_scores, q_heads, preferred_element_type=jnp.float32
    ).reshape(keys_back.shape)
    d_keys_own, d_values_own = (
        lax.psum_scatter(d_keys, "seq", scatter_dimension=1, tiled=True),
        lax.psum_scatter(d_values.reshape(keys_back.shape), "seq", scatter_dimension=1, tiled=True),
    )
    d_qkv = jnp.concatenate([d_queries, d_keys_own, d_values_own], -1).astype(jnp.bfloat16)
    qkv_grad = jnp.einsum("lsd,lse->de", normed_first, d_qkv, preferred_element_type=jnp.float32)
    qv_bias_grad = jnp.concatenate(
        [
            jnp.sum(d_qkv[..., :features].astype(jnp.float32), (0, 1)),
            jnp.sum(d_qkv[..., 2 * features :].astype(jnp.float32), (0, 1)),
        ]
    )
    d_normed_first = jnp.einsum("lse,de->lsd", d_qkv, qkv_back, preferred_element_type=jnp.float32)
    back_first = jax.vjp(modulate, stream, shift_first, scale_first)[1](d_normed_first)
    latents_grad = d_residual + back_first[0]
    d_modulation = jnp.concatenate(
        [
            back_first[1][:, 0],
            back_first[2][:, 0],
            d_gate_first,
            back_second[1][:, 0],
            back_second[2][:, 0],
            d_gate_second,
        ],
        -1,
    )
    d_condition = jnp.einsum(
        "le,de->ld", d_modulation, ada_back, precision=highest, preferred_element_type=jnp.float32
    )
    d_embedded = jax.vjp(jax.nn.silu, embedded)[1](d_condition)[0]
    ada_grad = jnp.dot(condition.astype(jnp.float32).T, d_modulation, precision=highest)
    ada_bias_grad = jnp.sum(d_modulation, 0)
    time_grad = jnp.dot(time_hot.astype(jnp.float32).T, d_embedded, precision=highest)
    class_grad = jnp.dot(class_hot.astype(jnp.float32).T, d_embedded, precision=highest)
    owned = tuple(
        (
            lax.psum_scatter(time_grad, ("fsdp", "seq"), scatter_dimension=0, tiled=True),
            lax.psum_scatter(class_grad, ("fsdp", "seq"), scatter_dimension=0, tiled=True),
            lax.psum_scatter(ada_grad, ("fsdp", "seq"), scatter_dimension=0, tiled=True),
            lax.psum_scatter(ada_bias_grad, ("fsdp", "seq"), scatter_dimension=0, tiled=True),
            lax.psum_scatter(qkv_grad, ("fsdp", "seq"), scatter_dimension=0, tiled=True),
            lax.psum_scatter(qv_bias_grad, ("fsdp", "seq"), scatter_dimension=0, tiled=True),
            lax.psum_scatter(proj_grad, ("fsdp", "seq"), scatter_dimension=0, tiled=True),
            lax.psum_scatter(proj_bias_grad, ("fsdp", "seq"), scatter_dimension=0, tiled=True),
            lax.psum_scatter(
                first_feedforward_gradient, ("fsdp", "seq"), scatter_dimension=0, tiled=True
            ),
            lax.psum_scatter(fc1_bias_grad, ("fsdp", "seq"), scatter_dimension=0, tiled=True),
            lax.psum_scatter(
                second_feedforward_gradient, ("fsdp", "seq"), scatter_dimension=0, tiled=True
            ),
            lax.psum_scatter(fc2_bias_grad, ("fsdp", "seq"), scatter_dimension=0, tiled=True),
        )
    )
    return (
        output,
        latents_grad,
        owned[0],
        owned[1],
        owned[2],
        owned[3],
        owned[4],
        owned[5],
        owned[6],
        owned[7],
        owned[8],
        owned[9],
        owned[10],
        owned[11],
    )


def solution(mesh):
    in_specs = (
        P("fsdp", "seq", None),
        P("fsdp"),
        P("fsdp"),
        P(("fsdp", "seq"), None),
        P(("fsdp", "seq"), None),
        P(("fsdp", "seq"), None),
        P(("fsdp", "seq")),
        P(("fsdp", "seq"), None),
        P(("fsdp", "seq")),
        P(("fsdp", "seq"), None),
        P(("fsdp", "seq")),
        P(("fsdp", "seq"), None),
        P(("fsdp", "seq")),
        P(("fsdp", "seq"), None),
        P(("fsdp", "seq")),
        P("fsdp", "seq", None),
    )
    out_specs = (
        P("fsdp", "seq", None),
        P("fsdp", "seq", None),
        P(("fsdp", "seq"), None),
        P(("fsdp", "seq"), None),
        P(("fsdp", "seq"), None),
        P(("fsdp", "seq")),
        P(("fsdp", "seq"), None),
        P(("fsdp", "seq")),
        P(("fsdp", "seq"), None),
        P(("fsdp", "seq")),
        P(("fsdp", "seq"), None),
        P(("fsdp", "seq")),
        P(("fsdp", "seq"), None),
        P(("fsdp", "seq")),
    )
    return jax.shard_map(shards, mesh=mesh, in_specs=in_specs, out_specs=out_specs, check_vma=False)
```

profile of v0, /device:TPU:0, one launch (start us, length us, event | category | flops | bytes accessed | tf_op | source)
XLA Modules:
  0.0 1384.7 jit_solution(8307622063614662808)
XLA Ops:
  17.5 42.4 %all-reduce.11 = (bf16[4608]{0:T(1024)(128)(2,1)S(1)}, bf16[1536]{0:T(1024)(128)(2,1)S(1)}, bf16[768]{0:T(1024)(128)(2,1)S(1)}, bf16[768]{0:T(1024)(128)(2,1)S(1)}, bf16[3072]{0:T(1024)(128)(2,1)S(1)}) all-reduce(bf16[4608]{0:T(1024)(128)(2,1)S(1)} %dynamic-update-slice, ...), channel_id=1, replica_groups=mesh['fsdp'=16,'seq'=2] {'fsdp','seq'}, use_global_device_ids=true, to_apply=%add | all-reduce | flops 10752 | bytes 43008
  62.7 6.2 all-gather.8.cloned.1.call-done
  70.6 54.9 %all-gather.10.cloned.1.call-done = bf16[1024,768]{1,0:T(8,128)(2,1)} async-done(((bf16[32,768]{1,0:T(8,128)(2,1)}), bf16[1024,768]{1,0:T(8,128)(2,1)}) %all-gather.10.cloned.1.call-update) | async-done | bytes 1572880 | tf_op jit(solution)/shard_map/all_gather | solution.py:62
  127.9 71.9 %all-gather.12.cloned.1.call-done = bf16[768,4608]{1,0:T(8,128)(2,1)} async-done(((bf16[24,4608]{1,0:T(8,128)(2,1)}), bf16[768,4608]{1,0:T(8,128)(2,1)}) %all-gather.12.cloned.1.call-update) | async-done | bytes 7077904 | tf_op jit(solution)/shard_map/all_gather | solution.py:63
  204.0 57.2 %all-gather.14.cloned.1.call-done = bf16[768,2304]{1,0:T(8,128)(2,1)} async-done(((bf16[24,2304]{1,0:T(8,128)(2,1)}), bf16[768,2304]{1,0:T(8,128)(2,1)}) %all-gather.14.cloned.1.call-update) | async-done | bytes 3538960 | tf_op jit(solution)/shard_map/all_gather | solution.py:65
  270.4 46.4 %all-gather.16.cloned.1.call-done = bf16[768,768]{1,0:T(8,128)(2,1)} async-done(((bf16[24,768]{1,0:T(8,128)(2,1)}), bf16[768,768]{1,0:T(8,128)(2,1)}) %all-gather.16.cloned.1.call-update) | async-done | bytes 1179664 | tf_op jit(solution)/shard_map/all_gather | solution.py:67
  318.8 63.4 %all-gather.18.cloned.1.call-done = bf16[768,3072]{1,0:T(8,128)(2,1)} async-done(((bf16[24,3072]{1,0:T(8,128)(2,1)}), bf16[768,3072]{1,0:T(8,128)(2,1)}) %all-gather.18.cloned.1.call-update) | async-done | bytes 4718608 | tf_op jit(solution)/shard_map/all_gather | solution.py:69
  382.2 4.4 convolution_add_fusion
  386.6 61.0 %all-gather.20.cloned.1.call-done = bf16[3072,768]{1,0:T(8,128)(2,1)} async-done(((bf16[96,768]{1,0:T(8,128)(2,1)}), bf16[3072,768]{1,0:T(8,128)(2,1)}) %all-gather.20.cloned.1.call-update) | async-done | bytes 4718608 | tf_op jit(solution)/shard_map/all_gather | solution.py:71
  447.6 5.5 convert_reduce_fusion
  469.8 10.6 reduce-scatter.10.cloned.1.call-done
  485.3 7.8 convolution_reduce_fusion.1
  497.0 4.1 fusion.28
  502.2 5.1 fusion.60
  508.7 5.2 fusion.38
  514.6 6.8 broadcast_multiply_fusion
  522.1 41.3 %all-reduce.10 = (f32[4608]{0:T(1024)S(1)}, f32[1536]{0:T(1024)S(1)}, f32[768]{0:T(1024)S(1)}, f32[3072]{0:T(1024)S(1)}, f32[768]{0:T(1024)S(1)}) all-reduce(f32[4608]{0:T(1024)S(1)} %reduce.34, f32[1536]{0:T(1024)S(1)} %pad_maximum_fusion.3, f32[768]{0:T(1024)S(1)} %copy-done.37, ...), channel_id=7, replica_groups=mesh['fsdp'=16,'seq'=2] {'fsdp','seq'}, use_global_device_ids=true, to_apply=%region_21.22.clone | all-reduce | flops 10752 | bytes 86016
  567.4 19.1 %reduce-scatter.22.cloned.1.call-done = f32[24,768]{1,0:T(8,128)} async-done(((f32[768,768]{1,0:T(8,128)}), f32[24,768]{1,0:T(8,128)}) %reduce-scatter.22.cloned.1.call-update) | async-done | bytes 73744 | tf_op jit(solution)/shard_map/reduce_scatter | solution.py:256
  586.4 107.5 %reduce-scatter.14.cloned.1.call-done = f32[32,768]{1,0:T(8,128)} async-done(((f32[1024,768]{1,0:T(8,128)}), f32[32,768]{1,0:T(8,128)}) %reduce-scatter.14.cloned.1.call-update) | async-done | bytes 98320 | tf_op jit(solution)/shard_map/reduce_scatter | solution.py:250
  693.9 107.3 %reduce-scatter.16.cloned.1.call-done = f32[32,768]{1,0:T(8,128)} async-done(((f32[1024,768]{1,0:T(8,128)}), f32[32,768]{1,0:T(8,128)}) %reduce-scatter.16.cloned.1.call-update) | async-done | bytes 98320 | tf_op jit(solution)/shard_map/reduce_scatter | solution.py:251
  801.2 125.3 %reduce-scatter.20.cloned.1.call-done = f32[24,2304]{1,0:T(8,128)} async-done(((f32[768,2304]{1,0:T(8,128)}), f32[24,2304]{1,0:T(8,128)}) %reduce-scatter.20.cloned.1.call-update) | async-done | bytes 221200 | tf_op jit(solution)/shard_map/reduce_scatter | solution.py:254
  926.5 141.2 %reduce-scatter.24.cloned.1.call-done = f32[24,3072]{1,0:T(8,128)} async-done(((f32[768,3072]{1,0:T(8,128)}), f32[24,3072]{1,0:T(8,128)}) %reduce-scatter.24.cloned.1.call-update) | async-done | bytes 294928 | tf_op jit(solution)/shard_map/reduce_scatter | solution.py:258
  1067.8 142.0 %reduce-scatter.26.cloned.1.call-done = f32[96,768]{1,0:T(8,128)} async-done(((f32[3072,768]{1,0:T(8,128)}), f32[96,768]{1,0:T(8,128)}) %reduce-scatter.26.cloned.1.call-update) | async-done | bytes 294928 | tf_op jit(solution)/shard_map/reduce_scatter | solution.py:262
  1209.7 168.4 %reduce-scatter.18.cloned.1.call-done = f32[24,4608]{1,0:T(8,128)} async-done(((f32[768,4608]{1,0:T(8,128)}), f32[24,4608]{1,0:T(8,128)}) %reduce-scatter.18.cloned.1.call-update) | async-done | bytes 442384 | tf_op jit(solution)/shard_map/reduce_scatter | solution.py:252
  (208 shorter events, 63.8 us)
Async XLA Ops:
  7.2 61.7 %all-gather.8.cloned.1.call-start = ((), (), s32[]{:S(2)}) async-start(), calls=%async_computation.9 | async-start | bytes 1622016 | tf_op jit(solution)/shard_map/all_gather | solution.py:61
  7.9 117.6 %all-gather.10.cloned.1.call-start = ((), (), s32[]{:S(2)}) async-start(), calls=%async_computation.10 | async-start | bytes 1622016 | tf_op jit(solution)/shard_map/all_gather | solution.py:62
  8.7 191.1 %all-gather.12.cloned.1.call-start = ((), (), s32[]{:S(2)}) async-start(), calls=%async_computation.11 | async-start | bytes 7299072 | tf_op jit(solution)/shard_map/all_gather | solution.py:63
  9.4 251.8 %all-gather.14.cloned.1.call-start = ((), (), s32[]{:S(2)}) async-start(), calls=%async_computation.12 | async-start | bytes 3649536 | tf_op jit(solution)/shard_map/all_gather | solution.py:65
  10.0 306.8 %all-gather.16.cloned.1.call-start = ((), (), s32[]{:S(2)}) async-start(), calls=%async_computation.13 | async-start | bytes 1216512 | tf_op jit(solution)/shard_map/all_gather | solution.py:67
  10.6 371.6 %all-gather.18.cloned.1.call-start = ((), (), s32[]{:S(2)}) async-start(), calls=%async_computation.14 | async-start | bytes 4866048 | tf_op jit(solution)/shard_map/all_gather | solution.py:69
  11.1 436.4 %all-gather.20.cloned.1.call-start = ((), (), s32[]{:S(2)}) async-start(), calls=%async_computation.15 | async-start | bytes 4866048 | tf_op jit(solution)/shard_map/all_gather | solution.py:71
  11.9 456.7 %reduce-scatter.12.cloned.1.call-start = ((), (), s32[]{:S(2)}) async-start(), calls=%async_computation.17 | async-start | bytes 1179648 | tf_op jit(solution)/shard_map/reduce_scatter | solution.py:216
  61.1 200.1 %copy-start.26 = (f32[128]{0:T(128)}, f32[128]{0:T(128)S(1)}, u32[]{:S(2)}) copy-start(f32[128]{0:T(128)S(1)} %broadcast_multiply_fusion.4) | copy-start | bytes 1540
  62.7 198.5 %copy-start.24 = (f32[128]{0:T(128)}, f32[128]{0:T(128)S(1)}, u32[]{:S(2)}) copy-start(f32[128]{0:T(128)S(1)} %fusion.53) | copy-start | bytes 1540
  127.9 133.4 %copy-start.1 = (bf16[1,128,768]{2,1,0:T(8,128)(2,1)S(1)}, bf16[1,128,768]{2,1,0:T(8,128)(2,1)}, u32[]{:S(2)}) copy-start(bf16[1,128,768]{2,1,0:T(8,128)(2,1)} %param.16) | copy-start | bytes 589828
  203.9 251.7 %copy-start.28 = (f32[768]{0:T(1024)}, f32[768]{0:T(1024)S(1)}, u32[]{:S(2)}) copy-start(f32[768]{0:T(1024)S(1)} %get-tuple-element.21) | copy-start | bytes 9220
  270.4 191.0 %copy-start.10 = (bf16[12,64,128]{2,1,0:T(8,128)(2,1)}, bf16[12,64,128]{2,1,0:T(8,128)(2,1)S(1)}, u32[]{:S(2)}) copy-start(bf16[12,64,128]{2,1,0:T(8,128)(2,1)S(1)} %convolution_convert_fusion.2) | copy-start | bytes 589828
  318.6 136.8 %copy-start.22 = (f32[128]{0:T(128)}, f32[128]{0:T(128)S(1)}, u32[]{:S(2)}) copy-start(f32[128]{0:T(128)S(1)} %broadcast_multiply_fusion.3) | copy-start | bytes 1540
  318.8 136.6 %copy-start.33 = (f32[128]{0:T(128)}, f32[128]{0:T(128)S(1)}, u32[]{:S(2)}) copy-start(f32[128]{0:T(128)S(1)} %fusion.54) | copy-start | bytes 1540
  382.2 65.4 %copy-start.16 = (bf16[1,128,768]{2,1,0:T(8,128)(2,1)S(1)}, bf16[1,128,768]{2,1,0:T(8,128)(2,1)}, u32[]{:S(2)}) copy-start(bf16[1,128,768]{2,1,0:T(8,128)(2,1)} %param.31) | copy-start | bytes 589828
  461.4 19.0 %reduce-scatter.10.cloned.1.call-start = ((), (), s32[]{:S(2)}) async-start(), calls=%async_computation.16 | async-start | bytes 1179648 | tf_op jit(solution)/shard_map/reduce_scatter | solution.py:215
  464.5 121.9 %reduce-scatter.22.cloned.1.call-start = ((), (), s32[]{:S(2)}) async-start(), calls=%async_computation.22 | async-start | bytes 2433024 | tf_op jit(solution)/shard_map/reduce_scatter | solution.py:256
  466.5 227.4 %reduce-scatter.14.cloned.1.call-start = ((), (), s32[]{:S(2)}) async-start(), calls=%async_computation.18 | async-start | bytes 3244032 | tf_op jit(solution)/shard_map/reduce_scatter | solution.py:250
  496.3 304.9 %reduce-scatter.16.cloned.1.call-start = ((), (), s32[]{:S(2)}) async-start(), calls=%async_computation.19 | async-start | bytes 3244032 | tf_op jit(solution)/shard_map/reduce_scatter | solution.py:251
  496.9 429.6 %reduce-scatter.20.cloned.1.call-start = ((), (), s32[]{:S(2)}) async-start(), calls=%async_computation.21 | async-start | bytes 7299072 | tf_op jit(solution)/shard_map/reduce_scatter | solution.py:254
  501.1 566.7 %reduce-scatter.24.cloned.1.call-start = ((), (), s32[]{:S(2)}) async-start(), calls=%async_computation.23 | async-start | bytes 9732096 | tf_op jit(solution)/shard_map/reduce_scatter | solution.py:258
  507.3 702.4 %reduce-scatter.26.cloned.1.call-start = ((), (), s32[]{:S(2)}) async-start(), calls=%async_computation.24 | async-start | bytes 9732096 | tf_op jit(solution)/shard_map/reduce_scatter | solution.py:262
  513.9 864.2 %reduce-scatter.18.cloned.1.call-start = ((), (), s32[]{:S(2)}) async-start(), calls=%async_computation.20 | async-start | bytes 14598144 | tf_op jit(solution)/shard_map/reduce_scatter | solution.py:252
  (37 other events, 230.6 us)
Sparse Core Ops, SparseCore 0:
  10.9 57.9 all-gather.7
  71.8 53.6 all-gather.9
  128.4 71.3 all-gather.11
  202.6 58.5 all-gather.13
  263.9 52.8 all-gather.15
  319.6 62.5 all-gather.17
  385.1 62.4 all-gather.19
  461.5 7.0 reduce-scatter.11
  471.0 9.3 reduce-scatter.9
  486.1 100.2 reduce-scatter.21
  593.3 100.5 reduce-scatter.13
  700.7 100.5 reduce-scatter.15
  808.4 118.0 reduce-scatter.19
  932.9 134.8 reduce-scatter.23
  1075.1 134.5 reduce-scatter.25
  1216.1 161.9 reduce-scatter.17
where the time goes:
time: 1390 us; the launch traced here: 1380 us
  waiting for transfers between devices  1190 us (86%)
  blocking collectives  88.1 us (6%)
  matrix products  60.1 us (4%)
  other arithmetic  17.5 us (1%)
  between operations  16 us (1%)
  local copies, waits for them, and re-layouts  14.1 us (1%)
    reduce_scatter x1, waiting for transfers between devices, shards(): lax.psum_scatter(ada_grad, ('fsdp', 'seq'), scatter_dimension=0, tiled=True)  168 us
    reduce_scatter x1, waiting for transfers between devices, shards(): lax.psum_scatter(second_feedforward_gradient, ('fsdp', 'seq'), scatter_di...  142 us
    reduce_scatter x1, waiting for transfers between devices, shards(): lax.psum_scatter(first_feedforward_gradient, ('fsdp', 'seq'), scatter_dim...  141 us
    reduce_scatter x1, waiting for transfers between devices, shards(): lax.psum_scatter(qkv_grad, ('fsdp', 'seq'), scatter_dimension=0, tiled=True)  125 us
    reduce_scatter x1, waiting for transfers between devices, shards(): lax.psum_scatter(time_grad, ('fsdp', 'seq'), scatter_dimension=0, tiled=T...  108 us
    reduce_scatter x1, waiting for transfers between devices, shards(): lax.psum_scatter(class_grad, ('fsdp', 'seq'), scatter_dimension=0, tiled=...  107 us
    unnamed x2, blocking collectives  83.8 us
    all_gather x1, waiting for transfers between devices, shards(): lax.all_gather(ada_w, ('fsdp', 'seq'), axis=0, tiled=True)  71.9 us
  transfers between devices with their start and end apart: 16, of which 16 were waited for; matrix products, arithmetic and copies ran while one was open for 5% of the time, Pallas kernels for 0%

commit v1 on v0

v1 whole, which is shorter than its diff:
```python
import functools

import jax
import jax.numpy as jnp
from jax import lax
from jax.experimental import pallas as pl
from jax.experimental.pallas import tpu as pltpu
from jax.sharding import PartitionSpec as P

HD = 64
norm_eps = 1e-06
highest = lax.Precision.HIGHEST
f32 = jnp.float32
bf16 = jnp.bfloat16
BOTH = ("fsdp", "seq")


def layer_norm(stream):
    center = stream - jnp.mean(stream, -1, keepdims=True)
    spread = jnp.mean(center * center, -1, keepdims=True)
    return center * lax.rsqrt(spread + norm_eps)


def modulate(stream, shift_part, scale_part):
    return layer_norm(stream) * (1.0 + scale_part) + shift_part


def gelu_tanh(values):
    return jax.nn.gelu(values, approximate=True)


def dot(a, b, out=f32):
    return jnp.dot(a, b, preferred_element_type=f32).astype(out)


def dot_t(a, b, out=f32):
    return lax.dot_general(a, b, (((0,), (0,)), ((), ())), preferred_element_type=f32).astype(out)


def dot_nt(a, b, out=f32):
    return lax.dot_general(a, b, (((1,), (1,)), ((), ())), preferred_element_type=f32).astype(out)


class Chips:
    def __init__(self, count):
        self.count = count
        self.bits = count.bit_length() - 1
        assert count == 1 << self.bits and self.bits >= 2
        outer = list(range(2, self.bits))
        self.orders = (outer + [0, 1], outer + [1, 0])

    def step(self, x, k):
        pairs = [
            (2 * i + core, 2 * (i ^ (1 << self.orders[core][k])) + core)
            for i in range(self.count)
            for core in range(2)
        ]
        return lax.ppermute(x, BOTH, pairs)

    def flips(self, core):
        order = self.orders[core]
        return [
            sum(1 << order[k] for k in range(self.bits) if (r >> k) & 1) for r in range(self.count)
        ]

    def places(self):
        me, core = lax.axis_index("fsdp"), lax.axis_index("seq")
        return [
            jnp.bitwise_xor(me, jnp.where(core == 0, a, b))
            for a, b in zip(self.flips(0), self.flips(1))
        ]

    def gather(self, block):
        held = block[None]
        for k in range(self.bits - 1):
            held = jnp.concatenate([held, self.step(held, k)], 0)
        return place(self, [held, self.step(held, self.bits - 1)])

    def scatter(self, blocks):
        half = self.count // 2
        recv = self.step(blocks[half:], self.bits - 1)
        total = blocks[:half].astype(f32) + recv.astype(f32)
        for k in range(self.bits - 2, -1, -1):
            half //= 2
            recv = self.step(total[half:].astype(bf16), k)
            total = total[:half] + recv.astype(f32)
        return total[0]


def place_kernel(chips, inward, widths, *refs):
    out = refs[-1]
    ins = refs[:-1]
    half = chips.count // 2
    for r, chip in enumerate(chips.places()):
        if inward:
            out[chip] = ins[r // half][r % half]
        else:
            start = 0
            for ref, w in zip(ins, widths):
                out[r, :, start : start + w] = ref[chip]
                start += w


def place(chips, halves):
    _, rows, columns = halves[0].shape
    if rows % 16 or columns % 128:
        held = jnp.concatenate(halves, 0)
        me, core = lax.axis_index("fsdp"), lax.axis_index("seq")
        inverse = []
        for c in range(2):
            flips = chips.flips(c)
            inverse.append(jnp.array([flips.index(x) for x in range(chips.count)], jnp.int32))
        table = jnp.where(core == 0, inverse[0], inverse[1])
        return held[table[jnp.bitwise_xor(me, jnp.arange(chips.count))]]
    return pl.pallas_call(
        functools.partial(place_kernel, chips, True, None),
        out_shape=jax.ShapeDtypeStruct((chips.count, rows, columns), halves[0].dtype),
        in_specs=[pl.BlockSpec(memory_space=pltpu.VMEM)] * 2,
        out_specs=pl.BlockSpec(memory_space=pltpu.VMEM),
        compiler_params=pltpu.CompilerParams(vmem_limit_bytes=32 << 20),
        name="place",
    )(*halves)


def relative(chips, arrays):
    rows = arrays[0].shape[1]
    widths = [a.shape[2] for a in arrays]
    if rows % 16 or any(w % 128 for w in widths):
        return jnp.concatenate(arrays, 2)[jnp.stack(chips.places())]
    return pl.pallas_call(
        functools.partial(place_kernel, chips, False, widths),
        out_shape=jax.ShapeDtypeStruct((chips.count, rows, sum(widths)), arrays[0].dtype),
        in_specs=[pl.BlockSpec(memory_space=pltpu.VMEM)] * len(arrays),
        out_specs=pl.BlockSpec(memory_space=pltpu.VMEM),
        compiler_params=pltpu.CompilerParams(vmem_limit_bytes=32 << 20),
        name="relative",
    )(*arrays)


def other_core(x):
    return lax.ppermute(x, "seq", [(0, 1), (1, 0)])


def shards(
    chips,
    latents,
    time_ids,
    class_ids,
    time_table,
    class_table,
    ada_w,
    ada_b,
    qkv_w,
    qv_b,
    proj_w,
    proj_b,
    fc1_w,
    fc1_b,
    fc2_w,
    fc2_b,
    cotangent,
):
    n = chips.count
    nd = 2 * n
    me, core = lax.axis_index("fsdp"), lax.axis_index("seq")
    first = core == 0
    own_tokens, D = latents.shape[1:]
    half = D // 2
    FF = fc1_w.shape[1]
    rows = qkv_w.shape[0]
    ff_rows = fc2_w.shape[0]
    table_rows = time_table.shape[0]
    root_inv = HD ** (-0.5)

    def pick(pair):
        return jnp.where(first, pair[0], pair[1]), jnp.where(first, pair[1], pair[0])

    def in_order(mine, others, axis):
        a, b = pick((mine, others))
        return jnp.concatenate([a, b], axis)

    qkv_parts = qkv_w.reshape(rows, 3, 2, half)
    qkv_mine, qkv_others = pick((qkv_parts[:, :, 0], qkv_parts[:, :, 1]))
    proj_mine, proj_others = pick((proj_w[:, :half], proj_w[:, half:]))
    fc1_parts = fc1_w.reshape(rows, n, 2, ff_rows)
    fc1_mine, fc1_others = pick((fc1_parts[:, :, 0], fc1_parts[:, :, 1]))

    def across(mine, others):
        return in_order(mine, other_core(others), 0)

    block_q = across(
        jnp.concatenate([qkv_mine.reshape(rows, 3 * half), proj_mine], 1),
        jnp.concatenate([qkv_others.reshape(rows, 3 * half), proj_others], 1),
    )
    tokens = jnp.concatenate([latents, cotangent], 0)
    tokens = jnp.concatenate([tokens, other_core(tokens)], 1)
    stream = tokens[0].astype(f32)
    upstream = tokens[1].astype(f32)

    width = 2 * table_rows
    cols = D // nd
    table = jnp.concatenate([time_table, class_table], 0).T.reshape(nd, cols, width)
    ids = jnp.stack([time_ids[0], class_ids[0]])
    extras = jnp.concatenate(
        [fc1_b, qv_b, proj_b, fc2_b, ada_b, (ids // 32).astype(bf16), (ids % 32).astype(bf16)]
    )
    extra_count = extras.shape[0]
    extra_rows = -(-extra_count // width)
    extras = jnp.pad(extras, (0, extra_rows * width - extra_count)).reshape(1, extra_rows, width)
    sent = jnp.concatenate([table, jnp.broadcast_to(extras, (nd, extra_rows, width))], 1)
    got = lax.all_to_all(sent, BOTH, 0, 0, tiled=True)
    extras = got[:, cols:].reshape(nd, extra_rows * width)
    bounds = [0]
    for b in (fc1_b, qv_b, proj_b, fc2_b, ada_b):
        bounds.append(bounds[-1] + b.shape[0])
    fc1_bias, qv_bias, proj_bias, fc2_bias, ada_bias = (
        extras[:, a:b].astype(f32) for a, b in zip(bounds[:-1], bounds[1:])
    )
    fc1_bias = fc1_bias.reshape(n, 2, ff_rows)
    fc1_bias = pick((fc1_bias[:, 0], fc1_bias[:, 1]))[0].reshape(n * ff_rows)
    qv_bias = qv_bias.reshape(2, 2, half)
    qv_bias = pick((qv_bias[:, 0], qv_bias[:, 1]))[0]
    id_parts = extras[::2, bounds[-1] : bounds[-1] + 4].astype(jnp.int32)
    all_ids = id_parts[:, :2] * 32 + id_parts[:, 2:]

    def hot(which, base):
        rows_of = base + lax.broadcasted_iota(jnp.int32, (nd, table_rows, n), 1)
        return (all_ids[:, which][None, None] == rows_of).astype(bf16)

    base = lax.broadcasted_iota(jnp.int32, (nd, table_rows, n), 0) * table_rows
    hot_both = jnp.concatenate([hot(0, base), hot(1, base)], 1)
    embedded = jnp.einsum("sdr,srl->ld", got[:, :cols], hot_both, preferred_element_type=f32)
    condition = jax.nn.silu(embedded).astype(bf16)
    partial = dot(condition, ada_w)
    lanes = 128 if (6 * D) % 128 == 0 else 6 * D
    partial = lax.all_to_all(partial.reshape(n, 6 * D // lanes, lanes), "fsdp", 0, 0, tiled=True)
    modulation = jnp.sum(partial, 0)
    modulation = (modulation + other_core(modulation)).reshape(6 * D) + ada_bias.reshape(6 * D)
    shift_first, scale_first, gate_first, shift_second, scale_second, gate_second = (
        modulation[None, i * D : (i + 1) * D] for i in range(6)
    )

    weights_q = chips.gather(block_q)
    qkv_full = weights_q[:, :, : 3 * half].reshape(D, 3 * half)
    proj_cols = weights_q[:, :, 3 * half :].reshape(2, half, half)
    block_1 = across(fc1_mine.reshape(rows, FF // 2), fc1_others.reshape(rows, FF // 2))
    fc1_full = chips.gather(block_1).reshape(D, FF // 2)
    fc2_full = chips.gather(fc2_w).reshape(FF // 2, D)
    proj_rows_mine, proj_rows_others = pick((proj_cols[0], proj_cols[1]))
    proj_full = in_order(proj_rows_mine, other_core(proj_rows_others), 1)

    normed_first = modulate(stream, shift_first, scale_first).astype(bf16)
    qkv_out = dot(normed_first, qkv_full)
    queries = (qkv_out[:, :half] + qv_bias[0]).astype(bf16)
    keys = qkv_out[:, half : 2 * half].astype(bf16)
    values = (qkv_out[:, 2 * half :] + qv_bias[1]).astype(bf16)

    def heads(x):
        return x.reshape(x.shape[0], half // HD, HD)

    q_heads, k_heads, v_heads = heads(queries), heads(keys), heads(values)
    scores = jnp.einsum("qhd,khd->hqk", q_heads, k_heads, preferred_element_type=f32) * root_inv
    row_max = jnp.max(scores, -1, keepdims=True)
    log_total = row_max + jnp.log(jnp.sum(jnp.exp(scores - row_max), -1, keepdims=True))
    exact = jnp.exp(scores - log_total)
    probs = exact.astype(bf16)
    attended = jnp.einsum("hqk,khd->qhd", probs, v_heads, preferred_element_type=f32)
    attended = attended.reshape(stream.shape[0], half).astype(bf16)

    def summed(x):
        got = other_core(x)
        return x + jnp.concatenate([got[own_tokens:], got[:own_tokens]], 0)

    branch = summed(dot(attended, proj_full)) + proj_bias.reshape(D)
    residual = stream + gate_first * branch
    normed_second = modulate(residual, shift_second, scale_second).astype(bf16)
    pre_act = dot(normed_second, fc1_full) + fc1_bias
    activated = gelu_tanh(pre_act).astype(bf16)
    mlp_part = dot(activated, fc2_full)
    mlp_own = mlp_part[:own_tokens] + other_core(mlp_part[own_tokens:]) + fc2_bias.reshape(D)
    output = (residual[:own_tokens] + gate_second * mlp_own).astype(bf16)

    d_gate_second = jnp.sum(upstream[:own_tokens] * mlp_own, 0)
    d_mlp = (upstream * gate_second).astype(bf16)
    fc2_grad = dot_t(activated, d_mlp, bf16).reshape(n, ff_rows, D)
    fc2_grad = chips.scatter(relative(chips, [fc2_grad]))
    fc2_b_grad = jnp.sum(d_mlp[:own_tokens].astype(f32), 0)
    d_act = dot_nt(d_mlp, fc2_full)
    d_pre = jax.vjp(gelu_tanh, pre_act)[1](d_act)[0].astype(bf16)
    fc1_grad = dot_t(normed_second, d_pre, bf16).reshape(n, 2 * rows, FF // 2)
    fc1_b_grad = jnp.sum(d_pre.astype(f32), 0)
    d_normed_second = summed(dot_nt(d_pre, fc1_full))
    back_second = jax.vjp(lambda v: modulate(v, shift_second, scale_second), residual)[1](
        d_normed_second
    )[0]
    d_residual = upstream + back_second
    own_normed = d_normed_second[:own_tokens]
    d_shift_second = jnp.sum(own_normed, 0)
    d_scale_second = jnp.sum(own_normed * layer_norm(residual[:own_tokens]), 0)
    d_gate_first = jnp.sum(d_residual[:own_tokens] * branch[:own_tokens], 0)
    d_branch = (d_residual * gate_first).astype(bf16)
    proj_b_grad = jnp.sum(d_branch[:own_tokens].astype(f32), 0)
    proj_grad = dot_t(attended, d_branch, bf16)
    proj_g_mine, proj_g_others = pick((proj_grad[:, :half], proj_grad[:, half:]))
    proj_grad = in_order(proj_g_mine, other_core(proj_g_others), 0).reshape(n, 2 * rows, half)
    fc1_proj_grad = chips.scatter(relative(chips, [fc1_grad, proj_grad]))

    d_attended = dot_nt(d_branch, proj_full, bf16)
    do_heads = heads(d_attended)
    d_values = jnp.einsum("hqk,qhd->khd", probs, do_heads, preferred_element_type=f32)
    d_probs = jnp.einsum("qhd,khd->hqk", do_heads, v_heads, preferred_element_type=f32)
    delta = jnp.einsum("qhd,qhd->hq", do_heads, heads(attended), preferred_element_type=f32)
    d_scores = (exact * (d_probs - delta[..., None]) * root_inv).astype(bf16)
    d_queries = jnp.einsum("hqk,khd->qhd", d_scores, k_heads, preferred_element_type=f32)
    d_keys = jnp.einsum("hqk,qhd->khd", d_scores, q_heads, preferred_element_type=f32)
    d_qkv = jnp.concatenate(
        [x.reshape(x.shape[0], half).astype(bf16) for x in (d_queries, d_keys, d_values)], -1
    )
    qkv_grad = dot_t(normed_first, d_qkv, bf16).reshape(n, 2 * rows, 3 * half)
    qkv_grad = chips.scatter(relative(chips, [qkv_grad]))
    d_qkv_sum = jnp.sum(d_qkv.astype(f32), 0)
    d_normed_part = dot_nt(d_qkv, qkv_full)
    d_normed_first = d_normed_part[:own_tokens] + other_core(d_normed_part[own_tokens:])
    own_stream = stream[:own_tokens]
    back_first = jax.vjp(lambda v: modulate(v, shift_first, scale_first), own_stream)[1](
        d_normed_first
    )[0]
    latents_grad = d_residual[:own_tokens] + back_first
    d_shift_first = jnp.sum(d_normed_first, 0)
    d_scale_first = jnp.sum(d_normed_first * layer_norm(own_stream), 0)

    def by_core(x):
        zero = jnp.zeros_like(x)
        return jnp.stack([jnp.where(first, x, zero), jnp.where(first, zero, x)], 1)

    fc1_b_part = by_core(fc1_b_grad.reshape(n, ff_rows))
    qv_part = by_core(
        jnp.stack([d_qkv_sum[:half], d_qkv_sum[2 * half :]])
    )
    qv_part = qv_part.reshape(n, 2, D // n)
    d_mod = jnp.concatenate(
        [d_shift_first, d_scale_first, d_gate_first, d_shift_second, d_scale_second, d_gate_second]
    )
    bias_part = jnp.concatenate(
        [
            fc1_b_part,
            qv_part,
            proj_b_grad.reshape(n, 2, rows),
            fc2_b_grad.reshape(n, 2, rows),
        ],
        2,
    ).reshape(n, -1)
    small = jnp.concatenate([d_mod, bias_part.reshape(-1)])
    small = small + other_core(small)
    d_mod, bias_part = small[: 6 * D], small[6 * D :].reshape(n, -1)
    ada_b_grad = None
    sent = jnp.concatenate([jnp.broadcast_to(d_mod[None], (n, 6 * D)), bias_part], 1)
    got = lax.all_to_all(sent, "fsdp", 0, 0, tiled=True)
    d_modulation = got[:, : 6 * D]
    bias_sum = jnp.sum(got[:, 6 * D :], 0).reshape(2, -1)
    bias_own = pick((bias_sum[0], bias_sum[1]))[0]
    mod_sum = jnp.sum(d_modulation, 0)
    ada_b_grad = lax.dynamic_index_in_dim(
        mod_sum.reshape(nd, 6 * D // nd), 2 * me + core, 0, keepdims=False
    )
    ada_w_grad = lax.dot_general(
        condition.astype(f32), d_modulation, (((0,), (0,)), ((), ())), precision=highest
    )
    d_condition = lax.dot_general(
        ada_w.astype(f32), d_modulation, (((1,), (1,)), ((), ())), precision=highest
    )
    d_embedded = jax.vjp(jax.nn.silu, embedded.T)[1](d_condition)[0]
    d_embedded = lax.all_to_all(
        jnp.broadcast_to(d_embedded[None], (nd, cols, n)), BOTH, 0, 0, tiled=True
    ).reshape(D, n)

    def table_grad(which):
        own = (2 * me + core) * table_rows + lax.broadcasted_iota(jnp.int32, (table_rows, n), 0)
        mask = (all_ids[:, which][None] == own).astype(f32)
        return lax.dot_general(mask, d_embedded, (((1,), (1,)), ((), ())), precision=highest)

    def to_rows(grad):
        pair = grad.reshape(2, rows, grad.shape[1])
        mine, others = pick((pair[0], pair[1]))
        return pick((mine, other_core(others)))

    fp = to_rows(fc1_proj_grad)
    fc1_w_grad = jnp.stack(
        [x[:, : FF // 2].reshape(rows, n, ff_rows) for x in fp], 2
    ).reshape(rows, FF)
    proj_w_grad = jnp.concatenate([x[:, FF // 2 :] for x in fp], 1)
    qkv_w_grad = jnp.stack([x.reshape(rows, 3, half) for x in to_rows(qkv_grad)], 2).reshape(
        rows, 3 * D
    )
    a, b, c = ff_rows, ff_rows + D // n, ff_rows + D // n + rows
    return (
        output[None],
        latents_grad[None],
        table_grad(0),
        table_grad(1),
        ada_w_grad,
        ada_b_grad,
        qkv_w_grad,
        bias_own[a:b],
        proj_w_grad,
        bias_own[b:c],
        fc1_w_grad,
        bias_own[:a],
        fc2_grad,
        bias_own[c:],
    )


def solution(mesh):
    assert mesh.shape["seq"] == 2
    chips = Chips(mesh.shape["fsdp"])
    tokens = P("fsdp", "seq", None)
    matrix = P(BOTH, None)
    vector = P(BOTH)
    in_specs = (tokens, P("fsdp"), P("fsdp")) + (matrix,) * 3 + (vector, matrix) * 4 + (vector, tokens)
    in_specs = (
        tokens,
        P("fsdp"),
        P("fsdp"),
        matrix,
        matrix,
        matrix,
        vector,
        matrix,
        vector,
        matrix,
        vector,
        matrix,
        vector,
        matrix,
        vector,
        tokens,
    )
    out_specs = (
        tokens,
        tokens,
        matrix,
        matrix,
        matrix,
        vector,
        matrix,
        vector,
        matrix,
        vector,
        matrix,
        vector,
        matrix,
        vector,
    )
    return jax.shard_map(
        functools.partial(shards, chips),
        mesh=mesh,
        in_specs=in_specs,
        out_specs=out_specs,
        check_vma=False,
    )
```

time: 1390 us -> 282 us (0.20)
  waiting for transfers between devices: 1190 us -> 110 us
  blocking collectives: 88.1 us -> 0 us
  starting transfers between devices: 0.86 us -> 51.3 us
  matrix products: 60.1 us -> 25.7 us
  local copies, waits for them, and re-layouts: 14.1 us -> 44.1 us
  other arithmetic: 17.5 us -> 40.1 us
    reduce_scatter x9 -> x0, waiting for transfers between devices: 822 us -> none  [the longest x1 168 us: shards(): lax.psum_scatter(ada_grad, ('fsdp', 'seq'), scatter_dimension=0, tiled=True)]
    all_gather x7 -> x0, waiting for transfers between devices: 361 us -> none  [the longest x1 71.9 us: shards(): lax.all_gather(ada_w, ('fsdp', 'seq'), axis=0, tiled=True)]
    ppermute x0 -> x37, waiting for transfers between devices: none -> 95.5 us  [the longest x24 95.4 us: step(): return lax.ppermute(x, BOTH, pairs)]
    unnamed x2 -> x0, blocking collectives: 83.8 us -> none
    dot_general x22 -> x24, matrix products: 60.1 us -> 25.7 us  [the longest x4 6.9 us: dot_t(): lax.dot_general(a, b, (((0,), (0,)), ((), ())), preferred_element_type=f32)]
    ppermute x0 -> x37, starting transfers between devices: none -> 29.2 us  [the longest x24 26.8 us: step(): return lax.ppermute(x, BOTH, pairs)]
    all_to_all x0 -> x4, starting transfers between devices: none -> 22.1 us  [the longest x1 7.3 us: shards(): got = lax.all_to_all(sent, BOTH, 0, 0, tiled=True)]
    slice x1 -> x37, local copies, waits for them, and re-layouts: 0.02 us -> 16.1 us  [the longest x3 3.45 us: scatter(): recv = self.step(blocks[half:], self.bits - 1)]
  transfers between devices with their start and end apart: 16 -> 41, of which waited for: 16 -> 16; matrix products, arithmetic and copies ran while one was open for 5% -> 29% of each run, Pallas kernels for 0% -> 2%
where the time goes in v1:
time: 282 us; the launch traced here: 280 us
  waiting for transfers between devices  110 us (39%)
  starting transfers between devices  51.3 us (18%)
  local copies, waits for them, and re-layouts  44.1 us (16%)
  other arithmetic  40.1 us (14%)
  matrix products  25.7 us (9%)
  Pallas kernels  5.19 us (2%)
  between operations  3.65 us (1%)
    ppermute x24, waiting for transfers between devices, step(): return lax.ppermute(x, BOTH, pairs)  95.4 us
    ppermute x24, starting transfers between devices, step(): return lax.ppermute(x, BOTH, pairs)  26.8 us
    unnamed x166, local copies, waits for them, and re-layouts  10.8 us
    concatenate x9, other arithmetic, gather(): held = jnp.concatenate([held, self.step(held, k)], 0)  8.71 us
    all_to_all x1, waiting for transfers between devices, shards(): got = lax.all_to_all(sent, 'fsdp', 0, 0, tiled=True)  8.01 us
    all_to_all x1, starting transfers between devices, shards(): got = lax.all_to_all(sent, BOTH, 0, 0, tiled=True)  7.3 us
    dot_general x4, matrix products, dot_t(): lax.dot_general(a, b, (((0,), (0,)), ((), ())), preferred_element_type=f32)  6.9 us
    all_to_all x1, waiting for transfers between devices, shards(): lax.all_to_all(jnp.broadcast_to(d_embedded[None], (nd, cols, n)), BOTH, 0...  6.5 us
  transfers between devices with their start and end apart: 41, of which 16 were waited for; matrix products, arithmetic and copies ran while one was open for 29% of the time, Pallas kernels for 2%

profile of v1, /device:TPU:0, one launch (start us, length us, event | category | flops | bytes accessed | tf_op | source)
XLA Modules:
  0.0 280.1 jit_solution(1176269626047137651)
XLA Ops:
  2.2 3.4 %concatenate.110 = bf16[340]{0:T(512)(128)(2,1)S(1)} concatenate(bf16[96]{0:T(256)(128)(2,1)} %param.28, bf16[48]{0:T(256)(128)(2,1)} %param.24, bf16[24]{0:T(256)(128)(2,1)} %param.26, bf16[24]{0:T(256)(128)(2,1)} %param.30, bf16[144]{0:T(256)(128)(2,1)} %param.22, bf16[2]{0:T(256)(128)(2,1)S(1)} %fusion.72, bf16[2]{0:T(256)(128)(2,1)S(1)} %get-tuple-element.39), dimensions={0} | concatenate | bytes 1360 | tf_op jit(solution)/shard_map/concatenate | solution.py:204
  7.7 7.3 %all-to-all-start = ((bf16[32,2,960]{2,1,0:T(2,128)(2,1)}), bf16[32,2,960]{2,1,0:T(2,128)(2,1)S(1)}, u32[]{:S(2)}, u32[]{:S(2)}) async-start(bf16[32,2,960]{2,1,0:T(2,128)(2,1)} %reshape.487), calls=%async_computation | async-start | bytes 262144 | tf_op jit(solution)/shard_map/all_to_all | solution.py:211
  24.4 2.4 collective-permute-start.15
  27.5 2.4 collective-permute-start.4
  29.9 3.5 %collective-permute-done.10 = bf16[1,48,1536]{2,1,0:T(8,128)(2,1)S(1)} collective-permute-done((bf16[1,48,1536]{2,1,0:T(8,128)(2,1)S(1)}, bf16[1,48,1536]{2,1,0:T(8,128)(2,1)S(1)}, u32[]{:S(2)}, u32[]{:S(2)}) %collective-permute-start.10) | collective-permute-done | bytes 147488 | tf_op jit(solution)/shard_map/ppermute | solution.py:58
  38.2 6.4 %all-to-all-start.1 = ((f32[16,36,128]{2,1,0:T(8,128)}), f32[16,36,128]{2,1,0:T(8,128)S(1)}, u32[]{:S(2)}, u32[]{:S(2)}) async-start(f32[16,36,128]{2,1,0:T(8,128)} %reshape.433), calls=%async_computation.1 | async-start | bytes 655360 | tf_op jit(solution)/shard_map/all_to_all | solution.py:236
  44.9 19.4 %collective-permute-done.4 = bf16[2,48,1536]{2,1,0:T(8,128)(2,1)} collective-permute-done((bf16[2,48,1536]{2,1,0:T(8,128)(2,1)}, bf16[2,48,1536]{2,1,0:T(8,128)(2,1)}, u32[]{:S(2)}, u32[]{:S(2)}) %collective-permute-start.4) | collective-permute-done | bytes 294944 | tf_op jit(solution)/shard_map/ppermute | solution.py:58
  68.4 7.7 %collective-permute-done.5 = bf16[4,48,1536]{2,1,0:T(8,128)(2,1)S(1)} collective-permute-done((bf16[4,48,1536]{2,1,0:T(8,128)(2,1)S(1)}, bf16[4,48,1536]{2,1,0:T(8,128)(2,1)S(1)}, u32[]{:S(2)}, u32[]{:S(2)}) %collective-permute-start.5) | collective-permute-done | bytes 589856 | tf_op jit(solution)/shard_map/ppermute | solution.py:58
  76.2 2.1 pad_maximum_fusion.refs_0_
  83.2 13.1 %collective-permute-done.16 = bf16[4,96,768]{2,1,0:T(8,128)(2,1)} collective-permute-done((bf16[4,96,768]{2,1,0:T(8,128)(2,1)S(1)}, bf16[4,96,768]{2,1,0:T(8,128)(2,1)}, u32[]{:S(2)}, u32[]{:S(2)}) %collective-permute-start.16) | collective-permute-done | bytes 589856 | tf_op jit(solution)/shard_map/ppermute | solution.py:58
  98.0 10.8 %collective-permute-done.12 = bf16[4,48,1536]{2,1,0:T(8,128)(2,1)S(1)} collective-permute-done((bf16[4,48,1536]{2,1,0:T(8,128)(2,1)S(1)}, bf16[4,48,1536]{2,1,0:T(8,128)(2,1)S(1)}, u32[]{:S(2)}, u32[]{:S(2)}) %collective-permute-start.12) | collective-permute-done | bytes 589856 | tf_op jit(solution)/shard_map/ppermute | solution.py:58
  134.8 2.2 fusion.86
  138.2 2.0 fusion.81
  150.3 2.7 convolution_convert_fusion.1
  186.9 4.5 %all-to-all-start.2 = ((f32[16,1,4992]{2,1,0:T(1,128)}), f32[16,1,4992]{2,1,0:T(1,128)S(1)}, u32[]{:S(2)}, u32[]{:S(2)}) async-start(f32[16,1,4992]{2,1,0:T(1,128)} %all_to_all.19), calls=%async_computation.2 | async-start | bytes 638976 | tf_op jit(solution)/shard_map/all_to_all | solution.py:358
  196.0 8.0 %collective-permute-done.34 = bf16[4,96,768]{2,1,0:T(8,128)(2,1)} collective-permute-done((bf16[4,96,768]{2,1,0:T(8,128)(2,1)}, bf16[4,96,768]{2,1,0:T(8,128)(2,1)}, u32[]{:S(2)}, u32[]{:S(2)}) %collective-permute-start.34) | collective-permute-done | bytes 589856 | tf_op jit(solution)/shard_map/ppermute | solution.py:58
  206.4 8.0 %all-to-all-done.2 = f32[16,1,4992]{2,1,0:T(1,128)S(1)} async-done(((f32[16,1,4992]{2,1,0:T(1,128)}), f32[16,1,4992]{2,1,0:T(1,128)S(1)}, u32[]{:S(2)}, u32[]{:S(2)}) %all-to-all-start.2) | async-done | bytes 319520 | tf_op jit(solution)/shard_map/all_to_all | solution.py:358
  218.7 3.9 %all-to-all-start.3 = ((f32[32,1,384]{2,1,0:T(1,128)}), f32[32,1,384]{2,1,0:T(1,128)S(1)}, u32[]{:S(2)}, u32[]{:S(2)}) async-start(f32[32,1,384]{2,1,0:T(1,128)} %reshape.489), calls=%async_computation.3 | async-start | bytes 98304 | tf_op jit(solution)/shard_map/all_to_all | solution.py:373
  223.2 6.5 %all-to-all-done.3 = f32[32,1,384]{2,1,0:T(1,128)S(1)} async-done(((f32[32,1,384]{2,1,0:T(1,128)}), f32[32,1,384]{2,1,0:T(1,128)S(1)}, u32[]{:S(2)}, u32[]{:S(2)}) %all-to-all-start.3) | async-done | bytes 49184 | tf_op jit(solution)/shard_map/all_to_all | solution.py:373
  241.0 2.2 collective-permute-done.36
  243.9 6.6 %collective-permute-done.24 = bf16[2,48,1152]{2,1,0:T(8,128)(2,1)S(1)} collective-permute-done((bf16[2,48,1152]{2,1,0:T(8,128)(2,1)S(1)}, bf16[2,48,1152]{2,1,0:T(8,128)(2,1)S(1)}, u32[]{:S(2)}, u32[]{:S(2)}) %collective-permute-start.24) | collective-permute-done | bytes 221216 | tf_op jit(solution)/shard_map/ppermute | solution.py:58
  252.2 2.3 collective-permute-start.30
  256.2 13.8 %collective-permute-done.30 = bf16[2,48,1920]{2,1,0:T(8,128)(2,1)S(1)} collective-permute-done((bf16[2,48,1920]{2,1,0:T(8,128)(2,1)S(1)}, bf16[2,48,1920]{2,1,0:T(8,128)(2,1)S(1)}, u32[]{:S(2)}, u32[]{:S(2)}) %collective-permute-start.30) | collective-permute-done | bytes 368672 | tf_op jit(solution)/shard_map/ppermute | solution.py:58
  270.6 5.4 %collective-permute-done.31 = bf16[1,48,1920]{2,1,0:T(8,128)(2,1)S(1)} collective-permute-done((bf16[1,48,1920]{2,1,0:T(8,128)(2,1)S(1)}, bf16[1,48,1920]{2,1,0:T(8,128)(2,1)S(1)}, u32[]{:S(2)}, u32[]{:S(2)}) %collective-permute-start.31) | collective-permute-done | bytes 184352 | tf_op jit(solution)/shard_map/ppermute | solution.py:58
  (440 shorter events, 129.9 us)
Async XLA Ops:
  7.7 26.5 %all-to-all-start = ((bf16[32,2,960]{2,1,0:T(2,128)(2,1)}), bf16[32,2,960]{2,1,0:T(2,128)(2,1)S(1)}, u32[]{:S(2)}, u32[]{:S(2)}) async-start(bf16[32,2,960]{2,1,0:T(2,128)(2,1)} %reshape.487), calls=%async_computation | async-start | bytes 262144 | tf_op jit(solution)/shard_map/all_to_all | solution.py:211
  18.3 26.4 %collective-permute-start = (bf16[2,128,768]{2,1,0:T(8,128)(2,1)S(1)}, bf16[2,128,768]{2,1,0:T(8,128)(2,1)S(1)}, u32[]{:S(2)}, u32[]{:S(2)}) collective-permute-start(bf16[2,128,768]{2,1,0:T(8,128)(2,1)S(1)} %constant_dynamic-update-slice_fusion), channel_id=1, source_target_pairs={{0,1},{1,0},{2,3},{3,2},{4,5},{5,4},{6,7},{7,6},{8,9},{9,8},{10,11... | collective-permute-start | bytes 1179656 | tf_op jit(solution)/shard_map/ppermute | solution.py:141
  20.0 13.4 %collective-permute-start.10 = (bf16[1,48,1536]{2,1,0:T(8,128)(2,1)S(1)}, bf16[1,48,1536]{2,1,0:T(8,128)(2,1)S(1)}, u32[]{:S(2)}, u32[]{:S(2)}) collective-permute-start(bf16[1,48,1536]{2,1,0:T(8,128)(2,1)S(1)} %maximum_bitcast_fusion.1), channel_id=1, source_target_pairs={{0,8},{1,9},{2,10},{3,11},{4,12},{5,13},{6,14},{7,15},{8,0},{9,1},... | collective-permute-start | bytes 442376 | tf_op jit(solution)/shard_map/ppermute | solution.py:58
  24.4 55.4 %collective-permute-start.15 = (bf16[2,96,768]{2,1,0:T(8,128)(2,1)}, bf16[2,96,768]{2,1,0:T(8,128)(2,1)S(1)}, u32[]{:S(2)}, u32[]{:S(2)}) collective-permute-start(bf16[2,96,768]{2,1,0:T(8,128)(2,1)} %pad_maximum_fusion.16), channel_id=1, source_target_pairs={{0,16},{1,17},{2,18},{3,19},{4,20},{5,21},{6,22},{7,23},{8,24},{9,... | collective-permute-start | bytes 884744 | tf_op jit(solution)/shard_map/ppermute | solution.py:58
  27.5 36.8 %collective-permute-start.4 = (bf16[2,48,1536]{2,1,0:T(8,128)(2,1)}, bf16[2,48,1536]{2,1,0:T(8,128)(2,1)}, u32[]{:S(2)}, u32[]{:S(2)}) collective-permute-start(bf16[2,48,1536]{2,1,0:T(8,128)(2,1)} %pad_maximum_fusion.14), channel_id=1, source_target_pairs={{0,16},{1,17},{2,18},{3,19},{4,20},{5,21},{6,22},{7,23},{8,24},{9,... | collective-permute-start | bytes 884744 | tf_op jit(solution)/shard_map/ppermute | solution.py:58
  34.2 47.4 %collective-permute-start.11 = (bf16[2,48,1536]{2,1,0:T(8,128)(2,1)}, bf16[2,48,1536]{2,1,0:T(8,128)(2,1)}, u32[]{:S(2)}, u32[]{:S(2)}) collective-permute-start(bf16[2,48,1536]{2,1,0:T(8,128)(2,1)} %pad_maximum_fusion.15), channel_id=1, source_target_pairs={{0,16},{1,17},{2,18},{3,19},{4,20},{5,21},{6,22},{7,23},{8,24},{9,... | collective-permute-start | bytes 884744 | tf_op jit(solution)/shard_map/ppermute | solution.py:58
  38.2 43.2 %all-to-all-start.1 = ((f32[16,36,128]{2,1,0:T(8,128)}), f32[16,36,128]{2,1,0:T(8,128)S(1)}, u32[]{:S(2)}, u32[]{:S(2)}) async-start(f32[16,36,128]{2,1,0:T(8,128)} %reshape.433), calls=%async_computation.1 | async-start | bytes 655360 | tf_op jit(solution)/shard_map/all_to_all | solution.py:236
  78.3 32.2 %collective-permute-start.6 = (bf16[8,48,1536]{2,1,0:T(8,128)(2,1)}, bf16[8,48,1536]{2,1,0:T(8,128)(2,1)}, u32[]{:S(2)}, u32[]{:S(2)}) collective-permute-start(bf16[8,48,1536]{2,1,0:T(8,128)(2,1)} %pad_maximum_fusion.refs_0_), channel_id=1, source_target_pairs={{0,4},{1,3},{2,6},{3,1},{4,0},{5,7},{6,2},{7,5},{8,12},{9,11},{10,... | collective-permute-start | bytes 3538952 | tf_op jit(solution)/shard_map/ppermute | solution.py:58
  79.8 16.4 %collective-permute-start.16 = (bf16[4,96,768]{2,1,0:T(8,128)(2,1)S(1)}, bf16[4,96,768]{2,1,0:T(8,128)(2,1)}, u32[]{:S(2)}, u32[]{:S(2)}) collective-permute-start(bf16[4,96,768]{2,1,0:T(8,128)(2,1)S(1)} %pad_maximum_fusion.6), channel_id=1, source_target_pairs={{0,2},{1,5},{2,0},{3,7},{4,6},{5,1},{6,4},{7,3},{8,10},{9,13},{10,... | collective-permute-start | bytes 1769480 | tf_op jit(solution)/shard_map/ppermute | solution.py:58
  82.6 26.2 %collective-permute-start.12 = (bf16[4,48,1536]{2,1,0:T(8,128)(2,1)S(1)}, bf16[4,48,1536]{2,1,0:T(8,128)(2,1)S(1)}, u32[]{:S(2)}, u32[]{:S(2)}) collective-permute-start(bf16[4,48,1536]{2,1,0:T(8,128)(2,1)S(1)} %pad_maximum_fusion.5), channel_id=1, source_target_pairs={{0,2},{1,5},{2,0},{3,7},{4,6},{5,1},{6,4},{7,3},{8,10},{9,13},{10,... | collective-permute-start | bytes 1769480 | tf_op jit(solution)/shard_map/ppermute | solution.py:58
  97.5 33.1 %collective-permute-start.17 = (bf16[8,96,768]{2,1,0:T(8,128)(2,1)S(1)}, bf16[8,96,768]{2,1,0:T(8,128)(2,1)}, u32[]{:S(2)}, u32[]{:S(2)}) collective-permute-start(bf16[8,96,768]{2,1,0:T(8,128)(2,1)S(1)} %pad_maximum_fusion.2.refs_0_), channel_id=1, source_target_pairs={{0,4},{1,3},{2,6},{3,1},{4,0},{5,7},{6,2},{7,5},{8,12},{9,11},{10,... | collective-permute-start | bytes 3538952 | tf_op jit(solution)/shard_map/ppermute | solution.py:58
  109.9 22.2 %collective-permute-start.13 = (bf16[8,48,1536]{2,1,0:T(8,128)(2,1)S(1)}, bf16[8,48,1536]{2,1,0:T(8,128)(2,1)}, u32[]{:S(2)}, u32[]{:S(2)}) collective-permute-start(bf16[8,48,1536]{2,1,0:T(8,128)(2,1)S(1)} %pad_maximum_fusion.1.refs_0_), channel_id=1, source_target_pairs={{0,4},{1,3},{2,6},{3,1},{4,0},{5,7},{6,2},{7,5},{8,12},{9,11},{10,... | collective-permute-start | bytes 3538952 | tf_op jit(solution)/shard_map/ppermute | solution.py:58
  113.3 13.3 %collective-permute-start.7 = (bf16[384,384]{1,0:T(8,128)(2,1)}, bf16[384,384]{1,0:T(8,128)(2,1)}, u32[]{:S(2)}, u32[]{:S(2)}) collective-permute-start(bf16[384,384]{1,0:T(8,128)(2,1)} %bitcast.16), channel_id=1, source_target_pairs={{0,1},{1,0},{2,3},{3,2},{4,5},{5,4},{6,7},{7,6},{8,9},{9,8},{10,11... | collective-permute-start | bytes 884744 | tf_op jit(solution)/shard_map/ppermute | solution.py:141
  147.4 24.7 %collective-permute-start.18 = (f32[128,768]{1,0:T(8,128)}, f32[128,768]{1,0:T(8,128)}, u32[]{:S(2)}, u32[]{:S(2)}) collective-permute-start(f32[128,768]{1,0:T(8,128)} %slice.484), channel_id=1, source_target_pairs={{0,1},{1,0},{2,3},{3,2},{4,5},{5,4},{6,7},{7,6},{8,9},{9,8},{10,11... | collective-permute-start | bytes 1179656 | tf_op jit(solution)/shard_map/ppermute | solution.py:141
  148.6 31.8 %collective-permute-start.33 = (bf16[8,96,768]{2,1,0:T(8,128)(2,1)}, bf16[8,96,768]{2,1,0:T(8,128)(2,1)}, u32[]{:S(2)}, u32[]{:S(2)}) collective-permute-start(bf16[8,96,768]{2,1,0:T(8,128)(2,1)} %slice.530), channel_id=1, source_target_pairs={{0,4},{1,3},{2,6},{3,1},{4,0},{5,7},{6,2},{7,5},{8,12},{9,11},{10,... | collective-permute-start | bytes 3538952 | tf_op jit(solution)/shard_map/ppermute | solution.py:58
  170.8 20.5 %collective-permute-start.22 = (bf16[8,48,1152]{2,1,0:T(8,128)(2,1)}, bf16[8,48,1152]{2,1,0:T(8,128)(2,1)}, u32[]{:S(2)}, u32[]{:S(2)}) collective-permute-start(bf16[8,48,1152]{2,1,0:T(8,128)(2,1)} %slice.503), channel_id=1, source_target_pairs={{0,4},{1,3},{2,6},{3,1},{4,0},{5,7},{6,2},{7,5},{8,12},{9,11},{10,... | collective-permute-start | bytes 2654216 | tf_op jit(solution)/shard_map/ppermute | solution.py:58
  177.4 61.2 %collective-permute-start.28 = (bf16[8,48,1920]{2,1,0:T(8,128)(2,1)}, bf16[8,48,1920]{2,1,0:T(8,128)(2,1)}, u32[]{:S(2)}, u32[]{:S(2)}) collective-permute-start(bf16[8,48,1920]{2,1,0:T(8,128)(2,1)} %slice.516), channel_id=1, source_target_pairs={{0,4},{1,3},{2,6},{3,1},{4,0},{5,7},{6,2},{7,5},{8,12},{9,11},{10,... | collective-permute-start | bytes 4423688 | tf_op jit(solution)/shard_map/ppermute | solution.py:58
  184.8 19.1 %collective-permute-start.34 = (bf16[4,96,768]{2,1,0:T(8,128)(2,1)}, bf16[4,96,768]{2,1,0:T(8,128)(2,1)}, u32[]{:S(2)}, u32[]{:S(2)}) collective-permute-start(bf16[4,96,768]{2,1,0:T(8,128)(2,1)} %slice.686), channel_id=1, source_target_pairs={{0,2},{1,5},{2,0},{3,7},{4,6},{5,1},{6,4},{7,3},{8,10},{9,13},{10,... | collective-permute-start | bytes 1769480 | tf_op jit(solution)/shard_map/ppermute | solution.py:58
  186.9 27.5 %all-to-all-start.2 = ((f32[16,1,4992]{2,1,0:T(1,128)}), f32[16,1,4992]{2,1,0:T(1,128)S(1)}, u32[]{:S(2)}, u32[]{:S(2)}) async-start(f32[16,1,4992]{2,1,0:T(1,128)} %all_to_all.19), calls=%async_computation.2 | async-start | bytes 638976 | tf_op jit(solution)/shard_map/all_to_all | solution.py:358
  194.0 42.7 %collective-permute-start.23 = (bf16[4,48,1152]{2,1,0:T(8,128)(2,1)}, bf16[4,48,1152]{2,1,0:T(8,128)(2,1)}, u32[]{:S(2)}, u32[]{:S(2)}) collective-permute-start(bf16[4,48,1152]{2,1,0:T(8,128)(2,1)} %slice.687), channel_id=1, source_target_pairs={{0,2},{1,5},{2,0},{3,7},{4,6},{5,1},{6,4},{7,3},{8,10},{9,13},{10,... | collective-permute-start | bytes 1327112 | tf_op jit(solution)/shard_map/ppermute | solution.py:58
  206.4 28.5 %collective-permute-start.35 = (bf16[2,96,768]{2,1,0:T(8,128)(2,1)}, bf16[2,96,768]{2,1,0:T(8,128)(2,1)}, u32[]{:S(2)}, u32[]{:S(2)}) collective-permute-start(bf16[2,96,768]{2,1,0:T(8,128)(2,1)} %slice.689), channel_id=1, source_target_pairs={{0,16},{1,17},{2,18},{3,19},{4,20},{5,21},{6,22},{7,23},{8,24},{9,... | collective-permute-start | bytes 884744 | tf_op jit(solution)/shard_map/ppermute | solution.py:58
  237.9 12.6 %collective-permute-start.24 = (bf16[2,48,1152]{2,1,0:T(8,128)(2,1)S(1)}, bf16[2,48,1152]{2,1,0:T(8,128)(2,1)S(1)}, u32[]{:S(2)}, u32[]{:S(2)}) collective-permute-start(bf16[2,48,1152]{2,1,0:T(8,128)(2,1)S(1)} %slice.690), channel_id=1, source_target_pairs={{0,16},{1,17},{2,18},{3,19},{4,20},{5,21},{6,22},{7,23},{8,24},{9,... | collective-permute-start | bytes 663560 | tf_op jit(solution)/shard_map/ppermute | solution.py:58
  240.4 11.5 %collective-permute-start.29 = (bf16[4,48,1920]{2,1,0:T(8,128)(2,1)S(1)}, bf16[4,48,1920]{2,1,0:T(8,128)(2,1)S(1)}, u32[]{:S(2)}, u32[]{:S(2)}) collective-permute-start(bf16[4,48,1920]{2,1,0:T(8,128)(2,1)S(1)} %slice.685), channel_id=1, source_target_pairs={{0,2},{1,5},{2,0},{3,7},{4,6},{5,1},{6,4},{7,3},{8,10},{9,13},{10,... | collective-permute-start | bytes 2211848 | tf_op jit(solution)/shard_map/ppermute | solution.py:58
  252.2 17.9 %collective-permute-start.30 = (bf16[2,48,1920]{2,1,0:T(8,128)(2,1)S(1)}, bf16[2,48,1920]{2,1,0:T(8,128)(2,1)S(1)}, u32[]{:S(2)}, u32[]{:S(2)}) collective-permute-start(bf16[2,48,1920]{2,1,0:T(8,128)(2,1)S(1)} %slice.688), channel_id=1, source_target_pairs={{0,16},{1,17},{2,18},{3,19},{4,20},{5,21},{6,22},{7,23},{8,24},{9,... | collective-permute-start | bytes 1105928 | tf_op jit(solution)/shard_map/ppermute | solution.py:58
  (92 other events, 671.0 us)

commit v2 on v1

v2 whole, which is shorter than its diff:
```python
import functools

import jax
import jax.numpy as jnp
from jax import lax
from jax.experimental import pallas as pl
from jax.experimental.pallas import tpu as pltpu
from jax.sharding import PartitionSpec as P

HD = 64
norm_eps = 1e-06
highest = lax.Precision.HIGHEST
f32 = jnp.float32
bf16 = jnp.bfloat16
BOTH = ("fsdp", "seq")


def dot(a, b, out=f32):
    return jnp.dot(a, b, preferred_element_type=f32).astype(out)


def dot_t(a, b, out=f32):
    return lax.dot_general(a, b, (((0,), (0,)), ((), ())), preferred_element_type=f32).astype(out)


def dot_nt(a, b, out=f32):
    return lax.dot_general(a, b, (((1,), (1,)), ((), ())), preferred_element_type=f32).astype(out)


class Chips:
    def __init__(self, count):
        self.count = count
        self.ring = count // 4
        assert count == 4 * self.ring
        self.back = self.ring // 2
        self.ahead = self.ring - 1 - self.back
        self.offsets = [0]
        self.offsets += [-j for j in range(1, self.back + 1)]
        self.offsets += list(range(1, self.ahead + 1))

    def shift(self, x, by):
        pairs = [(i, (i + 4 * by) % self.count) for i in range(self.count)]
        with jax.named_scope(f"ring_by_{by % self.ring}"):
            return lax.ppermute(x, "fsdp", pairs)

    def swap(self, x, last):
        pairs = [
            (2 * i + core, 2 * (i ^ (1 << (core ^ last))) + core)
            for i in range(self.count)
            for core in range(2)
        ]
        with jax.named_scope("last_swap" if last else "first_swap"):
            return lax.ppermute(x, BOTH, pairs)

    def places(self, ring_first):
        me, core = lax.axis_index("fsdp"), lax.axis_index("seq")
        outer, inner = me // 4, me % 4
        places = []
        for r in range(self.count):
            swaps, place = (r // self.ring, r % self.ring) if ring_first else (r % 4, r // 4)
            a, b = swaps % 2, swaps // 2
            flip = jnp.where(core == 0, a + 2 * b, 2 * a + b)
            place = lax.rem(outer + self.offsets[place] + self.ring, self.ring)
            places.append(4 * place + jnp.bitwise_xor(inner, flip))
        return places

    def ring_gather(self, blocks, direct, tie=None):
        held = [blocks]
        if direct:
            return held + [self.shift(blocks, -offset) for offset in self.offsets[1:]], tie
        up, down = self.shift(blocks, 1), self.shift(blocks, -1)
        if tie is not None:
            (up, down), tie = after((up, down), tie)
        for count, by, moved in ((self.back, 1, up), (self.ahead, -1, down)):
            for j in range(count):
                moved = self.shift(moved, by) if j else moved
                held.append(moved)
        return held, tie

    def direct_scatter(self, blocks):
        return [self.shift(x.astype(bf16), o) for x, o in zip(blocks[1:], self.offsets[1:])]

    def ring_scatter(self, blocks):
        total = blocks[0].astype(f32)
        early = []
        for first, last, by in ((self.back, 1, -1), (self.ring - 1, self.back + 1, 1)):
            term = None
            for r in range(first, last - 1, -1):
                term = blocks[r] if term is None else blocks[r].astype(f32) + term
                term = self.shift(term.astype(bf16), by)
                if r == first:
                    early.append(term)
                term = term.astype(f32)
            if term is not None:
                total = total + term
        return total, early

    def swap_add(self, kept, sent, last):
        got = self.swap(sent, last)
        half = kept.shape[0] // 2
        return [
            (kept[i * half : (i + 1) * half].astype(f32) + got[i * half : (i + 1) * half].astype(f32))
            for i in range(2)
        ]


def after(x, earlier):
    return lax.optimization_barrier((x, earlier))


def turned(chips, place):
    return lax.rem(place + lax.axis_index("seq") * (chips.count // 2), chips.count)


def place_kernel(chips, ring_first, sizes, widths, *refs):
    ins, outs = refs[: len(sizes)], refs[len(sizes) :]
    places = chips.places(ring_first)
    r = 0
    for ref, size in zip(ins, sizes):
        for i in range(size):
            outs[0][places[r]] = ref[i, :, : widths[0]]
            if len(outs) > 1:
                outs[1][turned(chips, places[r])] = ref[i, :, widths[0] :]
            r += 1


def relative_kernel(chips, ring_first, count, width, *refs):
    ins, outs = refs[:-count], refs[-count:]
    size, half = chips.count // count, chips.count // 2
    for r, place in enumerate(chips.places(ring_first)):
        outs[r // size][r % size, :, :width] = ins[0][place]
        if len(ins) > 1:
            at = turned(chips, place)
            low = ins[1][jnp.minimum(at, half - 1)]
            high = ins[2][jnp.maximum(at - half, 0)]
            outs[r // size][r % size, :, width:] = jnp.where(at < half, low, high)


def kernel(body, name, outs, *args, flops=0):
    shapes = [jax.ShapeDtypeStruct(shape, dtype) for shape, dtype in outs]
    moved = sum(x.size * x.dtype.itemsize for x in (*args, *shapes))
    return pl.pallas_call(
        body,
        out_shape=shapes,
        in_specs=[pl.BlockSpec(memory_space=pltpu.VMEM)] * len(args),
        out_specs=[pl.BlockSpec(memory_space=pltpu.VMEM)] * len(shapes),
        compiler_params=pltpu.CompilerParams(vmem_limit_bytes=16 << 20),
        cost_estimate=pl.CostEstimate(flops=flops, bytes_accessed=moved, transcendentals=0),
        name=name,
    )(*args)


def place(chips, ring_first, parts, widths):
    rows = parts[0].shape[1]
    if rows % 16 or any(w % 128 for w in widths):
        held = jnp.concatenate(parts, 0)
        places = jnp.stack(chips.places(ring_first))
        outs = [jnp.zeros_like(held).at[places].set(held)[:, :, : widths[0]]]
        if len(widths) > 1:
            held = held[:, :, widths[0] :]
            outs.append(jnp.zeros_like(held).at[turned(chips, places)].set(held))
        return outs
    body = functools.partial(place_kernel, chips, ring_first, [p.shape[0] for p in parts], widths)
    outs = [((chips.count, rows, w), parts[0].dtype) for w in widths]
    return kernel(body, "place", outs, *parts)


def relative(chips, ring_first, count, arrays):
    rows, width = arrays[0].shape[1:]
    widths = [a.shape[2] for a in arrays[:2]]
    if rows % 16 or any(w % 128 for w in widths):
        places = jnp.stack(chips.places(ring_first))
        held = arrays[0][places]
        if len(arrays) > 1:
            second = jnp.concatenate(arrays[1:], 0)[turned(chips, places)]
            held = jnp.concatenate([held, second], 2)
        return jnp.split(held, count)
    body = functools.partial(relative_kernel, chips, ring_first, count, width)
    shape = (chips.count // count, rows, sum(widths))
    return kernel(body, "relative", [(shape, arrays[0].dtype)] * count, *arrays)


def tiles(length, tile, body):
    def step(i, carry):
        body(pl.ds(pl.multiple_of(i * tile, tile), tile))
        return carry

    lax.fori_loop(0, length // tile, step, 0)


def normalize(v):
    center = v - jnp.mean(v, -1, keepdims=True)
    scale = lax.rsqrt(jnp.mean(center * center, -1, keepdims=True) + norm_eps)
    return center * scale, scale


def normalize_back(g, normed, scale):
    along = jnp.mean(g * normed, -1, keepdims=True)
    return scale * (g - jnp.mean(g, -1, keepdims=True) - normed * along)


def both(part, got):
    own = part.shape[0] // 2
    return part + jnp.concatenate([got[own:], got[:own]], 0)


def attention_kernel(x_ref, mod_ref, w_ref, b_ref, normed_ref, qkv_ref, att_ref, log_ref):
    normed = normalize(x_ref[...].astype(f32))[0]
    normed_ref[...] = (normed * (1.0 + mod_ref[1:2]) + mod_ref[0:1]).astype(bf16)
    half = att_ref.shape[1]
    for j in range(3):
        part = dot(normed_ref[...], w_ref[:, half * j : half * (j + 1)])
        if j != 1:
            part = part + b_ref[j // 2 : j // 2 + 1]
        qkv_ref[:, half * j : half * (j + 1)] = part.astype(bf16)
    lanes = lax.broadcasted_iota(jnp.int32, log_ref.shape, 1)
    logs = jnp.zeros(log_ref.shape, f32)
    pair = []
    for h in range(half // HD):
        q, k, v = (qkv_ref[:, half * j + HD * h : half * j + HD * (h + 1)] for j in range(3))
        scores = dot_nt(q, k) * HD ** (-0.5)
        top = jnp.max(scores, -1, keepdims=True)
        total = top + jnp.log(jnp.sum(jnp.exp(scores - top), -1, keepdims=True))
        pair.append(dot(jnp.exp(scores - total).astype(bf16), v, bf16))
        logs = jnp.where(lanes == h, total, logs)
        if h % 2:
            att_ref[:, HD * (h - 1) : HD * (h + 1)] = jnp.concatenate(pair, 1)
            pair = []
    log_ref[...] = logs


def project_kernel(att_ref, mine_ref, other_ref, part_ref, w_ref):
    half = att_ref.shape[1]
    first = lax.axis_index("seq") == 0
    w_ref[:, :half] = jnp.where(first, mine_ref[...], other_ref[...])
    w_ref[:, half:] = jnp.where(first, other_ref[...], mine_ref[...])
    part_ref[...] = dot(att_ref[...], w_ref[...])


def mlp_kernel(
    x_ref, part_ref, got_ref, bias_ref, mod_ref, cot_ref, w_ref, b_ref,
    residual_ref, branch_ref, normed_ref, act_ref, slope_ref, d_mlp_ref, grad_ref,
):
    branch = both(part_ref[...], got_ref[...]) + bias_ref[...]
    branch_ref[...] = branch[: branch_ref.shape[0]]
    residual = x_ref[...].astype(f32) + mod_ref[2:3] * branch
    residual_ref[...] = residual
    normed = normalize(residual)[0]
    normed_ref[...] = (normed * (1.0 + mod_ref[4:5]) + mod_ref[3:4]).astype(bf16)
    d_mlp_ref[...] = (cot_ref[...].astype(f32) * mod_ref[5:6]).astype(bf16)

    def tile(cols):
        v = dot(normed_ref[...], w_ref[:, cols]) + b_ref[:, cols]
        a, c = (2.0 / 3.141592653589793) ** 0.5, 0.044715
        square = v * v
        t = jnp.tanh(a * (v + c * (square * v)))
        act = (0.5 * v * (1.0 + t)).astype(bf16)
        act_ref[:, cols] = act
        slope_ref[:, cols] = 0.5 * (1.0 + t) + 0.5 * v * (1.0 - t * t) * (a * (1.0 + 3.0 * c * square))
        grad_ref[cols, :] = dot_t(act, d_mlp_ref[...], bf16)

    tiles(w_ref.shape[1], 256, tile)


def mlp_back_kernel(d_mlp_ref, slope_ref, w2_ref, w1_ref, d_pre_ref, sum_ref, d_normed_ref):
    d_normed_ref[...] = jnp.zeros_like(d_normed_ref)

    def tile(cols):
        d_pre = (dot_nt(d_mlp_ref[...], w2_ref[cols, :]) * slope_ref[:, cols]).astype(bf16)
        d_pre_ref[:, cols] = d_pre
        sum_ref[:, cols] = jnp.sum(d_pre.astype(f32), 0, keepdims=True)
        d_normed_ref[...] += dot_nt(d_pre, w1_ref[:, cols])

    tiles(w1_ref.shape[1], 256, tile)


def mlp_grad_kernel(act_ref, w2_ref, normed_ref, d_pre_ref, own_ref, sent_ref, grad_ref):
    own = own_ref.shape[0]

    def out_tile(cols):
        out = dot(act_ref[...], w2_ref[:, cols])
        own_ref[:, cols] = out[:own]
        sent_ref[:, cols] = out[own:]

    def grad_tile(cols):
        grad_ref[:, cols] = dot_t(normed_ref[...], d_pre_ref[:, cols], bf16)

    tiles(w2_ref.shape[1], 256, out_tile)
    tiles(d_pre_ref.shape[1], 256, grad_tile)


def branch_back_kernel(
    residual_ref, part_ref, got_ref, cot_ref, mod_ref, branch_ref, att_ref, w_ref, d_mlp_ref,
    d_residual_ref, d_att_ref, mine_ref, others_ref, sums_ref,
):
    own = d_residual_ref.shape[0]
    d_normed = both(part_ref[...], got_ref[...])
    normed, scale = normalize(residual_ref[...])
    back = normalize_back(d_normed * (1.0 + mod_ref[4:5]), normed, scale)
    d_residual = cot_ref[...].astype(f32) + back
    d_residual_ref[...] = d_residual[:own]
    d_branch = (d_residual * mod_ref[2:3]).astype(bf16)
    rows = (
        d_residual[:own] * branch_ref[...],
        d_normed[:own],
        d_normed[:own] * normed[:own],
        d_branch[:own].astype(f32),
        d_mlp_ref[:own, :].astype(f32),
    )
    for i, row in enumerate(rows):
        sums_ref[i : i + 1, :] = jnp.sum(row, 0, keepdims=True)
    d_att_ref[...] = dot_nt(d_branch, w_ref[...], bf16)
    grad = dot_t(att_ref[...], d_branch, bf16)
    half = mine_ref.shape[1]
    first = lax.axis_index("seq") == 0
    mine_ref[...] = jnp.where(first, grad[:, :half], grad[:, half:])
    others_ref[...] = jnp.where(first, grad[:, half:], grad[:, :half])


def attention_back_kernel(
    qkv_ref, att_ref, d_att_ref, log_ref, w_ref, d_qkv_ref, sum_ref, own_ref, sent_ref
):
    half = att_ref.shape[1]
    own = own_ref.shape[0]
    pairs = ([], [], [])
    for h in range(half // HD):
        q, k, v = (qkv_ref[:, half * j + HD * h : half * j + HD * (h + 1)] for j in range(3))
        att, d_att = (ref[:, HD * h : HD * (h + 1)] for ref in (att_ref, d_att_ref))
        exact = jnp.exp(dot_nt(q, k) * HD ** (-0.5) - log_ref[:, h : h + 1])
        delta = jnp.sum(d_att.astype(f32) * att.astype(f32), -1, keepdims=True)
        d_scores = (exact * (dot_nt(d_att, v) - delta) * HD ** (-0.5)).astype(bf16)
        pairs[0].append(dot(d_scores, k, bf16))
        pairs[1].append(dot_t(d_scores, q, bf16))
        pairs[2].append(dot_t(exact.astype(bf16), d_att, bf16))
        if h % 2:
            for j in range(3):
                cols = slice(half * j + HD * (h - 1), half * j + HD * (h + 1))
                value = jnp.concatenate(pairs[j], 1)
                d_qkv_ref[:, cols] = value
                sum_ref[:, cols] = jnp.sum(value.astype(f32), 0, keepdims=True)
            pairs = ([], [], [])

    def tile(cols):
        out = dot_nt(d_qkv_ref[...], w_ref[cols, :])
        own_ref[:, cols] = out[:own]
        sent_ref[:, cols] = out[own:]

    for start in range(0, own_ref.shape[1], 256):
        tile(slice(start, start + 256))


def qkv_grad_kernel(normed_ref, d_qkv_ref, grad_ref):
    tiles(d_qkv_ref.shape[1], 384, lambda cols: grad_ref.__setitem__(
        (slice(None), cols), dot_t(normed_ref[...], d_qkv_ref[:, cols], bf16)
    ))


def finish_kernel(
    part_ref, got_ref, x_ref, d_residual_ref, mod_ref, mlp_ref, mlp_got_ref, bias_ref, residual_ref,
    cot_ref, sums_ref, fc1_sum_ref, qkv_sum_ref, grad_ref, out_ref, small_ref,
):
    own, D = grad_ref.shape
    half = D // 2
    d_normed = part_ref[...] + got_ref[...]
    normed, scale = normalize(x_ref[...].astype(f32))
    back = normalize_back(d_normed * (1.0 + mod_ref[1:2]), normed, scale)
    grad_ref[...] = d_residual_ref[...] + back
    mlp = mlp_ref[...] + mlp_got_ref[...] + bias_ref[...]
    out_ref[...] = (residual_ref[:own, :] + mod_ref[5:6] * mlp).astype(bf16)
    first = lax.axis_index("seq") == 0
    small_ref[...] = jnp.zeros_like(small_ref)
    small_ref[0:1, :] = jnp.sum(d_normed, 0, keepdims=True)
    small_ref[1:2, :] = jnp.sum(d_normed * normed, 0, keepdims=True)
    small_ref[2:5, :] = sums_ref[0:3, :]
    small_ref[5:6, :] = jnp.sum(cot_ref[:own, :].astype(f32) * mlp, 0, keepdims=True)
    small_ref[6:8, :] = sums_ref[3:5, :]
    for i in range(2):
        part = qkv_sum_ref[:, 2 * half * i : 2 * half * i + half]
        small_ref[8 + i : 9 + i, :half] = jnp.where(first, part, 0.0)
        small_ref[8 + i : 9 + i, half:] = jnp.where(first, 0.0, part)
    count = fc1_sum_ref.shape[1] // D
    for i in range(count):
        part = fc1_sum_ref[:, D * i : D * (i + 1)]
        small_ref[10 + i : 11 + i, :] = jnp.where(first, part, 0.0)
        small_ref[10 + count + i : 11 + count + i, :] = jnp.where(first, 0.0, part)


def modulation_back_kernel(got_ref, w_ref, cond_ref, embedded_ref, grad_ref, d_embedded_ref, sums_ref):
    got = got_ref[...].astype(f32)
    sums_ref[...] = jnp.sum(got, 0)
    D = got.shape[2]
    total = jnp.zeros(d_embedded_ref.shape, f32)
    for k in range(6):
        cols = slice(D * k, D * (k + 1))
        d_mod = got[:, k].astype(bf16)
        total += dot_nt(w_ref[:, cols], d_mod)
        grad_ref[:, cols] = dot_t(cond_ref[...], d_mod)
    e = embedded_ref[...]
    gate = 1.0 / (1.0 + jnp.exp(-e))
    d_embedded_ref[...] = total * (gate * (1.0 + e * (1.0 - gate)))


def other_core(x):
    return lax.ppermute(x, "seq", [(0, 1), (1, 0)])


def shards(
    chips,
    latents,
    time_ids,
    class_ids,
    time_table,
    class_table,
    ada_w,
    ada_b,
    qkv_w,
    qv_b,
    proj_w,
    proj_b,
    fc1_w,
    fc1_b,
    fc2_w,
    fc2_b,
    cotangent,
):
    n = chips.count
    nd = 2 * n
    me, core = lax.axis_index("fsdp"), lax.axis_index("seq")
    first = core == 0
    own_tokens, D = latents.shape[1:]
    half = D // 2
    FF = fc1_w.shape[1]
    rows = qkv_w.shape[0]
    ff_rows = fc2_w.shape[0]
    table_rows = time_table.shape[0]

    def pick(pair):
        return jnp.where(first, pair[0], pair[1]), jnp.where(first, pair[1], pair[0])

    def in_order(mine, others, axis):
        a, b = pick((mine, others))
        return jnp.concatenate([a, b], axis)

    qkv_parts = qkv_w.reshape(rows, 3, 2, half)
    qkv_mine, qkv_others = pick((qkv_parts[:, :, 0], qkv_parts[:, :, 1]))
    proj_mine, proj_others = pick((proj_w[:, :half], proj_w[:, half:]))
    fc1_parts = fc1_w.reshape(rows, n, 2, ff_rows)
    fc1_mine, fc1_others = pick((fc1_parts[:, :, 0], fc1_parts[:, :, 1]))

    def across(mine, others):
        return in_order(mine, other_core(others), 0)

    block_q = across(
        jnp.concatenate([qkv_mine.reshape(rows, 3 * half), proj_mine], 1),
        jnp.concatenate([qkv_others.reshape(rows, 3 * half), proj_others], 1),
    )
    tokens = jnp.concatenate([latents, cotangent], 0)
    tokens = jnp.concatenate([tokens, other_core(tokens)], 1)

    width = 2 * table_rows
    cols = D // nd
    table = jnp.concatenate([time_table, class_table], 0).T.reshape(nd, cols, width)
    ids = jnp.stack([time_ids[0], class_ids[0]])
    ids = jnp.concatenate([ids // 32, ids % 32]).astype(bf16)
    lines, bounds = [], [cols]
    for vector in (fc1_b, qv_b, proj_b, fc2_b, ada_b, ids):
        count = -(-vector.shape[0] // width)
        lines.append(jnp.pad(vector, (0, count * width - vector.shape[0])).reshape(count, width))
        bounds.append(bounds[-1] + count)
    extras = jnp.concatenate(lines, 0)[None]
    sent = jnp.concatenate([table, jnp.broadcast_to(extras, (nd,) + extras.shape[1:])], 1)
    sent, block_q = after(sent, block_q)
    got = lax.all_to_all(sent, BOTH, 0, 0, tiled=True)

    held_2 = fc2_w[None]
    held_2 = jnp.concatenate([held_2, chips.swap(held_2, 0)], 0)
    held_2 = jnp.concatenate([held_2, chips.swap(held_2, 1)], 0)
    ring_q = jnp.concatenate(chips.ring_gather(block_q[None], True)[0], 0)
    swap_q = chips.swap(ring_q, 0)
    got, swap_q = after(got, swap_q)

    def extra(i, length):
        part = got[:, bounds[i] : bounds[i + 1]].reshape(nd, -1)
        return part[:, :length].astype(f32)

    fc1_bias, qv_bias, proj_bias, fc2_bias, ada_bias = (
        extra(i, b.shape[0]) for i, b in enumerate((fc1_b, qv_b, proj_b, fc2_b, ada_b))
    )
    fc1_bias = fc1_bias.reshape(n, 2, ff_rows)
    fc1_bias = pick((fc1_bias[:, 0], fc1_bias[:, 1]))[0].reshape(n * ff_rows)
    qv_bias = qv_bias.reshape(2, 2, half)
    qv_bias = pick((qv_bias[:, 0], qv_bias[:, 1]))[0]
    fc1_bias, proj_bias, fc2_bias = (x.reshape(1, -1) for x in (fc1_bias, proj_bias, fc2_bias))
    ada_bias = ada_bias.reshape(6 * D)
    id_parts = extra(5, 4)[::2].astype(jnp.int32)
    all_ids = id_parts[:, :2] * 32 + id_parts[:, 2:]

    def hot(which, base):
        rows_of = base + lax.broadcasted_iota(jnp.int32, (nd, table_rows, n), 1)
        return (all_ids[:, which][None, None] == rows_of).astype(bf16)

    base = lax.broadcasted_iota(jnp.int32, (nd, table_rows, n), 0) * table_rows
    hot_both = jnp.concatenate([hot(0, base), hot(1, base)], 1)
    embedded = jnp.einsum("sdr,srl->ld", got[:, :cols], hot_both, preferred_element_type=f32)
    condition = jax.nn.silu(embedded).astype(bf16)
    partial = dot(condition, ada_w)

    half_q = jnp.concatenate([ring_q, swap_q], 0)
    last_q = chips.swap(half_q, 1)
    block_1 = across(fc1_mine.reshape(rows, FF // 2), fc1_others.reshape(rows, FF // 2))
    block_1, swap_q = after(block_1, swap_q)
    ring_1 = jnp.concatenate(chips.ring_gather(block_1[None], True)[0], 0)
    swap_1 = chips.swap(ring_1, 0)
    half_1 = jnp.concatenate([ring_1, swap_1], 0)
    held_2, ring_1 = after(held_2, ring_1)

    lanes = 128 if (6 * D) % 128 == 0 else 6 * D
    partial = partial.reshape(n, 6 * D // lanes, lanes)
    partial = lax.all_to_all(partial, "fsdp", 0, 0, tiled=True)
    early = (fc1_bias, qv_bias, proj_bias, fc2_bias, ada_bias)
    partial, early = after(partial, early)
    fc1_bias, qv_bias, proj_bias, fc2_bias, ada_bias = early
    modulation = jnp.sum(partial, 0)
    modulation = (modulation + other_core(modulation)).reshape(6 * D) + ada_bias
    mod = modulation.reshape(6, D)

    qkv_full, proj_cols = place(chips, True, [ring_q, swap_q, last_q], [3 * half, half])
    qkv_full = qkv_full.reshape(D, 3 * half)
    proj_mine = proj_cols[: n // 2].reshape(half, half)
    proj_got = other_core(proj_cols[n // 2 :].reshape(half, half))
    (fc1_full,) = place(chips, True, [ring_1, swap_1, chips.swap(half_1, 1)], [FF // 2])
    fc1_full = fc1_full.reshape(D, FF // 2)

    all_tokens = 2 * own_tokens
    x, cot = tokens[0], tokens[1]
    wide, narrow = (all_tokens, D), (own_tokens, D)
    normed_first, qkv, attended, logs = kernel(
        attention_kernel,
        "attention",
        [(wide, bf16), ((all_tokens, 3 * half), bf16), ((all_tokens, half), bf16), ((all_tokens, 128), f32)],
        x, mod, qkv_full, qv_bias,
    )
    parts_2, attended = chips.ring_gather(held_2, False, attended)
    part, proj_full = kernel(
        project_kernel,
        "project",
        [(wide, f32), ((half, D), bf16)],
        attended, proj_mine, proj_got,
    )
    residual, branch, normed_second, activated, slope, d_mlp, fc2_grad = kernel(
        mlp_kernel,
        "mlp",
        [(wide, f32), (narrow, f32), (wide, bf16), ((all_tokens, FF // 2), bf16)]
        + [((all_tokens, FF // 2), f32), (wide, bf16), ((FF // 2, D), bf16)],
        x, part, other_core(part), proj_bias, mod, cot, fc1_full, fc1_bias,
    )
    kept_2, sent_2 = relative(chips, True, 2, [fc2_grad.reshape(n, ff_rows, D)])
    parts_2, (kept_2, sent_2) = after(parts_2, (kept_2, sent_2))
    (fc2_full,) = place(chips, False, parts_2, [D])
    fc2_full = fc2_full.reshape(FF // 2, D)
    total_2 = chips.swap_add(kept_2, sent_2, 1)

    d_pre, fc1_b_grad, part = kernel(
        mlp_back_kernel,
        "mlp_back",
        [((all_tokens, FF // 2), bf16), ((1, FF // 2), f32), (wide, f32)],
        d_mlp, slope, fc2_full, fc1_full,
    )
    got = other_core(part)
    mlp_own, mlp_sent, fc1_grad = kernel(
        mlp_grad_kernel,
        "mlp_grad",
        [(narrow, f32), (narrow, f32), ((D, FF // 2), bf16)],
        activated, fc2_full, normed_second, d_pre,
    )
    kept_1, sent_1 = relative(chips, True, 2, [fc1_grad.reshape(n, 2 * rows, FF // 2)])
    got, (kept_1, sent_1) = after(got, (kept_1, sent_1))
    total_1 = chips.swap_add(kept_1, sent_1, 1)
    d_residual, d_attended, proj_grad, proj_sent, sums_second = kernel(
        branch_back_kernel,
        "branch_back",
        [(narrow, f32), ((all_tokens, half), bf16), ((half, half), bf16), ((half, half), bf16), ((8, D), f32)],
        residual, part, got, cot, mod, branch, attended, proj_full, d_mlp,
    )
    proj_got = other_core(proj_sent)
    d_attended, total_2 = after(d_attended, total_2)
    total_2 = chips.swap_add(total_2[0], total_2[1].astype(bf16), 0)
    d_qkv, d_qkv_sum, part, sent = kernel(
        attention_back_kernel,
        "attention_back",
        [((all_tokens, 3 * half), bf16), ((1, 3 * half), f32), (narrow, f32), (narrow, f32)],
        qkv, attended, d_attended, logs, qkv_full,
    )
    got = other_core(sent)
    (qkv_grad,) = kernel(
        qkv_grad_kernel, "qkv_grad", [((D, 3 * half), bf16)], normed_first, d_qkv
    )
    blocks = (n // 2, 2 * rows, half)
    kept_q, sent_q = relative(
        chips,
        True,
        2,
        [qkv_grad.reshape(n, 2 * rows, 3 * half), proj_grad.reshape(blocks), proj_got.reshape(blocks)],
    )
    got, (kept_q, sent_q, total_2) = after(got, (kept_q, sent_q, total_2))
    total_2 = [x for half in total_2 for x in half]
    terms_2 = chips.direct_scatter(total_2)
    total_1 = chips.swap_add(total_1[0], total_1[1].astype(bf16), 0)
    mlp_got = other_core(mlp_sent)
    latents_grad, output, small = kernel(
        finish_kernel,
        "finish",
        [(narrow, f32), (narrow, bf16), ((16, D), f32)],
        part, got, latents[0], d_residual, mod, mlp_own, mlp_got, fc2_bias, residual, cot,
        sums_second, fc1_b_grad, d_qkv_sum,
    )
    total_q = chips.swap_add(kept_q, sent_q, 1)

    small = small + other_core(small)
    small, (total_q, total_1, terms_2) = after(small, (total_q, total_1, terms_2))
    total_1 = [x for half in total_1 for x in half]
    terms_1 = chips.direct_scatter(total_1)
    small = jnp.broadcast_to(small.astype(bf16)[None], (n, 16, D))
    got = lax.all_to_all(small, "fsdp", 0, 0, tiled=True)
    total_q = chips.swap_add(total_q[0], total_q[1].astype(bf16), 0)
    got, (total_q, terms_1) = after(got, (total_q, terms_1))
    total_q = [x for half in total_q for x in half]
    terms_q = chips.direct_scatter(total_q)
    ada_w_grad, d_embedded, sums = kernel(
        modulation_back_kernel,
        "modulation_back",
        [((cols, 6 * D), f32), ((cols, n), f32), ((16, D), f32)],
        got, ada_w, condition, embedded.T,
    )
    d_embedded = lax.all_to_all(
        jnp.broadcast_to(d_embedded[None], (nd, cols, n)), BOTH, 0, 0, tiled=True
    ).reshape(D, n)
    d_embedded, terms_q = after(d_embedded, terms_q)
    qkv_grad, fc1_grad, fc2_grad = (
        sum(x.astype(f32) for x in [total[0]] + terms)
        for total, terms in ((total_q, terms_q), (total_1, terms_1), (total_2, terms_2))
    )

    device = 2 * me + core
    own = device * table_rows + lax.broadcasted_iota(jnp.int32, (table_rows, n), 0)
    mask = jnp.concatenate([all_ids[:, i][None] == own for i in range(2)], 0).astype(f32)
    tables_grad = lax.dot_general(mask, d_embedded, (((1,), (1,)), ((), ())), precision=highest)

    def owned(rows_of, place, count):
        return lax.dynamic_slice(rows_of.reshape(-1), (place * count,), (count,))

    count = FF // 2 // D
    fc1_rows = lax.dynamic_slice(sums, (10 + core * count, 0), (count, D))

    def to_rows(grad):
        pair = grad.reshape(2, rows, grad.shape[1])
        mine, others = pick((pair[0], pair[1]))
        return pick((mine, other_core(others)))

    fc1_w_grad = jnp.stack(
        [x.reshape(rows, n, ff_rows) for x in to_rows(fc1_grad)], 2
    ).reshape(rows, FF)
    qp = to_rows(qkv_grad)
    proj_w_grad = jnp.concatenate([x[:, 3 * half :] for x in qp], 1)
    qkv_w_grad = jnp.stack([x[:, : 3 * half].reshape(rows, 3, half) for x in qp], 2).reshape(
        rows, 3 * D
    )
    return (
        output[None],
        latents_grad[None],
        tables_grad[:table_rows],
        tables_grad[table_rows:],
        ada_w_grad,
        owned(sums[:6], device, 6 * D // nd),
        qkv_w_grad,
        owned(sums[8:10], device, 2 * D // nd),
        proj_w_grad,
        owned(sums[6], device, rows),
        fc1_w_grad,
        owned(fc1_rows, me, ff_rows),
        fc2_grad,
        owned(sums[7], device, rows),
    )


def solution(mesh):
    assert mesh.shape["seq"] == 2
    chips = Chips(mesh.shape["fsdp"])
    tokens = P("fsdp", "seq", None)
    matrix = P(BOTH, None)
    vector = P(BOTH)
    in_specs = (
        tokens,
        P("fsdp"),
        P("fsdp"),
        matrix,
        matrix,
        matrix,
        vector,
        matrix,
        vector,
        matrix,
        vector,
        matrix,
        vector,
        matrix,
        vector,
        tokens,
    )
    out_specs = (
        tokens,
        tokens,
        matrix,
        matrix,
        matrix,
        vector,
        matrix,
        vector,
        matrix,
        vector,
        matrix,
        vector,
        matrix,
        vector,
    )
    return jax.shard_map(
        functools.partial(shards, chips),
        mesh=mesh,
        in_specs=in_specs,
        out_specs=out_specs,
        check_vma=False,
    )
```

time: 282 us -> 216 us (0.77)
  waiting for transfers between devices: 110 us -> 61.6 us
  Pallas kernels: 5.19 us -> 31.2 us
  other arithmetic: 40.1 us -> 15.6 us
  matrix products: 25.7 us -> 1.39 us
  starting transfers between devices: 51.3 us -> 70 us
  local copies, waits for them, and re-layouts: 44.1 us -> 32.1 us
    ppermute x24 -> x30, waiting for transfers between devices: 95.4 us -> 45.1 us  [the longest x12 24.1 us: swap(): return lax.ppermute(x, BOTH, pairs)]
    pallas_call x6 -> x16, Pallas kernels: 5.19 us -> 31.2 us  [kernel(): pl.pallas_call(body, out_shape=shapes, in_specs=[pl.BlockSpec(memory_spac...]
    ppermute x24 -> x30, starting transfers between devices: 26.8 us -> 51 us  [the longest x18 34.4 us: shift(): return lax.ppermute(x, 'fsdp', pairs)]
    dot_general x18 -> x1, matrix products: 20.4 us -> 0.36 us  [shards(): lax.dot_general(mask, d_embedded, (((1,), (1,)), ((), ())), precision=hig...]
    slice x34 -> x13, local copies, waits for them, and re-layouts: 15.5 us -> 1.72 us  [the longest x1 0.87 us: shards(): proj_got = other_core(proj_cols[n // 2:].reshape(half, half))]
    reduce_sum x20 -> x0, other arithmetic: 9.52 us -> none  [the longest x6 3.64 us: layer_norm(): center = stream - jnp.mean(stream, -1, keepdims=True)]
    concatenate x13 -> x6, other arithmetic: 9.57 us -> 0.95 us  [the longest x1 0.64 us: shards(): proj_w_grad = jnp.concatenate([x[:, 3 * half:] for x in qp], 1)]
    all_to_all x1, waiting for transfers between devices: 6.5 us -> 0.01 us  [shards(): lax.all_to_all(jnp.broadcast_to(d_embedded[None], (nd, cols, n)), BOTH, 0...]
  transfers between devices with their start and end apart: 41 -> 47, of which waited for: 16 -> 18; matrix products, arithmetic and copies ran while one was open for 29% -> 18% of each run, Pallas kernels for 2% -> 15%
where the time goes in v2:
time: 216 us; the launch traced here: 215 us
  starting transfers between devices  70 us (32%)
  waiting for transfers between devices  61.6 us (29%)
  local copies, waits for them, and re-layouts  32.1 us (15%)
  Pallas kernels  31.2 us (14%)
  other arithmetic  15.6 us (7%)
  between operations  3.39 us (2%)
    ppermute x18, starting transfers between devices, shift(): return lax.ppermute(x, 'fsdp', pairs)  34.4 us
    pallas_call x16, Pallas kernels, kernel(): pl.pallas_call(body, out_shape=shapes, in_specs=[pl.BlockSpec(memory_spac...  31.2 us
    ppermute x12, waiting for transfers between devices, swap(): return lax.ppermute(x, BOTH, pairs)  24.1 us
    ppermute x18, waiting for transfers between devices, shift(): return lax.ppermute(x, 'fsdp', pairs)  21 us
    ppermute x12, starting transfers between devices, swap(): return lax.ppermute(x, BOTH, pairs)  16.6 us
    unnamed x149, local copies, waits for them, and re-layouts  14.2 us
    all_to_all x1, waiting for transfers between devices, shards(): partial = lax.all_to_all(partial, 'fsdp', 0, 0, tiled=True)  12.2 us
    add x10, other arithmetic, swap_add(): kept[i * half:(i + 1) * half].astype(f32)  7.53 us
  transfers between devices with their start and end apart: 47, of which 18 were waited for; matrix products, arithmetic and copies ran while one was open for 18% of the time, Pallas kernels for 15%

profile of v2, /device:TPU:0, one launch (start us, length us, event | category | flops | bytes accessed | tf_op | source)
XLA Modules:
  0.0 215.4 jit_solution(6841815035646423599)
XLA Ops:
  3.4 2.9 %collective-permute-start.9 = (bf16[1,96,768]{2,1,0:T(8,128)(2,1)S(1)}, bf16[1,96,768]{2,1,0:T(8,128)(2,1)S(1)}, u32[]{:S(2)}, u32[]{:S(2)}) collective-permute-start(bf16[1,96,768]{2,1,0:T(8,128)(2,1)S(1)} %bitcast.143), channel_id=1, source_target_pairs={{0,2},{1,5},{2,0},{3,7},{4,6},{5,1},{6,4},{7,3},{8,10},{9,13},{10,... | collective-permute-start | bytes 442376 | tf_op jit(solution)/shard_map/first_swap/ppermute | solution.py:53
  11.7 2.6 %collective-permute-start.3 = (bf16[1,48,1536]{2,1,0:T(8,128)(2,1)S(1)}, bf16[1,48,1536]{2,1,0:T(8,128)(2,1)S(1)}, u32[]{:S(2)}, u32[]{:S(2)}) collective-permute-start(bf16[1,48,1536]{2,1,0:T(8,128)(2,1)S(1)} %bitcast.138), channel_id=1, source_target_pairs={{0,16},{2,18},{4,20},{6,22},{8,24},{10,26},{12,28},{14,30},{16,0},... | collective-permute-start | bytes 442376 | tf_op jit(solution)/shard_map/ring_by_2/ppermute | solution.py:44
  21.6 3.1 %collective-permute-done.3 = bf16[1,48,1536]{2,1,0:T(8,128)(2,1)S(1)} collective-permute-done((bf16[1,48,1536]{2,1,0:T(8,128)(2,1)S(1)}, bf16[1,48,1536]{2,1,0:T(8,128)(2,1)S(1)}, u32[]{:S(2)}, u32[]{:S(2)}) %collective-permute-start.3) | collective-permute-done | bytes 147488 | tf_op jit(solution)/shard_map/ring_by_2/ppermute | solution.py:44
  27.6 3.8 %all-to-all-done = bf16[32,2,1056]{2,1,0:T(2,128)(2,1)S(1)} async-done(((bf16[32,2,1056]{2,1,0:T(2,128)(2,1)}), bf16[32,2,1056]{2,1,0:T(2,128)(2,1)S(1)}, u32[]{:S(2)}, u32[]{:S(2)}) %all-to-all-start) | async-done | bytes 135200 | tf_op jit(solution)/shard_map/all_to_all | solution.py:473
  31.7 3.4 %collective-permute-done.5.refs_1_ = bf16[4,48,1536]{2,1,0:T(8,128)(2,1)S(1)} collective-permute-done((bf16[4,48,1536]{2,1,0:T(8,128)(2,1)S(1)}, bf16[4,48,1536]{2,1,0:T(8,128)(2,1)S(1)}, u32[]{:S(2)}, u32[]{:S(2)}) %collective-permute-start.5) | collective-permute-done | bytes 589856 | tf_op jit(solution)/shard_map/first_swap/ppermute | solution.py:53
  35.8 4.9 %collective-permute-start.11 = (bf16[1,48,1536]{2,1,0:T(8,128)(2,1)S(1)}, bf16[1,48,1536]{2,1,0:T(8,128)(2,1)S(1)}, u32[]{:S(2)}, u32[]{:S(2)}) collective-permute-start(bf16[1,48,1536]{2,1,0:T(8,128)(2,1)S(1)} %bitcast.133), channel_id=1, source_target_pairs={{0,8},{2,10},{4,12},{6,14},{8,16},{10,18},{12,20},{14,22},{16,24},... | collective-permute-start | bytes 442376 | tf_op jit(solution)/shard_map/ring_by_1/ppermute | solution.py:44
  48.0 3.6 %all-to-all-start.1 = ((f32[16,36,128]{2,1,0:T(8,128)}), f32[16,36,128]{2,1,0:T(8,128)S(1)}, u32[]{:S(2)}, u32[]{:S(2)}) async-start(f32[16,36,128]{2,1,0:T(8,128)} %reshape.238), calls=%async_computation.1 | async-start | bytes 655360 | tf_op jit(solution)/shard_map/all_to_all | solution.py:519
  61.3 12.2 %all-to-all-done.1 = f32[16,36,128]{2,1,0:T(8,128)S(1)} async-done(((f32[16,36,128]{2,1,0:T(8,128)}), f32[16,36,128]{2,1,0:T(8,128)S(1)}, u32[]{:S(2)}, u32[]{:S(2)}) %all-to-all-start.1) | async-done | bytes 294944 | tf_op jit(solution)/shard_map/all_to_all | solution.py:519
  92.7 5.4 %mlp.1 = (f32[256,768]{1,0:T(8,128)S(1)}, f32[128,768]{1,0:T(8,128)S(1)}, bf16[256,768]{1,0:T(8,128)(2,1)S(1)}, bf16[256,1536]{1,0:T(8,128)(2,1)S(1)}, f32[256,1...) custom-call(bf16[256,768]{1,0:T(8,128)(2,1)S(1)} %get-tuple-element.209.x_ref, ...), custom_call_target="tpu_custom_call" | custom-call | bytes 11430912 | tf_op jit(solution)/shard_map/mlp/pallas_call | solution.py:142
  98.4 6.9 %collective-permute-done.20.refs_2_ = bf16[4,96,768]{2,1,0:T(8,128)(2,1)S(1)} collective-permute-done((bf16[4,96,768]{2,1,0:T(8,128)(2,1)}, bf16[4,96,768]{2,1,0:T(8,128)(2,1)S(1)}, u32[]{:S(2)}, u32[]{:S(2)}) %collective-permute-start.20) | collective-permute-done | bytes 589856 | tf_op jit(solution)/shard_map/ring_by_1/ppermute | solution.py:44
  107.4 3.9 %mlp_back.1 = (bf16[256,1536]{1,0:T(8,128)(2,1)S(1)}, f32[1,1536]{1,0:T(1,128)S(1)}, f32[256,768]{1,0:T(8,128)S(1)}) custom-call(bf16[256,768]{1,0:T(8,128)(2,1)S(1)} %get-tuple-element.128.d_mlp_ref, f32[256,1536]{1,0:T(8,128)S(1)} %get-tuple-element.129.slope_ref, bf16[1536,768]{1,0:T(8,128)(2,1)S(1)} %bitcast.122, bf16[768,1536]{1,0:T(8,128)(2,1)S(1)} %bitcast.121), custom_call_target="tpu_custom_call" | custom-call | bytes 8263680 | tf_op jit(solution)/shard_map/mlp_back/pallas_call | solution.py:142
  111.4 3.0 %mlp_grad.1 = (f32[128,768]{1,0:T(8,128)S(1)}, f32[128,768]{1,0:T(8,128)S(1)}, bf16[768,1536]{1,0:T(8,128)(2,1)S(1)}) custom-call(bf16[256,1536]{1,0:T(8,128)(2,1)S(1)} %get-tuple-element.140.act_ref, bf16[1536,768]{1,0:T(8,128)(2,1)S(1)} %bitcast.123, bf16[256,768]{1,0:T(8,128)(2,1)S(1)} %get-tuple-element.141.normed_ref, ...), custom_call_target="tpu_custom_call" | custom-call | bytes 7471104 | tf_op jit(solution)/shard_map/mlp_grad/pallas_call | solution.py:142
  118.3 3.2 %collective-permute-done.22 = bf16[8,96,768]{2,1,0:T(8,128)(2,1)S(1)} collective-permute-done((bf16[8,96,768]{2,1,0:T(8,128)(2,1)S(1)}, bf16[8,96,768]{2,1,0:T(8,128)(2,1)S(1)}, u32[]{:S(2)}, u32[]{:S(2)}) %collective-permute-start.22) | collective-permute-done | bytes 1179680 | tf_op jit(solution)/shard_map/last_swap/ppermute | solution.py:53
  128.5 3.4 %attention_back.1 = (bf16[256,1152]{1,0:T(8,128)(2,1)S(1)}, f32[1,1152]{1,0:T(1,128)S(1)}, f32[128,768]{1,0:T(8,128)S(1)}, f32[128,768]{1,0:T(8,128)S(1)}) custom-call(bf16[256,1152]{1,0:T(8,128)(2,1)S(1)} %copy-done.19, bf16[256,384]{1,0:T(8,128)(2,1)S(1)} %get-tuple-element.121.att_ref, bf16[256,384]{1,0:T(8,128)(2,1)S(1)} %copy-done.29, ...), custom_call_target="tpu_custom_call" | custom-call | bytes 4264448 | tf_op jit(solution)/shard_map/attention_back/pallas_call | solution.py:142
  134.5 4.5 %collective-permute-done.25 = bf16[4,96,768]{2,1,0:T(8,128)(2,1)} collective-permute-done((bf16[4,96,768]{2,1,0:T(8,128)(2,1)}, bf16[4,96,768]{2,1,0:T(8,128)(2,1)}, u32[]{:S(2)}, u32[]{:S(2)}) %collective-permute-start.25) | collective-permute-done | bytes 589856 | tf_op jit(solution)/shard_map/first_swap/ppermute | solution.py:53
  147.9 3.3 %collective-permute-start.31 = (bf16[96,768]{1,0:T(8,128)(2,1)S(1)}, bf16[96,768]{1,0:T(8,128)(2,1)S(1)}, u32[]{:S(2)}, u32[]{:S(2)}) collective-permute-start(bf16[96,768]{1,0:T(8,128)(2,1)S(1)} %fusion.15), channel_id=1, source_target_pairs={{0,24},{2,26},{4,28},{6,30},{8,0},{10,2},{12,4},{14,6},{16,8},{18,... | collective-permute-start | bytes 442376 | tf_op jit(solution)/shard_map/ring_by_3/ppermute | solution.py:44
  151.3 7.1 %collective-permute-done.30 = bf16[4,48,1536]{2,1,0:T(8,128)(2,1)S(1)} collective-permute-done((bf16[4,48,1536]{2,1,0:T(8,128)(2,1)S(1)}, bf16[4,48,1536]{2,1,0:T(8,128)(2,1)S(1)}, u32[]{:S(2)}, u32[]{:S(2)}) %collective-permute-start.30) | collective-permute-done | bytes 589856 | tf_op jit(solution)/shard_map/first_swap/ppermute | solution.py:53
  158.5 4.0 %collective-permute-done.28 = bf16[8,48,1536]{2,1,0:T(8,128)(2,1)S(1)} collective-permute-done((bf16[8,48,1536]{2,1,0:T(8,128)(2,1)S(1)}, bf16[8,48,1536]{2,1,0:T(8,128)(2,1)S(1)}, u32[]{:S(2)}, u32[]{:S(2)}) %collective-permute-start.28) | collective-permute-done | bytes 1179680 | tf_op jit(solution)/shard_map/last_swap/ppermute | solution.py:53
  166.9 6.4 %all-to-all-start.2 = ((bf16[16,16,768]{2,1,0:T(8,128)(2,1)}), bf16[16,16,768]{2,1,0:T(8,128)(2,1)S(1)}, u32[]{:S(2)}, u32[]{:S(2)}) async-start(bf16[16,16,768]{2,1,0:T(8,128)(2,1)} %broadcast_in_dim.39), calls=%async_computation.2 | async-start | bytes 786432 | tf_op jit(solution)/shard_map/all_to_all | solution.py:624
  173.3 3.8 %collective-permute-start.35 = (bf16[48,1536]{1,0:T(8,128)(2,1)S(1)}, bf16[48,1536]{1,0:T(8,128)(2,1)}, u32[]{:S(2)}, u32[]{:S(2)}) collective-permute-start(bf16[48,1536]{1,0:T(8,128)(2,1)S(1)} %fusion.16), channel_id=1, source_target_pairs={{0,24},{2,26},{4,28},{6,30},{8,0},{10,2},{12,4},{14,6},{16,8},{18,... | collective-permute-start | bytes 442376 | tf_op jit(solution)/shard_map/ring_by_3/ppermute | solution.py:44
  180.0 2.9 %collective-permute-done.36 = bf16[48,1536]{1,0:T(8,128)(2,1)} collective-permute-done((bf16[48,1536]{1,0:T(8,128)(2,1)}, bf16[48,1536]{1,0:T(8,128)(2,1)}, u32[]{:S(2)}, u32[]{:S(2)}) %collective-permute-start.36) | collective-permute-done | bytes 147488 | tf_op jit(solution)/shard_map/ring_by_2/ppermute | solution.py:44
  182.9 6.0 %collective-permute-done.35 = bf16[48,1536]{1,0:T(8,128)(2,1)} collective-permute-done((bf16[48,1536]{1,0:T(8,128)(2,1)S(1)}, bf16[48,1536]{1,0:T(8,128)(2,1)}, u32[]{:S(2)}, u32[]{:S(2)}) %collective-permute-start.35) | collective-permute-done | bytes 147488 | tf_op jit(solution)/shard_map/ring_by_3/ppermute | solution.py:44
  192.2 4.4 %all-to-all-start.3 = ((f32[32,1,384]{2,1,0:T(1,128)}), f32[32,1,384]{2,1,0:T(1,128)S(1)}, u32[]{:S(2)}, u32[]{:S(2)}) async-start(f32[32,1,384]{2,1,0:T(1,128)} %reshape.299), calls=%async_computation.3 | async-start | bytes 98304 | tf_op jit(solution)/shard_map/all_to_all | solution.py:635
  196.6 2.7 %collective-permute-start.39 = (bf16[48,1536]{1,0:T(8,128)(2,1)S(1)}, bf16[48,1536]{1,0:T(8,128)(2,1)S(1)}, u32[]{:S(2)}, u32[]{:S(2)}) collective-permute-start(bf16[48,1536]{1,0:T(8,128)(2,1)S(1)} %get-tuple-element.223), channel_id=1, source_target_pairs={{0,16},{2,18},{4,20},{6,22},{8,24},{10,26},{12,28},{14,30},{16,0},... | collective-permute-start | bytes 442376 | tf_op jit(solution)/shard_map/ring_by_2/ppermute | solution.py:44
  (363 shorter events, 104.7 us)
Async XLA Ops:
  3.4 16.4 %collective-permute-start.9 = (bf16[1,96,768]{2,1,0:T(8,128)(2,1)S(1)}, bf16[1,96,768]{2,1,0:T(8,128)(2,1)S(1)}, u32[]{:S(2)}, u32[]{:S(2)}) collective-permute-start(bf16[1,96,768]{2,1,0:T(8,128)(2,1)S(1)} %bitcast.143), channel_id=1, source_target_pairs={{0,2},{1,5},{2,0},{3,7},{4,6},{5,1},{6,4},{7,3},{8,10},{9,13},{10,... | collective-permute-start | bytes 442376 | tf_op jit(solution)/shard_map/first_swap/ppermute | solution.py:53
  7.7 72.4 %collective-permute-start = (bf16[2,128,768]{2,1,0:T(8,128)(2,1)}, bf16[2,128,768]{2,1,0:T(8,128)(2,1)}, u32[]{:S(2)}, u32[]{:S(2)}) collective-permute-start(bf16[2,128,768]{2,1,0:T(8,128)(2,1)} %constant_dynamic-update-slice_fusion), channel_id=1, source_target_pairs={{0,1},{1,0},{2,3},{3,2},{4,5},{5,4},{6,7},{7,6},{8,9},{9,8},{10,11... | collective-permute-start | bytes 1179656 | tf_op jit(solution)/shard_map/ppermute | solution.py:404
  35.8 17.6 %collective-permute-start.11 = (bf16[1,48,1536]{2,1,0:T(8,128)(2,1)S(1)}, bf16[1,48,1536]{2,1,0:T(8,128)(2,1)S(1)}, u32[]{:S(2)}, u32[]{:S(2)}) collective-permute-start(bf16[1,48,1536]{2,1,0:T(8,128)(2,1)S(1)} %bitcast.133), channel_id=1, source_target_pairs={{0,8},{2,10},{4,12},{6,14},{8,16},{10,18},{12,20},{14,22},{16,24},... | collective-permute-start | bytes 442376 | tf_op jit(solution)/shard_map/ring_by_1/ppermute | solution.py:44
  44.0 30.6 %collective-permute-start.8 = (bf16[8,48,1536]{2,1,0:T(8,128)(2,1)}, bf16[8,48,1536]{2,1,0:T(8,128)(2,1)}, u32[]{:S(2)}, u32[]{:S(2)}) collective-permute-start(bf16[8,48,1536]{2,1,0:T(8,128)(2,1)} %constant_dynamic-update-slice_fusion.2), channel_id=1, source_target_pairs={{0,4},{1,3},{2,6},{3,1},{4,0},{5,7},{6,2},{7,5},{8,12},{9,11},{10,... | collective-permute-start | bytes 3538952 | tf_op jit(solution)/shard_map/last_swap/ppermute | solution.py:53
  48.0 25.5 %all-to-all-start.1 = ((f32[16,36,128]{2,1,0:T(8,128)}), f32[16,36,128]{2,1,0:T(8,128)S(1)}, u32[]{:S(2)}, u32[]{:S(2)}) async-start(f32[16,36,128]{2,1,0:T(8,128)} %reshape.238), calls=%async_computation.1 | async-start | bytes 655360 | tf_op jit(solution)/shard_map/all_to_all | solution.py:519
  53.5 20.0 %collective-permute-start.18 = (bf16[4,48,1536]{2,1,0:T(8,128)(2,1)S(1)}, bf16[4,48,1536]{2,1,0:T(8,128)(2,1)S(1)}, u32[]{:S(2)}, u32[]{:S(2)}) collective-permute-start(bf16[4,48,1536]{2,1,0:T(8,128)(2,1)S(1)} %pad_maximum_fusion.2.refs_0_), channel_id=1, source_target_pairs={{0,2},{1,5},{2,0},{3,7},{4,6},{5,1},{6,4},{7,3},{8,10},{9,13},{10,... | collective-permute-start | bytes 1769480 | tf_op jit(solution)/shard_map/first_swap/ppermute | solution.py:53
  55.5 29.1 %collective-permute-start.14 = (bf16[4,96,768]{2,1,0:T(8,128)(2,1)S(1)}, bf16[4,96,768]{2,1,0:T(8,128)(2,1)}, u32[]{:S(2)}, u32[]{:S(2)}) collective-permute-start(bf16[4,96,768]{2,1,0:T(8,128)(2,1)S(1)} %pad_maximum_fusion.1.refs_0_), channel_id=1, source_target_pairs={{0,8},{2,10},{4,12},{6,14},{8,16},{10,18},{12,20},{14,22},{16,24},... | collective-permute-start | bytes 1769480 | tf_op jit(solution)/shard_map/ring_by_1/ppermute | solution.py:44
  57.0 27.7 %collective-permute-start.15 = (bf16[4,96,768]{2,1,0:T(8,128)(2,1)S(1)}, bf16[4,96,768]{2,1,0:T(8,128)(2,1)}, u32[]{:S(2)}, u32[]{:S(2)}) collective-permute-start(bf16[4,96,768]{2,1,0:T(8,128)(2,1)S(1)} %pad_maximum_fusion.1.refs_0_), channel_id=1, source_target_pairs={{0,24},{2,26},{4,28},{6,30},{8,0},{10,2},{12,4},{14,6},{16,8},{18,... | collective-permute-start | bytes 1769480 | tf_op jit(solution)/shard_map/ring_by_3/ppermute | solution.py:44
  74.6 16.6 %collective-permute-start.19 = (bf16[8,48,1536]{2,1,0:T(8,128)(2,1)}, bf16[8,48,1536]{2,1,0:T(8,128)(2,1)}, u32[]{:S(2)}, u32[]{:S(2)}) collective-permute-start(bf16[8,48,1536]{2,1,0:T(8,128)(2,1)} %constant_dynamic-update-slice_fusion.7), channel_id=1, source_target_pairs={{0,4},{1,3},{2,6},{3,1},{4,0},{5,7},{6,2},{7,5},{8,12},{9,11},{10,... | collective-permute-start | bytes 3538952 | tf_op jit(solution)/shard_map/last_swap/ppermute | solution.py:53
  87.8 17.5 %collective-permute-start.20 = (bf16[4,96,768]{2,1,0:T(8,128)(2,1)}, bf16[4,96,768]{2,1,0:T(8,128)(2,1)S(1)}, u32[]{:S(2)}, u32[]{:S(2)}) collective-permute-start(bf16[4,96,768]{2,1,0:T(8,128)(2,1)} %collective-permute-done.14.refs_1_), channel_id=1, source_target_pairs={{0,8},{2,10},{4,12},{6,14},{8,16},{10,18},{12,20},{14,22},{16,24},... | collective-permute-start | bytes 1769480 | tf_op jit(solution)/shard_map/ring_by_1/ppermute | solution.py:44
  105.3 16.2 %collective-permute-start.22 = (bf16[8,96,768]{2,1,0:T(8,128)(2,1)S(1)}, bf16[8,96,768]{2,1,0:T(8,128)(2,1)S(1)}, u32[]{:S(2)}, u32[]{:S(2)}) collective-permute-start(bf16[8,96,768]{2,1,0:T(8,128)(2,1)S(1)} %get-tuple-element.151), channel_id=1, source_target_pairs={{0,4},{1,3},{2,6},{3,1},{4,0},{5,7},{6,2},{7,5},{8,12},{9,11},{10,... | collective-permute-start | bytes 3538952 | tf_op jit(solution)/shard_map/last_swap/ppermute | solution.py:53
  115.7 24.9 %collective-permute-start.29 = (bf16[8,48,1536]{2,1,0:T(8,128)(2,1)}, bf16[8,48,1536]{2,1,0:T(8,128)(2,1)}, u32[]{:S(2)}, u32[]{:S(2)}) collective-permute-start(bf16[8,48,1536]{2,1,0:T(8,128)(2,1)} %get-tuple-element.178), channel_id=1, source_target_pairs={{0,4},{1,3},{2,6},{3,1},{4,0},{5,7},{6,2},{7,5},{8,12},{9,11},{10,... | collective-permute-start | bytes 3538952 | tf_op jit(solution)/shard_map/last_swap/ppermute | solution.py:53
  123.7 15.3 %collective-permute-start.25 = (bf16[4,96,768]{2,1,0:T(8,128)(2,1)}, bf16[4,96,768]{2,1,0:T(8,128)(2,1)}, u32[]{:S(2)}, u32[]{:S(2)}) collective-permute-start(bf16[4,96,768]{2,1,0:T(8,128)(2,1)} %convert_add_fusion.3), channel_id=1, source_target_pairs={{0,2},{1,5},{2,0},{3,7},{4,6},{5,1},{6,4},{7,3},{8,10},{9,13},{10,... | collective-permute-start | bytes 1769480 | tf_op jit(solution)/shard_map/first_swap/ppermute | solution.py:53
  125.1 20.3 %collective-permute-start.26 = (f32[128,768]{1,0:T(8,128)}, f32[128,768]{1,0:T(8,128)S(1)}, u32[]{:S(2)}, u32[]{:S(2)}) collective-permute-start(f32[128,768]{1,0:T(8,128)} %copy-done.38), channel_id=1, source_target_pairs={{0,1},{1,0},{2,3},{3,2},{4,5},{5,4},{6,7},{7,6},{8,9},{9,8},{10,11... | collective-permute-start | bytes 1179656 | tf_op jit(solution)/shard_map/ppermute | solution.py:404
  142.1 16.2 %collective-permute-start.30 = (bf16[4,48,1536]{2,1,0:T(8,128)(2,1)S(1)}, bf16[4,48,1536]{2,1,0:T(8,128)(2,1)S(1)}, u32[]{:S(2)}, u32[]{:S(2)}) collective-permute-start(bf16[4,48,1536]{2,1,0:T(8,128)(2,1)S(1)} %get-tuple-element.206), channel_id=1, source_target_pairs={{0,2},{1,5},{2,0},{3,7},{4,6},{5,1},{6,4},{7,3},{8,10},{9,13},{10,... | collective-permute-start | bytes 1769480 | tf_op jit(solution)/shard_map/first_swap/ppermute | solution.py:53
  143.8 18.7 %collective-permute-start.28 = (bf16[8,48,1536]{2,1,0:T(8,128)(2,1)S(1)}, bf16[8,48,1536]{2,1,0:T(8,128)(2,1)S(1)}, u32[]{:S(2)}, u32[]{:S(2)}) collective-permute-start(bf16[8,48,1536]{2,1,0:T(8,128)(2,1)S(1)} %get-tuple-element.176), channel_id=1, source_target_pairs={{0,4},{1,3},{2,6},{3,1},{4,0},{5,7},{6,2},{7,5},{8,12},{9,11},{10,... | collective-permute-start | bytes 3538952 | tf_op jit(solution)/shard_map/last_swap/ppermute | solution.py:53
  146.7 16.9 %collective-permute-start.32 = (bf16[96,768]{1,0:T(8,128)(2,1)S(1)}, bf16[96,768]{1,0:T(8,128)(2,1)S(1)}, u32[]{:S(2)}, u32[]{:S(2)}) collective-permute-start(bf16[96,768]{1,0:T(8,128)(2,1)S(1)} %get-tuple-element.227), channel_id=1, source_target_pairs={{0,16},{2,18},{4,20},{6,22},{8,24},{10,26},{12,28},{14,30},{16,0},... | collective-permute-start | bytes 442376 | tf_op jit(solution)/shard_map/ring_by_2/ppermute | solution.py:44
  147.3 16.3 %collective-permute-start.33 = (bf16[96,768]{1,0:T(8,128)(2,1)S(1)}, bf16[96,768]{1,0:T(8,128)(2,1)S(1)}, u32[]{:S(2)}, u32[]{:S(2)}) collective-permute-start(bf16[96,768]{1,0:T(8,128)(2,1)S(1)} %get-tuple-element.226), channel_id=1, source_target_pairs={{0,8},{2,10},{4,12},{6,14},{8,16},{10,18},{12,20},{14,22},{16,24},... | collective-permute-start | bytes 442376 | tf_op jit(solution)/shard_map/ring_by_1/ppermute | solution.py:44
  147.9 15.7 %collective-permute-start.31 = (bf16[96,768]{1,0:T(8,128)(2,1)S(1)}, bf16[96,768]{1,0:T(8,128)(2,1)S(1)}, u32[]{:S(2)}, u32[]{:S(2)}) collective-permute-start(bf16[96,768]{1,0:T(8,128)(2,1)S(1)} %fusion.15), channel_id=1, source_target_pairs={{0,24},{2,26},{4,28},{6,30},{8,0},{10,2},{12,4},{14,6},{16,8},{18,... | collective-permute-start | bytes 442376 | tf_op jit(solution)/shard_map/ring_by_3/ppermute | solution.py:44
  165.0 17.8 %collective-permute-start.36 = (bf16[48,1536]{1,0:T(8,128)(2,1)}, bf16[48,1536]{1,0:T(8,128)(2,1)}, u32[]{:S(2)}, u32[]{:S(2)}) collective-permute-start(bf16[48,1536]{1,0:T(8,128)(2,1)} %get-tuple-element.225), channel_id=1, source_target_pairs={{0,16},{2,18},{4,20},{6,22},{8,24},{10,26},{12,28},{14,30},{16,0},... | collective-permute-start | bytes 442376 | tf_op jit(solution)/shard_map/ring_by_2/ppermute | solution.py:44
  165.7 17.1 %collective-permute-start.37 = (bf16[48,1536]{1,0:T(8,128)(2,1)}, bf16[48,1536]{1,0:T(8,128)(2,1)}, u32[]{:S(2)}, u32[]{:S(2)}) collective-permute-start(bf16[48,1536]{1,0:T(8,128)(2,1)} %get-tuple-element.224), channel_id=1, source_target_pairs={{0,8},{2,10},{4,12},{6,14},{8,16},{10,18},{12,20},{14,22},{16,24},... | collective-permute-start | bytes 442376 | tf_op jit(solution)/shard_map/ring_by_1/ppermute | solution.py:44
  166.9 22.0 %all-to-all-start.2 = ((bf16[16,16,768]{2,1,0:T(8,128)(2,1)}), bf16[16,16,768]{2,1,0:T(8,128)(2,1)S(1)}, u32[]{:S(2)}, u32[]{:S(2)}) async-start(bf16[16,16,768]{2,1,0:T(8,128)(2,1)} %broadcast_in_dim.39), calls=%async_computation.2 | async-start | bytes 786432 | tf_op jit(solution)/shard_map/all_to_all | solution.py:624
  173.3 15.6 %collective-permute-start.35 = (bf16[48,1536]{1,0:T(8,128)(2,1)S(1)}, bf16[48,1536]{1,0:T(8,128)(2,1)}, u32[]{:S(2)}, u32[]{:S(2)}) collective-permute-start(bf16[48,1536]{1,0:T(8,128)(2,1)S(1)} %fusion.16), channel_id=1, source_target_pairs={{0,24},{2,26},{4,28},{6,30},{8,0},{10,2},{12,4},{14,6},{16,8},{18,... | collective-permute-start | bytes 442376 | tf_op jit(solution)/shard_map/ring_by_3/ppermute | solution.py:44
  190.0 18.0 %collective-permute-start.42 = (f32[24,1536]{1,0:T(8,128)S(1)}, f32[24,1536]{1,0:T(8,128)S(1)}, u32[]{:S(2)}, u32[]{:S(2)}) collective-permute-start(f32[24,1536]{1,0:T(8,128)S(1)} %slice_select_fusion), channel_id=1, source_target_pairs={{0,1},{1,0},{2,3},{3,2},{4,5},{5,4},{6,7},{7,6},{8,9},{9,8},{10,11... | collective-permute-start | bytes 442376 | tf_op jit(solution)/shard_map/ppermute | solution.py:404
  (88 other events, 579.1 us)

commit v3 on v2

--- a/solution.py
+++ b/solution.py
@@ -70,7 +70,7 @@
             return held + [self.shift(blocks, -offset) for offset in self.offsets[1:]], tie
         up, down = self.shift(blocks, 1), self.shift(blocks, -1)
         if tie is not None:
-            (up, down), tie = after((up, down), tie)
+            up, tie = after(up, tie)
         for count, by, moved in ((self.back, 1, up), (self.ahead, -1, down)):
             for j in range(count):
                 moved = self.shift(moved, by) if j else moved
@@ -95,13 +95,12 @@
                 total = total + term
         return total, early
 
-    def swap_add(self, kept, sent, last):
+    def swap_add(self, kept, sent, last, count=2):
         got = self.swap(sent, last)
-        half = kept.shape[0] // 2
-        return [
-            (kept[i * half : (i + 1) * half].astype(f32) + got[i * half : (i + 1) * half].astype(f32))
-            for i in range(2)
-        ]
+        size = kept.shape[0] // count
+        shape = (size, *kept.shape[1:])
+        outs = [(shape, bf16)] * count
+        return kernel(functools.partial(add_kernel, size), "add", outs, kept, got)
 
 
 def after(x, earlier):
@@ -122,6 +121,13 @@
             if len(outs) > 1:
                 outs[1][turned(chips, places[r])] = ref[i, :, widths[0] :]
             r += 1
+
+
+def add_kernel(size, kept_ref, got_ref, *outs):
+    for i, out in enumerate(outs):
+        for j in range(size):
+            k = i * size + j
+            out[j] = (kept_ref[k].astype(f32) + got_ref[k].astype(f32)).astype(out.dtype)
 
 
 def relative_kernel(chips, ring_first, count, width, *refs):
@@ -477,7 +483,6 @@
     held_2 = jnp.concatenate([held_2, chips.swap(held_2, 1)], 0)
     ring_q = jnp.concatenate(chips.ring_gather(block_q[None], True)[0], 0)
     swap_q = chips.swap(ring_q, 0)
-    got, swap_q = after(got, swap_q)
 
     def extra(i, length):
         part = got[:, bounds[i] : bounds[i + 1]].reshape(nd, -1)
@@ -508,7 +513,7 @@
     half_q = jnp.concatenate([ring_q, swap_q], 0)
     last_q = chips.swap(half_q, 1)
     block_1 = across(fc1_mine.reshape(rows, FF // 2), fc1_others.reshape(rows, FF // 2))
-    block_1, swap_q = after(block_1, swap_q)
+    block_1, ring_q = after(block_1, ring_q)
     ring_1 = jnp.concatenate(chips.ring_gather(block_1[None], True)[0], 0)
     swap_1 = chips.swap(ring_1, 0)
     half_1 = jnp.concatenate([ring_1, swap_1], 0)
@@ -547,6 +552,7 @@
         [(wide, f32), ((half, D), bf16)],
         attended, proj_mine, proj_got,
     )
+    parts_2[-1], part = after(parts_2[-1], part)
     residual, branch, normed_second, activated, slope, d_mlp, fc2_grad = kernel(
         mlp_kernel,
         "mlp",
@@ -584,7 +590,7 @@
     )
     proj_got = other_core(proj_sent)
     d_attended, total_2 = after(d_attended, total_2)
-    total_2 = chips.swap_add(total_2[0], total_2[1].astype(bf16), 0)
+    total_2 = chips.swap_add(*total_2, 0, chips.ring)
     d_qkv, d_qkv_sum, part, sent = kernel(
         attention_back_kernel,
         "attention_back",
@@ -592,6 +598,7 @@
         qkv, attended, d_attended, logs, qkv_full,
     )
     got = other_core(sent)
+    d_qkv, proj_got = after(d_qkv, proj_got)
     (qkv_grad,) = kernel(
         qkv_grad_kernel, "qkv_grad", [((D, 3 * half), bf16)], normed_first, d_qkv
     )
@@ -602,10 +609,8 @@
         2,
         [qkv_grad.reshape(n, 2 * rows, 3 * half), proj_grad.reshape(blocks), proj_got.reshape(blocks)],
     )
-    got, (kept_q, sent_q, total_2) = after(got, (kept_q, sent_q, total_2))
-    total_2 = [x for half in total_2 for x in half]
-    terms_2 = chips.direct_scatter(total_2)
-    total_1 = chips.swap_add(total_1[0], total_1[1].astype(bf16), 0)
+    got, (kept_q, sent_q) = after(got, (kept_q, sent_q))
+    total_1 = chips.swap_add(*total_1, 0, chips.ring)
     mlp_got = other_core(mlp_sent)
     latents_grad, output, small = kernel(
         finish_kernel,
@@ -617,25 +622,27 @@
     total_q = chips.swap_add(kept_q, sent_q, 1)
 
     small = small + other_core(small)
-    small, (total_q, total_1, terms_2) = after(small, (total_q, total_1, terms_2))
-    total_1 = [x for half in total_1 for x in half]
-    terms_1 = chips.direct_scatter(total_1)
+    small, total_2 = after(small, total_2)
+    total_2 = [x for half in total_2 for x in half]
+    terms_2 = chips.direct_scatter(total_2)
     small = jnp.broadcast_to(small.astype(bf16)[None], (n, 16, D))
     got = lax.all_to_all(small, "fsdp", 0, 0, tiled=True)
-    total_q = chips.swap_add(total_q[0], total_q[1].astype(bf16), 0)
-    got, (total_q, terms_1) = after(got, (total_q, terms_1))
-    total_q = [x for half in total_q for x in half]
-    terms_q = chips.direct_scatter(total_q)
+    got, (total_q, total_1, terms_2) = after(got, (total_q, total_1, terms_2))
+    total_q = chips.swap_add(*total_q, 0, chips.ring)
+    total_q, total_1 = ([x for half in t for x in half] for t in (total_q, total_1))
+    terms_1 = chips.direct_scatter(total_1)
     ada_w_grad, d_embedded, sums = kernel(
         modulation_back_kernel,
         "modulation_back",
         [((cols, 6 * D), f32), ((cols, n), f32), ((16, D), f32)],
         got, ada_w, condition, embedded.T,
     )
+    d_embedded, total_q = after(d_embedded, total_q)
+    terms_q = chips.direct_scatter(total_q)
     d_embedded = lax.all_to_all(
         jnp.broadcast_to(d_embedded[None], (nd, cols, n)), BOTH, 0, 0, tiled=True
     ).reshape(D, n)
-    d_embedded, terms_q = after(d_embedded, terms_q)
+    d_embedded, (terms_q, terms_1) = after(d_embedded, (terms_q, terms_1))
     qkv_grad, fc1_grad, fc2_grad = (
         sum(x.astype(f32) for x in [total[0]] + terms)
         for total, terms in ((total_q, terms_q), (total_1, terms_1), (total_2, terms_2))

time: 216 us -> 206 us (0.954)
  other arithmetic: 15.6 us -> 6.96 us
  starting transfers between devices: 70 us -> 65.1 us
  Pallas kernels: 31.2 us -> 35.5 us
    all_to_all x1, waiting for transfers between devices: 12.2 us -> 0.01 us  [shards(): partial = lax.all_to_all(partial, 'fsdp', 0, 0, tiled=True)]
    all_to_all x1, waiting for transfers between devices: 0.01 us -> 10.6 us  [shards(): lax.all_to_all(jnp.broadcast_to(d_embedded[None], (nd, cols, n)), BOTH, 0...]
    add x10 -> x0, other arithmetic: 7.53 us -> none  [swap_add(): kept[i * half:(i + 1) * half].astype(f32)]
    ppermute x12, waiting for transfers between devices: 24.1 us -> 30.9 us  [swap(): return lax.ppermute(x, BOTH, pairs)]
    pallas_call x16 -> x22, Pallas kernels: 31.2 us -> 35.5 us  [kernel(): pl.pallas_call(body, out_shape=shapes, in_specs=[pl.BlockSpec(memory_spac...]
    all_to_all x1, waiting for transfers between devices: 3.77 us -> 0.01 us  [shards(): got = lax.all_to_all(sent, BOTH, 0, 0, tiled=True)]
    ppermute x18, starting transfers between devices: 34.4 us -> 31.1 us  [shift(): return lax.ppermute(x, 'fsdp', pairs)]
    all_to_all x1, starting transfers between devices: 6.38 us -> 4.02 us  [shards(): got = lax.all_to_all(small, 'fsdp', 0, 0, tiled=True)]
  transfers between devices with their start and end apart: 47 -> 47, of which waited for: 18 -> 16; matrix products, arithmetic and copies ran while one was open for 18% -> 13% of each run, Pallas kernels for 15% -> 17%
where the time goes in v3:
time: 206 us; the launch traced here: 205 us
  starting transfers between devices  65.1 us (32%)
  waiting for transfers between devices  61.7 us (30%)
  Pallas kernels  35.5 us (17%)
  local copies, waits for them, and re-layouts  32 us (16%)
  other arithmetic  6.96 us (3%)
  between operations  3.08 us (1%)
    pallas_call x22, Pallas kernels, kernel(): pl.pallas_call(body, out_shape=shapes, in_specs=[pl.BlockSpec(memory_spac...  35.5 us
    ppermute x18, starting transfers between devices, shift(): return lax.ppermute(x, 'fsdp', pairs)  31.1 us
    ppermute x12, waiting for transfers between devices, swap(): return lax.ppermute(x, BOTH, pairs)  30.9 us
    ppermute x18, waiting for transfers between devices, shift(): return lax.ppermute(x, 'fsdp', pairs)  19.1 us
    ppermute x12, starting transfers between devices, swap(): return lax.ppermute(x, BOTH, pairs)  17 us
    unnamed x104, local copies, waits for them, and re-layouts  16.4 us
    all_to_all x1, waiting for transfers between devices, shards(): lax.all_to_all(jnp.broadcast_to(d_embedded[None], (nd, cols, n)), BOTH, 0...  10.6 us
  transfers between devices with their start and end apart: 47, of which 16 were waited for; matrix products, arithmetic and copies ran while one was open for 13% of the time, Pallas kernels for 17%

profile of v3, /device:TPU:0, one launch (start us, length us, event | category | flops | bytes accessed | tf_op | source)
XLA Modules:
  0.0 205.2 jit_solution(1831315393832213205)
XLA Ops:
  3.4 2.9 %collective-permute-start.9 = (bf16[1,96,768]{2,1,0:T(8,128)(2,1)S(1)}, bf16[1,96,768]{2,1,0:T(8,128)(2,1)S(1)}, u32[]{:S(2)}, u32[]{:S(2)}) collective-permute-start(bf16[1,96,768]{2,1,0:T(8,128)(2,1)S(1)} %bitcast.134), channel_id=1, source_target_pairs={{0,2},{1,5},{2,0},{3,7},{4,6},{5,1},{6,4},{7,3},{8,10},{9,13},{10,... | collective-permute-start | bytes 442376 | tf_op jit(solution)/shard_map/first_swap/ppermute | solution.py:53
  11.7 2.6 %collective-permute-start.5 = (bf16[1,48,1536]{2,1,0:T(8,128)(2,1)S(1)}, bf16[1,48,1536]{2,1,0:T(8,128)(2,1)S(1)}, u32[]{:S(2)}, u32[]{:S(2)}) collective-permute-start(bf16[1,48,1536]{2,1,0:T(8,128)(2,1)S(1)} %bitcast.129), channel_id=1, source_target_pairs={{0,16},{2,18},{4,20},{6,22},{8,24},{10,26},{12,28},{14,30},{16,0},... | collective-permute-start | bytes 442376 | tf_op jit(solution)/shard_map/ring_by_2/ppermute | solution.py:44
  17.2 2.6 %all-to-all-start = ((bf16[32,2,1056]{2,1,0:T(2,128)(2,1)}), bf16[32,2,1056]{2,1,0:T(2,128)(2,1)S(1)}, u32[]{:S(2)}, u32[]{:S(2)}) async-start(bf16[32,2,1056]{2,1,0:T(2,128)(2,1)} %reshape.294), calls=%async_computation | async-start | bytes 294912 | tf_op jit(solution)/shard_map/all_to_all | solution.py:479
  21.6 3.1 %collective-permute-done.5 = bf16[1,48,1536]{2,1,0:T(8,128)(2,1)S(1)} collective-permute-done((bf16[1,48,1536]{2,1,0:T(8,128)(2,1)S(1)}, bf16[1,48,1536]{2,1,0:T(8,128)(2,1)S(1)}, u32[]{:S(2)}, u32[]{:S(2)}) %collective-permute-start.5) | collective-permute-done | bytes 147488 | tf_op jit(solution)/shard_map/ring_by_2/ppermute | solution.py:44
  25.4 5.3 %collective-permute-start.11 = (bf16[1,48,1536]{2,1,0:T(8,128)(2,1)S(1)}, bf16[1,48,1536]{2,1,0:T(8,128)(2,1)S(1)}, u32[]{:S(2)}, u32[]{:S(2)}) collective-permute-start(bf16[1,48,1536]{2,1,0:T(8,128)(2,1)S(1)} %bitcast.124), channel_id=1, source_target_pairs={{0,8},{2,10},{4,12},{6,14},{8,16},{10,18},{12,20},{14,22},{16,24},... | collective-permute-start | bytes 442376 | tf_op jit(solution)/shard_map/ring_by_1/ppermute | solution.py:44
  38.0 3.6 %all-to-all-start.1 = ((f32[16,36,128]{2,1,0:T(8,128)}), f32[16,36,128]{2,1,0:T(8,128)S(1)}, u32[]{:S(2)}, u32[]{:S(2)}) async-start(f32[16,36,128]{2,1,0:T(8,128)} %reshape.233), calls=%async_computation.1 | async-start | bytes 655360 | tf_op jit(solution)/shard_map/all_to_all | solution.py:524
  42.5 3.7 %collective-permute-start.13 = (bf16[1,48,1536]{2,1,0:T(8,128)(2,1)S(1)}, bf16[1,48,1536]{2,1,0:T(8,128)(2,1)S(1)}, u32[]{:S(2)}, u32[]{:S(2)}) collective-permute-start(bf16[1,48,1536]{2,1,0:T(8,128)(2,1)S(1)} %bitcast.126), channel_id=1, source_target_pairs={{0,24},{2,26},{4,28},{6,30},{8,0},{10,2},{12,4},{14,6},{16,8},{18,... | collective-permute-start | bytes 442376 | tf_op jit(solution)/shard_map/ring_by_3/ppermute | solution.py:44
  48.5 2.8 %collective-permute-done.13 = bf16[1,48,1536]{2,1,0:T(8,128)(2,1)S(1)} collective-permute-done((bf16[1,48,1536]{2,1,0:T(8,128)(2,1)S(1)}, bf16[1,48,1536]{2,1,0:T(8,128)(2,1)S(1)}, u32[]{:S(2)}, u32[]{:S(2)}) %collective-permute-start.13) | collective-permute-done | bytes 147488 | tf_op jit(solution)/shard_map/ring_by_3/ppermute | solution.py:44
  56.0 3.3 %collective-permute-start.14 = (bf16[4,96,768]{2,1,0:T(8,128)(2,1)S(1)}, bf16[4,96,768]{2,1,0:T(8,128)(2,1)}, u32[]{:S(2)}, u32[]{:S(2)}) collective-permute-start(bf16[4,96,768]{2,1,0:T(8,128)(2,1)S(1)} %pad_maximum_fusion.1.refs_0_), channel_id=1, source_target_pairs={{0,8},{2,10},{4,12},{6,14},{8,16},{10,18},{12,20},{14,22},{16,24},... | collective-permute-start | bytes 1769480 | tf_op jit(solution)/shard_map/ring_by_1/ppermute | solution.py:44
  59.9 7.8 %collective-permute-done.18.refs_1_ = bf16[4,48,1536]{2,1,0:T(8,128)(2,1)S(1)} collective-permute-done((bf16[4,48,1536]{2,1,0:T(8,128)(2,1)S(1)}, bf16[4,48,1536]{2,1,0:T(8,128)(2,1)S(1)}, u32[]{:S(2)}, u32[]{:S(2)}) %collective-permute-start.18) | collective-permute-done | bytes 589856 | tf_op jit(solution)/shard_map/first_swap/ppermute | solution.py:53
  80.2 3.0 %collective-permute-done.15.refs_3_ = bf16[4,96,768]{2,1,0:T(8,128)(2,1)} collective-permute-done((bf16[4,96,768]{2,1,0:T(8,128)(2,1)S(1)}, bf16[4,96,768]{2,1,0:T(8,128)(2,1)}, u32[]{:S(2)}, u32[]{:S(2)}) %collective-permute-start.15) | collective-permute-done | bytes 589856 | tf_op jit(solution)/shard_map/ring_by_3/ppermute | solution.py:44
  83.6 3.4 %collective-permute-done.19.refs_2_ = bf16[8,48,1536]{2,1,0:T(8,128)(2,1)} collective-permute-done((bf16[8,48,1536]{2,1,0:T(8,128)(2,1)}, bf16[8,48,1536]{2,1,0:T(8,128)(2,1)}, u32[]{:S(2)}, u32[]{:S(2)}) %collective-permute-start.19) | collective-permute-done | bytes 1179680 | tf_op jit(solution)/shard_map/last_swap/ppermute | solution.py:53
  88.5 5.4 %mlp.1 = (f32[256,768]{1,0:T(8,128)S(1)}, f32[128,768]{1,0:T(8,128)S(1)}, bf16[256,768]{1,0:T(8,128)(2,1)S(1)}, bf16[256,1536]{1,0:T(8,128)(2,1)S(1)}, f32[256,1...) custom-call(bf16[256,768]{1,0:T(8,128)(2,1)S(1)} %get-tuple-element.259.x_ref, ...), custom_call_target="tpu_custom_call" | custom-call | bytes 11430912 | tf_op jit(solution)/shard_map/mlp/pallas_call | solution.py:148
  94.1 7.7 %collective-permute-done.20.refs_2_ = bf16[4,96,768]{2,1,0:T(8,128)(2,1)S(1)} collective-permute-done((bf16[4,96,768]{2,1,0:T(8,128)(2,1)}, bf16[4,96,768]{2,1,0:T(8,128)(2,1)S(1)}, u32[]{:S(2)}, u32[]{:S(2)}) %collective-permute-start.20) | collective-permute-done | bytes 589856 | tf_op jit(solution)/shard_map/ring_by_1/ppermute | solution.py:44
  103.8 3.9 %mlp_back.1 = (bf16[256,1536]{1,0:T(8,128)(2,1)S(1)}, f32[1,1536]{1,0:T(1,128)S(1)}, f32[256,768]{1,0:T(8,128)S(1)}) custom-call(bf16[256,768]{1,0:T(8,128)(2,1)S(1)} %get-tuple-element.153.d_mlp_ref, f32[256,1536]{1,0:T(8,128)S(1)} %get-tuple-element.154.slope_ref, bf16[1536,768]{1,0:T(8,128)(2,1)S(1)} %bitcast.102, bf16[768,1536]{1,0:T(8,128)(2,1)S(1)} %bitcast.101), custom_call_target="tpu_custom_call" | custom-call | bytes 8263680 | tf_op jit(solution)/shard_map/mlp_back/pallas_call | solution.py:148
  108.4 3.0 %mlp_grad.1 = (f32[128,768]{1,0:T(8,128)S(1)}, f32[128,768]{1,0:T(8,128)S(1)}, bf16[768,1536]{1,0:T(8,128)(2,1)S(1)}) custom-call(bf16[256,1536]{1,0:T(8,128)(2,1)S(1)} %get-tuple-element.165.act_ref, bf16[1536,768]{1,0:T(8,128)(2,1)S(1)} %bitcast.103, bf16[256,768]{1,0:T(8,128)(2,1)S(1)} %get-tuple-element.166.normed_ref, ...), custom_call_target="tpu_custom_call" | custom-call | bytes 7471104 | tf_op jit(solution)/shard_map/mlp_grad/pallas_call | solution.py:148
  118.3 3.4 %attention_back.1 = (bf16[256,1152]{1,0:T(8,128)(2,1)S(1)}, f32[1,1152]{1,0:T(1,128)S(1)}, f32[128,768]{1,0:T(8,128)S(1)}, f32[128,768]{1,0:T(8,128)S(1)}) custom-call(bf16[256,1152]{1,0:T(8,128)(2,1)S(1)} %get-tuple-element.141.qkv_ref, bf16[256,384]{1,0:T(8,128)(2,1)S(1)} %get-tuple-element.145.att_ref, bf16[256,384]{1,0:T(8,128)(2,1)S(1)} %get-tuple-element.179.d_att_ref, ...), custom_call_target="tpu_custom_call" | custom-call | bytes 4264448 | tf_op jit(solution)/shard_map/attention_back/pallas_call | solution.py:148
  129.9 8.6 %collective-permute-done.27.got_ref = bf16[4,96,768]{2,1,0:T(8,128)(2,1)S(1)} collective-permute-done((bf16[4,96,768]{2,1,0:T(8,128)(2,1)S(1)}, bf16[4,96,768]{2,1,0:T(8,128)(2,1)S(1)}, u32[]{:S(2)}, u32[]{:S(2)}) %collective-permute-start.27) | collective-permute-done | bytes 589856 | tf_op jit(solution)/shard_map/first_swap/ppermute | solution.py:53
  139.5 4.0 %all-to-all-start.2 = ((bf16[16,16,768]{2,1,0:T(8,128)(2,1)}), bf16[16,16,768]{2,1,0:T(8,128)(2,1)S(1)}, u32[]{:S(2)}, u32[]{:S(2)}) async-start(bf16[16,16,768]{2,1,0:T(8,128)(2,1)} %broadcast_in_dim.39), calls=%async_computation.2 | async-start | bytes 786432 | tf_op jit(solution)/shard_map/all_to_all | solution.py:629
  149.1 3.3 %collective-permute-start.31 = (bf16[96,768]{1,0:T(8,128)(2,1)}, bf16[96,768]{1,0:T(8,128)(2,1)S(1)}, u32[]{:S(2)}, u32[]{:S(2)}) collective-permute-start(bf16[96,768]{1,0:T(8,128)(2,1)} %bitcast.119), channel_id=1, source_target_pairs={{0,24},{2,26},{4,28},{6,30},{8,0},{10,2},{12,4},{14,6},{16,8},{18,... | collective-permute-start | bytes 442376 | tf_op jit(solution)/shard_map/ring_by_3/ppermute | solution.py:44
  153.6 5.6 %collective-permute-done.30.got_ref = bf16[4,48,1536]{2,1,0:T(8,128)(2,1)} collective-permute-done((bf16[4,48,1536]{2,1,0:T(8,128)(2,1)}, bf16[4,48,1536]{2,1,0:T(8,128)(2,1)}, u32[]{:S(2)}, u32[]{:S(2)}) %collective-permute-start.30) | collective-permute-done | bytes 589856 | tf_op jit(solution)/shard_map/first_swap/ppermute | solution.py:53
  164.7 2.5 %collective-permute-done.32 = bf16[96,768]{1,0:T(8,128)(2,1)S(1)} collective-permute-done((bf16[96,768]{1,0:T(8,128)(2,1)}, bf16[96,768]{1,0:T(8,128)(2,1)S(1)}, u32[]{:S(2)}, u32[]{:S(2)}) %collective-permute-start.32) | collective-permute-done | bytes 147488 | tf_op jit(solution)/shard_map/ring_by_2/ppermute | solution.py:44
  182.9 3.6 %all-to-all-start.3 = ((f32[32,1,384]{2,1,0:T(1,128)}), f32[32,1,384]{2,1,0:T(1,128)S(1)}, u32[]{:S(2)}, u32[]{:S(2)}) async-start(f32[32,1,384]{2,1,0:T(1,128)} %reshape.296), calls=%async_computation.3 | async-start | bytes 98304 | tf_op jit(solution)/shard_map/all_to_all | solution.py:642
  187.1 10.6 %all-to-all-done.3 = f32[32,1,384]{2,1,0:T(1,128)S(1)} async-done(((f32[32,1,384]{2,1,0:T(1,128)}), f32[32,1,384]{2,1,0:T(1,128)S(1)}, u32[]{:S(2)}, u32[]{:S(2)}) %all-to-all-start.3) | async-done | bytes 49184 | tf_op jit(solution)/shard_map/all_to_all | solution.py:642
  (306 shorter events, 96.4 us)
Async XLA Ops:
  3.4 16.4 %collective-permute-start.9 = (bf16[1,96,768]{2,1,0:T(8,128)(2,1)S(1)}, bf16[1,96,768]{2,1,0:T(8,128)(2,1)S(1)}, u32[]{:S(2)}, u32[]{:S(2)}) collective-permute-start(bf16[1,96,768]{2,1,0:T(8,128)(2,1)S(1)} %bitcast.134), channel_id=1, source_target_pairs={{0,2},{1,5},{2,0},{3,7},{4,6},{5,1},{6,4},{7,3},{8,10},{9,13},{10,... | collective-permute-start | bytes 442376 | tf_op jit(solution)/shard_map/first_swap/ppermute | solution.py:53
  7.7 67.4 %collective-permute-start = (bf16[2,128,768]{2,1,0:T(8,128)(2,1)}, bf16[2,128,768]{2,1,0:T(8,128)(2,1)}, u32[]{:S(2)}, u32[]{:S(2)}) collective-permute-start(bf16[2,128,768]{2,1,0:T(8,128)(2,1)} %constant_dynamic-update-slice_fusion), channel_id=1, source_target_pairs={{0,1},{1,0},{2,3},{3,2},{4,5},{5,4},{6,7},{7,6},{8,9},{9,8},{10,11... | collective-permute-start | bytes 1179656 | tf_op jit(solution)/shard_map/ppermute | solution.py:410
  17.2 18.6 %all-to-all-start = ((bf16[32,2,1056]{2,1,0:T(2,128)(2,1)}), bf16[32,2,1056]{2,1,0:T(2,128)(2,1)S(1)}, u32[]{:S(2)}, u32[]{:S(2)}) async-start(bf16[32,2,1056]{2,1,0:T(2,128)(2,1)} %reshape.294), calls=%async_computation | async-start | bytes 294912 | tf_op jit(solution)/shard_map/all_to_all | solution.py:479
  19.9 35.1 %collective-permute-start.10 = (bf16[2,96,768]{2,1,0:T(8,128)(2,1)S(1)}, bf16[2,96,768]{2,1,0:T(8,128)(2,1)}, u32[]{:S(2)}, u32[]{:S(2)}) collective-permute-start(bf16[2,96,768]{2,1,0:T(8,128)(2,1)S(1)} %pad_maximum_fusion.6), channel_id=1, source_target_pairs={{0,4},{1,3},{2,6},{3,1},{4,0},{5,7},{6,2},{7,5},{8,12},{9,11},{10,... | collective-permute-start | bytes 884744 | tf_op jit(solution)/shard_map/last_swap/ppermute | solution.py:53
  25.4 21.6 %collective-permute-start.11 = (bf16[1,48,1536]{2,1,0:T(8,128)(2,1)S(1)}, bf16[1,48,1536]{2,1,0:T(8,128)(2,1)S(1)}, u32[]{:S(2)}, u32[]{:S(2)}) collective-permute-start(bf16[1,48,1536]{2,1,0:T(8,128)(2,1)S(1)} %bitcast.124), channel_id=1, source_target_pairs={{0,8},{2,10},{4,12},{6,14},{8,16},{10,18},{12,20},{14,22},{16,24},... | collective-permute-start | bytes 442376 | tf_op jit(solution)/shard_map/ring_by_1/ppermute | solution.py:44
  30.7 17.8 %collective-permute-start.12 = (bf16[1,48,1536]{2,1,0:T(8,128)(2,1)S(1)}, bf16[1,48,1536]{2,1,0:T(8,128)(2,1)S(1)}, u32[]{:S(2)}, u32[]{:S(2)}) collective-permute-start(bf16[1,48,1536]{2,1,0:T(8,128)(2,1)S(1)} %bitcast.125), channel_id=1, source_target_pairs={{0,16},{2,18},{4,20},{6,22},{8,24},{10,26},{12,28},{14,30},{16,0},... | collective-permute-start | bytes 442376 | tf_op jit(solution)/shard_map/ring_by_2/ppermute | solution.py:44
  38.0 21.9 %all-to-all-start.1 = ((f32[16,36,128]{2,1,0:T(8,128)}), f32[16,36,128]{2,1,0:T(8,128)S(1)}, u32[]{:S(2)}, u32[]{:S(2)}) async-start(f32[16,36,128]{2,1,0:T(8,128)} %reshape.233), calls=%async_computation.1 | async-start | bytes 655360 | tf_op jit(solution)/shard_map/all_to_all | solution.py:524
  47.0 23.5 %collective-permute-start.8 = (bf16[8,48,1536]{2,1,0:T(8,128)(2,1)}, bf16[8,48,1536]{2,1,0:T(8,128)(2,1)}, u32[]{:S(2)}, u32[]{:S(2)}) collective-permute-start(bf16[8,48,1536]{2,1,0:T(8,128)(2,1)} %constant_dynamic-update-slice_fusion.2), channel_id=1, source_target_pairs={{0,4},{1,3},{2,6},{3,1},{4,0},{5,7},{6,2},{7,5},{8,12},{9,11},{10,... | collective-permute-start | bytes 3538952 | tf_op jit(solution)/shard_map/last_swap/ppermute | solution.py:53
  51.4 16.3 %collective-permute-start.18 = (bf16[4,48,1536]{2,1,0:T(8,128)(2,1)S(1)}, bf16[4,48,1536]{2,1,0:T(8,128)(2,1)S(1)}, u32[]{:S(2)}, u32[]{:S(2)}) collective-permute-start(bf16[4,48,1536]{2,1,0:T(8,128)(2,1)S(1)} %pad_maximum_fusion.2.refs_0_), channel_id=1, source_target_pairs={{0,2},{1,5},{2,0},{3,7},{4,6},{5,1},{6,4},{7,3},{8,10},{9,13},{10,... | collective-permute-start | bytes 1769480 | tf_op jit(solution)/shard_map/first_swap/ppermute | solution.py:53
  56.0 22.9 %collective-permute-start.14 = (bf16[4,96,768]{2,1,0:T(8,128)(2,1)S(1)}, bf16[4,96,768]{2,1,0:T(8,128)(2,1)}, u32[]{:S(2)}, u32[]{:S(2)}) collective-permute-start(bf16[4,96,768]{2,1,0:T(8,128)(2,1)S(1)} %pad_maximum_fusion.1.refs_0_), channel_id=1, source_target_pairs={{0,8},{2,10},{4,12},{6,14},{8,16},{10,18},{12,20},{14,22},{16,24},... | collective-permute-start | bytes 1769480 | tf_op jit(solution)/shard_map/ring_by_1/ppermute | solution.py:44
  59.3 23.9 %collective-permute-start.15 = (bf16[4,96,768]{2,1,0:T(8,128)(2,1)S(1)}, bf16[4,96,768]{2,1,0:T(8,128)(2,1)}, u32[]{:S(2)}, u32[]{:S(2)}) collective-permute-start(bf16[4,96,768]{2,1,0:T(8,128)(2,1)S(1)} %pad_maximum_fusion.1.refs_0_), channel_id=1, source_target_pairs={{0,24},{2,26},{4,28},{6,30},{8,0},{10,2},{12,4},{14,6},{16,8},{18,... | collective-permute-start | bytes 1769480 | tf_op jit(solution)/shard_map/ring_by_3/ppermute | solution.py:44
  70.5 16.5 %collective-permute-start.19 = (bf16[8,48,1536]{2,1,0:T(8,128)(2,1)}, bf16[8,48,1536]{2,1,0:T(8,128)(2,1)}, u32[]{:S(2)}, u32[]{:S(2)}) collective-permute-start(bf16[8,48,1536]{2,1,0:T(8,128)(2,1)} %constant_dynamic-update-slice_fusion.7), channel_id=1, source_target_pairs={{0,4},{1,3},{2,6},{3,1},{4,0},{5,7},{6,2},{7,5},{8,12},{9,11},{10,... | collective-permute-start | bytes 3538952 | tf_op jit(solution)/shard_map/last_swap/ppermute | solution.py:53
  83.2 18.6 %collective-permute-start.20 = (bf16[4,96,768]{2,1,0:T(8,128)(2,1)}, bf16[4,96,768]{2,1,0:T(8,128)(2,1)S(1)}, u32[]{:S(2)}, u32[]{:S(2)}) collective-permute-start(bf16[4,96,768]{2,1,0:T(8,128)(2,1)} %collective-permute-done.14.refs_1_), channel_id=1, source_target_pairs={{0,8},{2,10},{4,12},{6,14},{8,16},{10,18},{12,20},{14,22},{16,24},... | collective-permute-start | bytes 1769480 | tf_op jit(solution)/shard_map/ring_by_1/ppermute | solution.py:44
  101.8 16.2 %collective-permute-start.22 = (bf16[8,96,768]{2,1,0:T(8,128)(2,1)S(1)}, bf16[8,96,768]{2,1,0:T(8,128)(2,1)S(1)}, u32[]{:S(2)}, u32[]{:S(2)}) collective-permute-start(bf16[8,96,768]{2,1,0:T(8,128)(2,1)S(1)} %get-tuple-element.176), channel_id=1, source_target_pairs={{0,4},{1,3},{2,6},{3,1},{4,0},{5,7},{6,2},{7,5},{8,12},{9,11},{10,... | collective-permute-start | bytes 3538952 | tf_op jit(solution)/shard_map/last_swap/ppermute | solution.py:53
  113.6 30.0 %collective-permute-start.29 = (bf16[8,48,1536]{2,1,0:T(8,128)(2,1)}, bf16[8,48,1536]{2,1,0:T(8,128)(2,1)}, u32[]{:S(2)}, u32[]{:S(2)}) collective-permute-start(bf16[8,48,1536]{2,1,0:T(8,128)(2,1)} %get-tuple-element.214), channel_id=1, source_target_pairs={{0,4},{1,3},{2,6},{3,1},{4,0},{5,7},{6,2},{7,5},{8,12},{9,11},{10,... | collective-permute-start | bytes 3538952 | tf_op jit(solution)/shard_map/last_swap/ppermute | solution.py:53
  122.2 16.3 %collective-permute-start.27 = (bf16[4,96,768]{2,1,0:T(8,128)(2,1)S(1)}, bf16[4,96,768]{2,1,0:T(8,128)(2,1)S(1)}, u32[]{:S(2)}, u32[]{:S(2)}) collective-permute-start(bf16[4,96,768]{2,1,0:T(8,128)(2,1)S(1)} %get-tuple-element.203), channel_id=1, source_target_pairs={{0,2},{1,5},{2,0},{3,7},{4,6},{5,1},{6,4},{7,3},{8,10},{9,13},{10,... | collective-permute-start | bytes 1769480 | tf_op jit(solution)/shard_map/first_swap/ppermute | solution.py:53
  126.4 36.0 %collective-permute-start.28 = (bf16[8,48,1536]{2,1,0:T(8,128)(2,1)}, bf16[8,48,1536]{2,1,0:T(8,128)(2,1)S(1)}, u32[]{:S(2)}, u32[]{:S(2)}) collective-permute-start(bf16[8,48,1536]{2,1,0:T(8,128)(2,1)} %get-tuple-element.210), channel_id=1, source_target_pairs={{0,4},{1,3},{2,6},{3,1},{4,0},{5,7},{6,2},{7,5},{8,12},{9,11},{10,... | collective-permute-start | bytes 3538952 | tf_op jit(solution)/shard_map/last_swap/ppermute | solution.py:53
  139.5 28.4 %all-to-all-start.2 = ((bf16[16,16,768]{2,1,0:T(8,128)(2,1)}), bf16[16,16,768]{2,1,0:T(8,128)(2,1)S(1)}, u32[]{:S(2)}, u32[]{:S(2)}) async-start(bf16[16,16,768]{2,1,0:T(8,128)(2,1)} %broadcast_in_dim.39), calls=%async_computation.2 | async-start | bytes 786432 | tf_op jit(solution)/shard_map/all_to_all | solution.py:629
  149.1 15.6 %collective-permute-start.31 = (bf16[96,768]{1,0:T(8,128)(2,1)}, bf16[96,768]{1,0:T(8,128)(2,1)S(1)}, u32[]{:S(2)}, u32[]{:S(2)}) collective-permute-start(bf16[96,768]{1,0:T(8,128)(2,1)} %bitcast.119), channel_id=1, source_target_pairs={{0,24},{2,26},{4,28},{6,30},{8,0},{10,2},{12,4},{14,6},{16,8},{18,... | collective-permute-start | bytes 442376 | tf_op jit(solution)/shard_map/ring_by_3/ppermute | solution.py:44
  169.8 29.6 %collective-permute-start.39 = (bf16[48,1536]{1,0:T(8,128)(2,1)S(1)}, bf16[48,1536]{1,0:T(8,128)(2,1)S(1)}, u32[]{:S(2)}, u32[]{:S(2)}) collective-permute-start(bf16[48,1536]{1,0:T(8,128)(2,1)S(1)} %bitcast.116), channel_id=1, source_target_pairs={{0,16},{2,18},{4,20},{6,22},{8,24},{10,26},{12,28},{14,30},{16,0},... | collective-permute-start | bytes 442376 | tf_op jit(solution)/shard_map/ring_by_2/ppermute | solution.py:44
  170.3 29.1 %collective-permute-start.40 = (bf16[48,1536]{1,0:T(8,128)(2,1)S(1)}, bf16[48,1536]{1,0:T(8,128)(2,1)S(1)}, u32[]{:S(2)}, u32[]{:S(2)}) collective-permute-start(bf16[48,1536]{1,0:T(8,128)(2,1)S(1)} %bitcast.115), channel_id=1, source_target_pairs={{0,8},{2,10},{4,12},{6,14},{8,16},{10,18},{12,20},{14,22},{16,24},... | collective-permute-start | bytes 442376 | tf_op jit(solution)/shard_map/ring_by_1/ppermute | solution.py:44
  178.2 21.2 %collective-permute-start.35 = (bf16[48,1536]{1,0:T(8,128)(2,1)S(1)}, bf16[48,1536]{1,0:T(8,128)(2,1)S(1)}, u32[]{:S(2)}, u32[]{:S(2)}) collective-permute-start(bf16[48,1536]{1,0:T(8,128)(2,1)S(1)} %bitcast.123), channel_id=1, source_target_pairs={{0,24},{2,26},{4,28},{6,30},{8,0},{10,2},{12,4},{14,6},{16,8},{18,... | collective-permute-start | bytes 442376 | tf_op jit(solution)/shard_map/ring_by_3/ppermute | solution.py:44
  179.8 19.6 %collective-permute-start.36 = (bf16[48,1536]{1,0:T(8,128)(2,1)S(1)}, bf16[48,1536]{1,0:T(8,128)(2,1)S(1)}, u32[]{:S(2)}, u32[]{:S(2)}) collective-permute-start(bf16[48,1536]{1,0:T(8,128)(2,1)S(1)} %bitcast.122), channel_id=1, source_target_pairs={{0,16},{2,18},{4,20},{6,22},{8,24},{10,26},{12,28},{14,30},{16,0},... | collective-permute-start | bytes 442376 | tf_op jit(solution)/shard_map/ring_by_2/ppermute | solution.py:44
  180.5 19.0 %collective-permute-start.37 = (bf16[48,1536]{1,0:T(8,128)(2,1)S(1)}, bf16[48,1536]{1,0:T(8,128)(2,1)S(1)}, u32[]{:S(2)}, u32[]{:S(2)}) collective-permute-start(bf16[48,1536]{1,0:T(8,128)(2,1)S(1)} %bitcast.121), channel_id=1, source_target_pairs={{0,8},{2,10},{4,12},{6,14},{8,16},{10,18},{12,20},{14,22},{16,24},... | collective-permute-start | bytes 442376 | tf_op jit(solution)/shard_map/ring_by_1/ppermute | solution.py:44
  (65 other events, 402.8 us)

commit v4 on v3

--- a/solution.py
+++ b/solution.py
@@ -265,7 +265,7 @@
         slope_ref[:, cols] = 0.5 * (1.0 + t) + 0.5 * v * (1.0 - t * t) * (a * (1.0 + 3.0 * c * square))
         grad_ref[cols, :] = dot_t(act, d_mlp_ref[...], bf16)
 
-    tiles(w_ref.shape[1], 256, tile)
+    tiles(w_ref.shape[1], 512, tile)
 
 
 def mlp_back_kernel(d_mlp_ref, slope_ref, w2_ref, w1_ref, d_pre_ref, sum_ref, d_normed_ref):
@@ -277,7 +277,7 @@
         sum_ref[:, cols] = jnp.sum(d_pre.astype(f32), 0, keepdims=True)
         d_normed_ref[...] += dot_nt(d_pre, w1_ref[:, cols])
 
-    tiles(w1_ref.shape[1], 256, tile)
+    tiles(w1_ref.shape[1], 512, tile)
 
 
 def mlp_grad_kernel(act_ref, w2_ref, normed_ref, d_pre_ref, own_ref, sent_ref, grad_ref):
@@ -291,8 +291,8 @@
     def grad_tile(cols):
         grad_ref[:, cols] = dot_t(normed_ref[...], d_pre_ref[:, cols], bf16)
 
-    tiles(w2_ref.shape[1], 256, out_tile)
-    tiles(d_pre_ref.shape[1], 256, grad_tile)
+    tiles(w2_ref.shape[1], 384, out_tile)
+    tiles(d_pre_ref.shape[1], 512, grad_tile)
 
 
 def branch_back_kernel(
@@ -478,7 +478,7 @@
     sent, block_q = after(sent, block_q)
     got = lax.all_to_all(sent, BOTH, 0, 0, tiled=True)
 
-    held_2 = fc2_w[None]
+    held_2, block_q = after(fc2_w[None], block_q)
     held_2 = jnp.concatenate([held_2, chips.swap(held_2, 0)], 0)
     held_2 = jnp.concatenate([held_2, chips.swap(held_2, 1)], 0)
     ring_q = jnp.concatenate(chips.ring_gather(block_q[None], True)[0], 0)
@@ -627,7 +627,7 @@
     terms_2 = chips.direct_scatter(total_2)
     small = jnp.broadcast_to(small.astype(bf16)[None], (n, 16, D))
     got = lax.all_to_all(small, "fsdp", 0, 0, tiled=True)
-    got, (total_q, total_1, terms_2) = after(got, (total_q, total_1, terms_2))
+    got, (total_q, total_1, terms_2[0]) = after(got, (total_q, total_1, terms_2[0]))
     total_q = chips.swap_add(*total_q, 0, chips.ring)
     total_q, total_1 = ([x for half in t for x in half] for t in (total_q, total_1))
     terms_1 = chips.direct_scatter(total_1)
@@ -637,7 +637,7 @@
         [((cols, 6 * D), f32), ((cols, n), f32), ((16, D), f32)],
         got, ada_w, condition, embedded.T,
     )
-    d_embedded, total_q = after(d_embedded, total_q)
+    d_embedded, (total_q, terms_2) = after(d_embedded, (total_q, terms_2))
     terms_q = chips.direct_scatter(total_q)
     d_embedded = lax.all_to_all(
         jnp.broadcast_to(d_embedded[None], (nd, cols, n)), BOTH, 0, 0, tiled=True

time: 206 us -> 201 us (0.976)
  Pallas kernels: 35.5 us -> 31.2 us
    ppermute x12, waiting for transfers between devices: 30.9 us -> 42 us  [swap(): return lax.ppermute(x, BOTH, pairs)]
    all_to_all x1, waiting for transfers between devices: 10.6 us -> 0.91 us  [shards(): lax.all_to_all(jnp.broadcast_to(d_embedded[None], (nd, cols, n)), BOTH, 0...]
    pallas_call x22, Pallas kernels: 35.5 us -> 31.2 us  [kernel(): pl.pallas_call(body, out_shape=shapes, in_specs=[pl.BlockSpec(memory_spac...]
    unnamed x104 -> x100, local copies, waits for them, and re-layouts: 16.4 us -> 15.8 us
  transfers between devices with their start and end apart: 47 -> 47, of which waited for: 16 -> 15; matrix products, arithmetic and copies ran while one was open for 13% -> 13% of each run, Pallas kernels for 17% -> 16%
where the time goes in v4:
time: 201 us
  starting transfers between devices  65.9 us (33%)
  waiting for transfers between devices  62.2 us (31%)
  local copies, waits for them, and re-layouts  31.4 us (16%)
  Pallas kernels  31.2 us (16%)
  other arithmetic  5.99 us (3%)
  between operations  3.08 us (2%)
    ppermute x12, waiting for transfers between devices, swap(): return lax.ppermute(x, BOTH, pairs)  42 us
    ppermute x18, starting transfers between devices, shift(): return lax.ppermute(x, 'fsdp', pairs)  33.1 us
    pallas_call x22, Pallas kernels, kernel(): pl.pallas_call(body, out_shape=shapes, in_specs=[pl.BlockSpec(memory_spac...  31.2 us
    ppermute x18, waiting for transfers between devices, shift(): return lax.ppermute(x, 'fsdp', pairs)  17.5 us
    unnamed x100, local copies, waits for them, and re-layouts  15.8 us
    ppermute x12, starting transfers between devices, swap(): return lax.ppermute(x, BOTH, pairs)  15.3 us
    all_to_all x1, starting transfers between devices, shards(): partial = lax.all_to_all(partial, 'fsdp', 0, 0, tiled=True)  4.36 us
  transfers between devices with their start and end apart: 47, of which 15 were waited for; matrix products, arithmetic and copies ran while one was open for 13% of the time, Pallas kernels for 16%

profile of v4, /device:TPU:0, one launch (start us, length us, event | category | flops | bytes accessed | tf_op | source)
XLA Modules:
  0.0 200.6 jit_solution(5628484554416122602)
XLA Ops:
  7.6 2.6 %collective-permute-start.4 = (bf16[1,48,1536]{2,1,0:T(8,128)(2,1)S(1)}, bf16[1,48,1536]{2,1,0:T(8,128)(2,1)S(1)}, u32[]{:S(2)}, u32[]{:S(2)}) collective-permute-start(bf16[1,48,1536]{2,1,0:T(8,128)(2,1)S(1)} %bitcast.128), channel_id=1, source_target_pairs={{0,8},{2,10},{4,12},{6,14},{8,16},{10,18},{12,20},{14,22},{16,24},... | collective-permute-start | bytes 442376 | tf_op jit(solution)/shard_map/ring_by_1/ppermute | solution.py:44
  10.2 2.6 %collective-permute-start.5 = (bf16[1,48,1536]{2,1,0:T(8,128)(2,1)S(1)}, bf16[1,48,1536]{2,1,0:T(8,128)(2,1)S(1)}, u32[]{:S(2)}, u32[]{:S(2)}) collective-permute-start(bf16[1,48,1536]{2,1,0:T(8,128)(2,1)S(1)} %bitcast.129), channel_id=1, source_target_pairs={{0,16},{2,18},{4,20},{6,22},{8,24},{10,26},{12,28},{14,30},{16,0},... | collective-permute-start | bytes 442376 | tf_op jit(solution)/shard_map/ring_by_2/ppermute | solution.py:44
  17.2 2.6 %all-to-all-start = ((bf16[32,2,1056]{2,1,0:T(2,128)(2,1)}), bf16[32,2,1056]{2,1,0:T(2,128)(2,1)S(1)}, u32[]{:S(2)}, u32[]{:S(2)}) async-start(bf16[32,2,1056]{2,1,0:T(2,128)(2,1)} %reshape.294), calls=%async_computation | async-start | bytes 294912 | tf_op jit(solution)/shard_map/all_to_all | solution.py:479
  19.8 3.3 %collective-permute-done.5 = bf16[1,48,1536]{2,1,0:T(8,128)(2,1)S(1)} collective-permute-done((bf16[1,48,1536]{2,1,0:T(8,128)(2,1)S(1)}, bf16[1,48,1536]{2,1,0:T(8,128)(2,1)S(1)}, u32[]{:S(2)}, u32[]{:S(2)}) %collective-permute-start.5) | collective-permute-done | bytes 147488 | tf_op jit(solution)/shard_map/ring_by_2/ppermute | solution.py:44
  23.9 5.3 %collective-permute-start.11 = (bf16[1,48,1536]{2,1,0:T(8,128)(2,1)S(1)}, bf16[1,48,1536]{2,1,0:T(8,128)(2,1)S(1)}, u32[]{:S(2)}, u32[]{:S(2)}) collective-permute-start(bf16[1,48,1536]{2,1,0:T(8,128)(2,1)S(1)} %bitcast.124), channel_id=1, source_target_pairs={{0,8},{2,10},{4,12},{6,14},{8,16},{10,18},{12,20},{14,22},{16,24},... | collective-permute-start | bytes 442376 | tf_op jit(solution)/shard_map/ring_by_1/ppermute | solution.py:44
  37.2 4.4 %all-to-all-start.1 = ((f32[16,36,128]{2,1,0:T(8,128)}), f32[16,36,128]{2,1,0:T(8,128)S(1)}, u32[]{:S(2)}, u32[]{:S(2)}) async-start(f32[16,36,128]{2,1,0:T(8,128)} %reshape.233), calls=%async_computation.1 | async-start | bytes 655360 | tf_op jit(solution)/shard_map/all_to_all | solution.py:524
  49.8 4.9 %collective-permute-done.10 = bf16[2,96,768]{2,1,0:T(8,128)(2,1)S(1)} collective-permute-done((bf16[2,96,768]{2,1,0:T(8,128)(2,1)S(1)}, bf16[2,96,768]{2,1,0:T(8,128)(2,1)S(1)}, u32[]{:S(2)}, u32[]{:S(2)}) %collective-permute-start.10) | collective-permute-done | bytes 294944 | tf_op jit(solution)/shard_map/last_swap/ppermute | solution.py:53
  56.2 2.4 %collective-permute-start.15 = (bf16[4,96,768]{2,1,0:T(8,128)(2,1)S(1)}, bf16[4,96,768]{2,1,0:T(8,128)(2,1)}, u32[]{:S(2)}, u32[]{:S(2)}) collective-permute-start(bf16[4,96,768]{2,1,0:T(8,128)(2,1)S(1)} %pad_maximum_fusion.1.refs_0_), channel_id=1, source_target_pairs={{0,24},{2,26},{4,28},{6,30},{8,0},{10,2},{12,4},{14,6},{16,8},{18,... | collective-permute-start | bytes 1769480 | tf_op jit(solution)/shard_map/ring_by_3/ppermute | solution.py:44
  58.7 4.3 %collective-permute-done.18.refs_1_ = bf16[4,48,1536]{2,1,0:T(8,128)(2,1)S(1)} collective-permute-done((bf16[4,48,1536]{2,1,0:T(8,128)(2,1)S(1)}, bf16[4,48,1536]{2,1,0:T(8,128)(2,1)S(1)}, u32[]{:S(2)}, u32[]{:S(2)}) %collective-permute-start.18) | collective-permute-done | bytes 589856 | tf_op jit(solution)/shard_map/first_swap/ppermute | solution.py:53
  63.9 6.7 %collective-permute-done.8.refs_2_ = bf16[8,48,1536]{2,1,0:T(8,128)(2,1)} collective-permute-done((bf16[8,48,1536]{2,1,0:T(8,128)(2,1)}, bf16[8,48,1536]{2,1,0:T(8,128)(2,1)}, u32[]{:S(2)}, u32[]{:S(2)}) %collective-permute-start.8) | collective-permute-done | bytes 1179680 | tf_op jit(solution)/shard_map/last_swap/ppermute | solution.py:53
  76.4 2.4 %attention.1 = (bf16[256,768]{1,0:T(8,128)(2,1)S(1)}, bf16[256,1152]{1,0:T(8,128)(2,1)S(1)}, bf16[256,384]{1,0:T(8,128)(2,1)S(1)}, f32[256,128]{1,0:T(8,128)S(1)}) custom-call(bf16[256,768]{1,0:T(8,128)(2,1)S(1)} %get-tuple-element.265.x_ref, f32[6,768]{1,0:T(8,128)S(1)} %reshape.250.mod_ref, bf16[768,1152]{1,0:T(8,128)(2,1)S(1)} %bitcast.104, ...), custom_call_target="tpu_custom_call" | custom-call | bytes 3494912 | tf_op jit(solution)/shard_map/attention/pallas_call | solution.py:148
  82.0 5.1 %collective-permute-done.19.refs_2_ = bf16[8,48,1536]{2,1,0:T(8,128)(2,1)} collective-permute-done((bf16[8,48,1536]{2,1,0:T(8,128)(2,1)}, bf16[8,48,1536]{2,1,0:T(8,128)(2,1)}, u32[]{:S(2)}, u32[]{:S(2)}) %collective-permute-start.19) | collective-permute-done | bytes 1179680 | tf_op jit(solution)/shard_map/last_swap/ppermute | solution.py:53
  88.6 3.4 %mlp.1 = (f32[256,768]{1,0:T(8,128)S(1)}, f32[128,768]{1,0:T(8,128)S(1)}, bf16[256,768]{1,0:T(8,128)(2,1)S(1)}, bf16[256,1536]{1,0:T(8,128)(2,1)S(1)}, f32[256,1...) custom-call(bf16[256,768]{1,0:T(8,128)(2,1)S(1)} %get-tuple-element.265.x_ref, ...), custom_call_target="tpu_custom_call" | custom-call | bytes 11430912 | tf_op jit(solution)/shard_map/mlp/pallas_call | solution.py:148
  92.2 6.0 %collective-permute-done.20.refs_2_ = bf16[4,96,768]{2,1,0:T(8,128)(2,1)S(1)} collective-permute-done((bf16[4,96,768]{2,1,0:T(8,128)(2,1)}, bf16[4,96,768]{2,1,0:T(8,128)(2,1)S(1)}, u32[]{:S(2)}, u32[]{:S(2)}) %collective-permute-start.20) | collective-permute-done | bytes 589856 | tf_op jit(solution)/shard_map/ring_by_1/ppermute | solution.py:44
  109.7 4.7 %collective-permute-done.22.got_ref = bf16[8,96,768]{2,1,0:T(8,128)(2,1)S(1)} collective-permute-done((bf16[8,96,768]{2,1,0:T(8,128)(2,1)S(1)}, bf16[8,96,768]{2,1,0:T(8,128)(2,1)S(1)}, u32[]{:S(2)}, u32[]{:S(2)}) %collective-permute-start.22) | collective-permute-done | bytes 1179680 | tf_op jit(solution)/shard_map/last_swap/ppermute | solution.py:53
  114.7 3.4 %attention_back.1 = (bf16[256,1152]{1,0:T(8,128)(2,1)S(1)}, f32[1,1152]{1,0:T(1,128)S(1)}, f32[128,768]{1,0:T(8,128)S(1)}, f32[128,768]{1,0:T(8,128)S(1)}) custom-call(bf16[256,1152]{1,0:T(8,128)(2,1)S(1)} %get-tuple-element.145.qkv_ref, bf16[256,384]{1,0:T(8,128)(2,1)S(1)} %get-tuple-element.150.att_ref, bf16[256,384]{1,0:T(8,128)(2,1)S(1)} %get-tuple-element.184.d_att_ref, ...), custom_call_target="tpu_custom_call" | custom-call | bytes 4264448 | tf_op jit(solution)/shard_map/attention_back/pallas_call | solution.py:148
  126.2 8.6 %collective-permute-done.27.got_ref = bf16[4,96,768]{2,1,0:T(8,128)(2,1)S(1)} collective-permute-done((bf16[4,96,768]{2,1,0:T(8,128)(2,1)S(1)}, bf16[4,96,768]{2,1,0:T(8,128)(2,1)S(1)}, u32[]{:S(2)}, u32[]{:S(2)}) %collective-permute-start.27) | collective-permute-done | bytes 589856 | tf_op jit(solution)/shard_map/first_swap/ppermute | solution.py:53
  135.9 3.6 %all-to-all-start.2 = ((bf16[16,16,768]{2,1,0:T(8,128)(2,1)}), bf16[16,16,768]{2,1,0:T(8,128)(2,1)S(1)}, u32[]{:S(2)}, u32[]{:S(2)}) async-start(bf16[16,16,768]{2,1,0:T(8,128)(2,1)} %broadcast_in_dim.39), calls=%async_computation.2 | async-start | bytes 786432 | tf_op jit(solution)/shard_map/all_to_all | solution.py:629
  144.9 3.3 %collective-permute-start.31 = (bf16[96,768]{1,0:T(8,128)(2,1)}, bf16[96,768]{1,0:T(8,128)(2,1)}, u32[]{:S(2)}, u32[]{:S(2)}) collective-permute-start(bf16[96,768]{1,0:T(8,128)(2,1)} %bitcast.119), channel_id=1, source_target_pairs={{0,24},{2,26},{4,28},{6,30},{8,0},{10,2},{12,4},{14,6},{16,8},{18,... | collective-permute-start | bytes 442376 | tf_op jit(solution)/shard_map/ring_by_3/ppermute | solution.py:44
  149.4 5.6 %collective-permute-done.30.got_ref = bf16[4,48,1536]{2,1,0:T(8,128)(2,1)} collective-permute-done((bf16[4,48,1536]{2,1,0:T(8,128)(2,1)}, bf16[4,48,1536]{2,1,0:T(8,128)(2,1)}, u32[]{:S(2)}, u32[]{:S(2)}) %collective-permute-start.30) | collective-permute-done | bytes 589856 | tf_op jit(solution)/shard_map/first_swap/ppermute | solution.py:53
  161.9 2.9 %collective-permute-start.38 = (bf16[48,1536]{1,0:T(8,128)(2,1)}, bf16[48,1536]{1,0:T(8,128)(2,1)S(1)}, u32[]{:S(2)}, u32[]{:S(2)}) collective-permute-start(bf16[48,1536]{1,0:T(8,128)(2,1)} %bitcast.120), channel_id=1, source_target_pairs={{0,24},{2,26},{4,28},{6,30},{8,0},{10,2},{12,4},{14,6},{16,8},{18,... | collective-permute-start | bytes 442376 | tf_op jit(solution)/shard_map/ring_by_3/ppermute | solution.py:44
  173.4 4.0 %all-to-all-start.3 = ((f32[32,1,384]{2,1,0:T(1,128)}), f32[32,1,384]{2,1,0:T(1,128)S(1)}, u32[]{:S(2)}, u32[]{:S(2)}) async-start(f32[32,1,384]{2,1,0:T(1,128)} %reshape.296), calls=%async_computation.3 | async-start | bytes 98304 | tf_op jit(solution)/shard_map/all_to_all | solution.py:642
  177.4 3.7 %collective-permute-start.35 = (bf16[48,1536]{1,0:T(8,128)(2,1)S(1)}, bf16[48,1536]{1,0:T(8,128)(2,1)S(1)}, u32[]{:S(2)}, u32[]{:S(2)}) collective-permute-start(bf16[48,1536]{1,0:T(8,128)(2,1)S(1)} %bitcast.123), channel_id=1, source_target_pairs={{0,24},{2,26},{4,28},{6,30},{8,0},{10,2},{12,4},{14,6},{16,8},{18,... | collective-permute-start | bytes 442376 | tf_op jit(solution)/shard_map/ring_by_3/ppermute | solution.py:44
  186.6 8.2 %collective-permute-done.36 = bf16[48,1536]{1,0:T(8,128)(2,1)S(1)} collective-permute-done((bf16[48,1536]{1,0:T(8,128)(2,1)S(1)}, bf16[48,1536]{1,0:T(8,128)(2,1)S(1)}, u32[]{:S(2)}, u32[]{:S(2)}) %collective-permute-start.36) | collective-permute-done | bytes 147488 | tf_op jit(solution)/shard_map/ring_by_2/ppermute | solution.py:44
  (302 shorter events, 93.6 us)
Async XLA Ops:
  4.8 70.3 %collective-permute-start = (bf16[2,128,768]{2,1,0:T(8,128)(2,1)}, bf16[2,128,768]{2,1,0:T(8,128)(2,1)}, u32[]{:S(2)}, u32[]{:S(2)}) collective-permute-start(bf16[2,128,768]{2,1,0:T(8,128)(2,1)} %constant_dynamic-update-slice_fusion), channel_id=1, source_target_pairs={{0,1},{1,0},{2,3},{3,2},{4,5},{5,4},{6,7},{7,6},{8,9},{9,8},{10,11... | collective-permute-start | bytes 1179656 | tf_op jit(solution)/shard_map/ppermute | solution.py:410
  14.8 18.1 %collective-permute-start.9 = (bf16[1,96,768]{2,1,0:T(8,128)(2,1)S(1)}, bf16[1,96,768]{2,1,0:T(8,128)(2,1)S(1)}, u32[]{:S(2)}, u32[]{:S(2)}) collective-permute-start(bf16[1,96,768]{2,1,0:T(8,128)(2,1)S(1)} %bitcast.134), channel_id=1, source_target_pairs={{0,2},{1,5},{2,0},{3,7},{4,6},{5,1},{6,4},{7,3},{8,10},{9,13},{10,... | collective-permute-start | bytes 442376 | tf_op jit(solution)/shard_map/first_swap/ppermute | solution.py:53
  17.2 17.9 %all-to-all-start = ((bf16[32,2,1056]{2,1,0:T(2,128)(2,1)}), bf16[32,2,1056]{2,1,0:T(2,128)(2,1)S(1)}, u32[]{:S(2)}, u32[]{:S(2)}) async-start(bf16[32,2,1056]{2,1,0:T(2,128)(2,1)} %reshape.294), calls=%async_computation | async-start | bytes 294912 | tf_op jit(solution)/shard_map/all_to_all | solution.py:479
  23.9 21.4 %collective-permute-start.11 = (bf16[1,48,1536]{2,1,0:T(8,128)(2,1)S(1)}, bf16[1,48,1536]{2,1,0:T(8,128)(2,1)S(1)}, u32[]{:S(2)}, u32[]{:S(2)}) collective-permute-start(bf16[1,48,1536]{2,1,0:T(8,128)(2,1)S(1)} %bitcast.124), channel_id=1, source_target_pairs={{0,8},{2,10},{4,12},{6,14},{8,16},{10,18},{12,20},{14,22},{16,24},... | collective-permute-start | bytes 442376 | tf_op jit(solution)/shard_map/ring_by_1/ppermute | solution.py:44
  29.2 16.5 %collective-permute-start.12 = (bf16[1,48,1536]{2,1,0:T(8,128)(2,1)S(1)}, bf16[1,48,1536]{2,1,0:T(8,128)(2,1)S(1)}, u32[]{:S(2)}, u32[]{:S(2)}) collective-permute-start(bf16[1,48,1536]{2,1,0:T(8,128)(2,1)S(1)} %bitcast.125), channel_id=1, source_target_pairs={{0,16},{2,18},{4,20},{6,22},{8,24},{10,26},{12,28},{14,30},{16,0},... | collective-permute-start | bytes 442376 | tf_op jit(solution)/shard_map/ring_by_2/ppermute | solution.py:44
  31.1 14.5 %collective-permute-start.13 = (bf16[1,48,1536]{2,1,0:T(8,128)(2,1)S(1)}, bf16[1,48,1536]{2,1,0:T(8,128)(2,1)S(1)}, u32[]{:S(2)}, u32[]{:S(2)}) collective-permute-start(bf16[1,48,1536]{2,1,0:T(8,128)(2,1)S(1)} %bitcast.126), channel_id=1, source_target_pairs={{0,24},{2,26},{4,28},{6,30},{8,0},{10,2},{12,4},{14,6},{16,8},{18,... | collective-permute-start | bytes 442376 | tf_op jit(solution)/shard_map/ring_by_3/ppermute | solution.py:44
  37.2 21.4 %all-to-all-start.1 = ((f32[16,36,128]{2,1,0:T(8,128)}), f32[16,36,128]{2,1,0:T(8,128)S(1)}, u32[]{:S(2)}, u32[]{:S(2)}) async-start(f32[16,36,128]{2,1,0:T(8,128)} %reshape.233), calls=%async_computation.1 | async-start | bytes 655360 | tf_op jit(solution)/shard_map/all_to_all | solution.py:524
  45.2 25.3 %collective-permute-start.8 = (bf16[8,48,1536]{2,1,0:T(8,128)(2,1)}, bf16[8,48,1536]{2,1,0:T(8,128)(2,1)}, u32[]{:S(2)}, u32[]{:S(2)}) collective-permute-start(bf16[8,48,1536]{2,1,0:T(8,128)(2,1)} %constant_dynamic-update-slice_fusion.2), channel_id=1, source_target_pairs={{0,4},{1,3},{2,6},{3,1},{4,0},{5,7},{6,2},{7,5},{8,12},{9,11},{10,... | collective-permute-start | bytes 3538952 | tf_op jit(solution)/shard_map/last_swap/ppermute | solution.py:53
  45.8 17.2 %collective-permute-start.18 = (bf16[4,48,1536]{2,1,0:T(8,128)(2,1)S(1)}, bf16[4,48,1536]{2,1,0:T(8,128)(2,1)S(1)}, u32[]{:S(2)}, u32[]{:S(2)}) collective-permute-start(bf16[4,48,1536]{2,1,0:T(8,128)(2,1)S(1)} %pad_maximum_fusion.2.refs_0_), channel_id=1, source_target_pairs={{0,2},{1,5},{2,0},{3,7},{4,6},{5,1},{6,4},{7,3},{8,10},{9,13},{10,... | collective-permute-start | bytes 1769480 | tf_op jit(solution)/shard_map/first_swap/ppermute | solution.py:53
  54.7 24.0 %collective-permute-start.14 = (bf16[4,96,768]{2,1,0:T(8,128)(2,1)S(1)}, bf16[4,96,768]{2,1,0:T(8,128)(2,1)}, u32[]{:S(2)}, u32[]{:S(2)}) collective-permute-start(bf16[4,96,768]{2,1,0:T(8,128)(2,1)S(1)} %pad_maximum_fusion.1.refs_0_), channel_id=1, source_target_pairs={{0,8},{2,10},{4,12},{6,14},{8,16},{10,18},{12,20},{14,22},{16,24},... | collective-permute-start | bytes 1769480 | tf_op jit(solution)/shard_map/ring_by_1/ppermute | solution.py:44
  56.2 23.9 %collective-permute-start.15 = (bf16[4,96,768]{2,1,0:T(8,128)(2,1)S(1)}, bf16[4,96,768]{2,1,0:T(8,128)(2,1)}, u32[]{:S(2)}, u32[]{:S(2)}) collective-permute-start(bf16[4,96,768]{2,1,0:T(8,128)(2,1)S(1)} %pad_maximum_fusion.1.refs_0_), channel_id=1, source_target_pairs={{0,24},{2,26},{4,28},{6,30},{8,0},{10,2},{12,4},{14,6},{16,8},{18,... | collective-permute-start | bytes 1769480 | tf_op jit(solution)/shard_map/ring_by_3/ppermute | solution.py:44
  70.6 16.5 %collective-permute-start.19 = (bf16[8,48,1536]{2,1,0:T(8,128)(2,1)}, bf16[8,48,1536]{2,1,0:T(8,128)(2,1)}, u32[]{:S(2)}, u32[]{:S(2)}) collective-permute-start(bf16[8,48,1536]{2,1,0:T(8,128)(2,1)} %constant_dynamic-update-slice_fusion.7), channel_id=1, source_target_pairs={{0,4},{1,3},{2,6},{3,1},{4,0},{5,7},{6,2},{7,5},{8,12},{9,11},{10,... | collective-permute-start | bytes 3538952 | tf_op jit(solution)/shard_map/last_swap/ppermute | solution.py:53
  80.7 17.5 %collective-permute-start.20 = (bf16[4,96,768]{2,1,0:T(8,128)(2,1)}, bf16[4,96,768]{2,1,0:T(8,128)(2,1)S(1)}, u32[]{:S(2)}, u32[]{:S(2)}) collective-permute-start(bf16[4,96,768]{2,1,0:T(8,128)(2,1)} %collective-permute-done.14.refs_1_), channel_id=1, source_target_pairs={{0,8},{2,10},{4,12},{6,14},{8,16},{10,18},{12,20},{14,22},{16,24},... | collective-permute-start | bytes 1769480 | tf_op jit(solution)/shard_map/ring_by_1/ppermute | solution.py:44
  98.2 16.2 %collective-permute-start.22 = (bf16[8,96,768]{2,1,0:T(8,128)(2,1)S(1)}, bf16[8,96,768]{2,1,0:T(8,128)(2,1)S(1)}, u32[]{:S(2)}, u32[]{:S(2)}) collective-permute-start(bf16[8,96,768]{2,1,0:T(8,128)(2,1)S(1)} %get-tuple-element.181), channel_id=1, source_target_pairs={{0,4},{1,3},{2,6},{3,1},{4,0},{5,7},{6,2},{7,5},{8,12},{9,11},{10,... | collective-permute-start | bytes 3538952 | tf_op jit(solution)/shard_map/last_swap/ppermute | solution.py:53
  107.5 32.0 %collective-permute-start.29 = (bf16[8,48,1536]{2,1,0:T(8,128)(2,1)}, bf16[8,48,1536]{2,1,0:T(8,128)(2,1)}, u32[]{:S(2)}, u32[]{:S(2)}) collective-permute-start(bf16[8,48,1536]{2,1,0:T(8,128)(2,1)} %get-tuple-element.219), channel_id=1, source_target_pairs={{0,4},{1,3},{2,6},{3,1},{4,0},{5,7},{6,2},{7,5},{8,12},{9,11},{10,... | collective-permute-start | bytes 3538952 | tf_op jit(solution)/shard_map/last_swap/ppermute | solution.py:53
  118.6 16.3 %collective-permute-start.27 = (bf16[4,96,768]{2,1,0:T(8,128)(2,1)S(1)}, bf16[4,96,768]{2,1,0:T(8,128)(2,1)S(1)}, u32[]{:S(2)}, u32[]{:S(2)}) collective-permute-start(bf16[4,96,768]{2,1,0:T(8,128)(2,1)S(1)} %get-tuple-element.208), channel_id=1, source_target_pairs={{0,2},{1,5},{2,0},{3,7},{4,6},{5,1},{6,4},{7,3},{8,10},{9,13},{10,... | collective-permute-start | bytes 1769480 | tf_op jit(solution)/shard_map/first_swap/ppermute | solution.py:53
  122.7 35.5 %collective-permute-start.28 = (bf16[8,48,1536]{2,1,0:T(8,128)(2,1)}, bf16[8,48,1536]{2,1,0:T(8,128)(2,1)S(1)}, u32[]{:S(2)}, u32[]{:S(2)}) collective-permute-start(bf16[8,48,1536]{2,1,0:T(8,128)(2,1)} %get-tuple-element.215), channel_id=1, source_target_pairs={{0,4},{1,3},{2,6},{3,1},{4,0},{5,7},{6,2},{7,5},{8,12},{9,11},{10,... | collective-permute-start | bytes 3538952 | tf_op jit(solution)/shard_map/last_swap/ppermute | solution.py:53
  135.9 24.7 %all-to-all-start.2 = ((bf16[16,16,768]{2,1,0:T(8,128)(2,1)}), bf16[16,16,768]{2,1,0:T(8,128)(2,1)S(1)}, u32[]{:S(2)}, u32[]{:S(2)}) async-start(bf16[16,16,768]{2,1,0:T(8,128)(2,1)} %broadcast_in_dim.39), calls=%async_computation.2 | async-start | bytes 786432 | tf_op jit(solution)/shard_map/all_to_all | solution.py:629
  144.9 15.6 %collective-permute-start.31 = (bf16[96,768]{1,0:T(8,128)(2,1)}, bf16[96,768]{1,0:T(8,128)(2,1)}, u32[]{:S(2)}, u32[]{:S(2)}) collective-permute-start(bf16[96,768]{1,0:T(8,128)(2,1)} %bitcast.119), channel_id=1, source_target_pairs={{0,24},{2,26},{4,28},{6,30},{8,0},{10,2},{12,4},{14,6},{16,8},{18,... | collective-permute-start | bytes 442376 | tf_op jit(solution)/shard_map/ring_by_3/ppermute | solution.py:44
  148.3 24.1 %collective-permute-start.33 = (bf16[96,768]{1,0:T(8,128)(2,1)}, bf16[96,768]{1,0:T(8,128)(2,1)}, u32[]{:S(2)}, u32[]{:S(2)}) collective-permute-start(bf16[96,768]{1,0:T(8,128)(2,1)} %bitcast.116), channel_id=1, source_target_pairs={{0,16},{2,18},{4,20},{6,22},{8,24},{10,26},{12,28},{14,30},{16,0},... | collective-permute-start | bytes 442376 | tf_op jit(solution)/shard_map/ring_by_2/ppermute | solution.py:44
  148.4 24.1 %collective-permute-start.34 = (bf16[96,768]{1,0:T(8,128)(2,1)}, bf16[96,768]{1,0:T(8,128)(2,1)}, u32[]{:S(2)}, u32[]{:S(2)}) collective-permute-start(bf16[96,768]{1,0:T(8,128)(2,1)} %bitcast.115), channel_id=1, source_target_pairs={{0,8},{2,10},{4,12},{6,14},{8,16},{10,18},{12,20},{14,22},{16,24},... | collective-permute-start | bytes 442376 | tf_op jit(solution)/shard_map/ring_by_1/ppermute | solution.py:44
  161.9 19.2 %collective-permute-start.38 = (bf16[48,1536]{1,0:T(8,128)(2,1)}, bf16[48,1536]{1,0:T(8,128)(2,1)S(1)}, u32[]{:S(2)}, u32[]{:S(2)}) collective-permute-start(bf16[48,1536]{1,0:T(8,128)(2,1)} %bitcast.120), channel_id=1, source_target_pairs={{0,24},{2,26},{4,28},{6,30},{8,0},{10,2},{12,4},{14,6},{16,8},{18,... | collective-permute-start | bytes 442376 | tf_op jit(solution)/shard_map/ring_by_3/ppermute | solution.py:44
  164.8 21.8 %collective-permute-start.39 = (bf16[48,1536]{1,0:T(8,128)(2,1)S(1)}, bf16[48,1536]{1,0:T(8,128)(2,1)S(1)}, u32[]{:S(2)}, u32[]{:S(2)}) collective-permute-start(bf16[48,1536]{1,0:T(8,128)(2,1)S(1)} %bitcast.118), channel_id=1, source_target_pairs={{0,16},{2,18},{4,20},{6,22},{8,24},{10,26},{12,28},{14,30},{16,0},... | collective-permute-start | bytes 442376 | tf_op jit(solution)/shard_map/ring_by_2/ppermute | solution.py:44
  170.7 15.9 %collective-permute-start.40 = (bf16[48,1536]{1,0:T(8,128)(2,1)S(1)}, bf16[48,1536]{1,0:T(8,128)(2,1)S(1)}, u32[]{:S(2)}, u32[]{:S(2)}) collective-permute-start(bf16[48,1536]{1,0:T(8,128)(2,1)S(1)} %bitcast.117), channel_id=1, source_target_pairs={{0,8},{2,10},{4,12},{6,14},{8,16},{10,18},{12,20},{14,22},{16,24},... | collective-permute-start | bytes 442376 | tf_op jit(solution)/shard_map/ring_by_1/ppermute | solution.py:44
  (63 other events, 375.1 us)

commit v5 on v4

--- a/solution.py
+++ b/solution.py
@@ -546,13 +546,13 @@
         x, mod, qkv_full, qv_bias,
     )
     parts_2, attended = chips.ring_gather(held_2, False, attended)
+    parts_2[-1], attended = after(parts_2[-1], attended)
     part, proj_full = kernel(
         project_kernel,
         "project",
         [(wide, f32), ((half, D), bf16)],
         attended, proj_mine, proj_got,
     )
-    parts_2[-1], part = after(parts_2[-1], part)
     residual, branch, normed_second, activated, slope, d_mlp, fc2_grad = kernel(
         mlp_kernel,
         "mlp",

time: 201 us -> 202 us (level)
  transfers between devices with their start and end apart: 47 -> 47, of which waited for: 15 -> 16; matrix products, arithmetic and copies ran while one was open for 13% -> 13% of each run, Pallas kernels for 16% -> 16%
where the time goes in v5:
time: 202 us; the launch traced here: 201 us
  starting transfers between devices  66.3 us (33%)
  waiting for transfers between devices  62.3 us (31%)
  local copies, waits for them, and re-layouts  31.4 us (16%)
  Pallas kernels  31.2 us (15%)
  other arithmetic  5.99 us (3%)
  between operations  3.08 us (2%)
    ppermute x12, waiting for transfers between devices, swap(): return lax.ppermute(x, BOTH, pairs)  41.5 us
    ppermute x18, starting transfers between devices, shift(): return lax.ppermute(x, 'fsdp', pairs)  33.1 us
    pallas_call x22, Pallas kernels, kernel(): pl.pallas_call(body, out_shape=shapes, in_specs=[pl.BlockSpec(memory_spac...  31.2 us
    ppermute x18, waiting for transfers between devices, shift(): return lax.ppermute(x, 'fsdp', pairs)  18.3 us
    unnamed x100, local copies, waits for them, and re-layouts  15.8 us
    ppermute x12, starting transfers between devices, swap(): return lax.ppermute(x, BOTH, pairs)  15.8 us
    all_to_all x1, starting transfers between devices, shards(): partial = lax.all_to_all(partial, 'fsdp', 0, 0, tiled=True)  4.36 us
    all_to_all x1, starting transfers between devices, shards(): lax.all_to_all(jnp.broadcast_to(d_embedded[None], (nd, cols, n)), BOTH, 0...  4.14 us
  transfers between devices with their start and end apart: 47, of which 16 were waited for; matrix products, arithmetic and copies ran while one was open for 13% of the time, Pallas kernels for 16%

profile of v5, /device:TPU:0, one launch (start us, length us, event | category | flops | bytes accessed | tf_op | source)
XLA Modules:
  0.0 201.0 jit_solution(4803537521585317165)
XLA Ops:
  7.6 2.6 %collective-permute-start.4 = (bf16[1,48,1536]{2,1,0:T(8,128)(2,1)S(1)}, bf16[1,48,1536]{2,1,0:T(8,128)(2,1)S(1)}, u32[]{:S(2)}, u32[]{:S(2)}) collective-permute-start(bf16[1,48,1536]{2,1,0:T(8,128)(2,1)S(1)} %bitcast.128), channel_id=1, source_target_pairs={{0,8},{2,10},{4,12},{6,14},{8,16},{10,18},{12,20},{14,22},{16,24},... | collective-permute-start | bytes 442376 | tf_op jit(solution)/shard_map/ring_by_1/ppermute | solution.py:44
  10.2 2.6 %collective-permute-start.5 = (bf16[1,48,1536]{2,1,0:T(8,128)(2,1)S(1)}, bf16[1,48,1536]{2,1,0:T(8,128)(2,1)S(1)}, u32[]{:S(2)}, u32[]{:S(2)}) collective-permute-start(bf16[1,48,1536]{2,1,0:T(8,128)(2,1)S(1)} %bitcast.129), channel_id=1, source_target_pairs={{0,16},{2,18},{4,20},{6,22},{8,24},{10,26},{12,28},{14,30},{16,0},... | collective-permute-start | bytes 442376 | tf_op jit(solution)/shard_map/ring_by_2/ppermute | solution.py:44
  17.2 2.6 %all-to-all-start = ((bf16[32,2,1056]{2,1,0:T(2,128)(2,1)}), bf16[32,2,1056]{2,1,0:T(2,128)(2,1)S(1)}, u32[]{:S(2)}, u32[]{:S(2)}) async-start(bf16[32,2,1056]{2,1,0:T(2,128)(2,1)} %reshape.294), calls=%async_computation | async-start | bytes 294912 | tf_op jit(solution)/shard_map/all_to_all | solution.py:479
  19.8 3.3 %collective-permute-done.5 = bf16[1,48,1536]{2,1,0:T(8,128)(2,1)S(1)} collective-permute-done((bf16[1,48,1536]{2,1,0:T(8,128)(2,1)S(1)}, bf16[1,48,1536]{2,1,0:T(8,128)(2,1)S(1)}, u32[]{:S(2)}, u32[]{:S(2)}) %collective-permute-start.5) | collective-permute-done | bytes 147488 | tf_op jit(solution)/shard_map/ring_by_2/ppermute | solution.py:44
  23.9 5.3 %collective-permute-start.11 = (bf16[1,48,1536]{2,1,0:T(8,128)(2,1)S(1)}, bf16[1,48,1536]{2,1,0:T(8,128)(2,1)S(1)}, u32[]{:S(2)}, u32[]{:S(2)}) collective-permute-start(bf16[1,48,1536]{2,1,0:T(8,128)(2,1)S(1)} %bitcast.124), channel_id=1, source_target_pairs={{0,8},{2,10},{4,12},{6,14},{8,16},{10,18},{12,20},{14,22},{16,24},... | collective-permute-start | bytes 442376 | tf_op jit(solution)/shard_map/ring_by_1/ppermute | solution.py:44
  37.2 4.4 %all-to-all-start.1 = ((f32[16,36,128]{2,1,0:T(8,128)}), f32[16,36,128]{2,1,0:T(8,128)S(1)}, u32[]{:S(2)}, u32[]{:S(2)}) async-start(f32[16,36,128]{2,1,0:T(8,128)} %reshape.233), calls=%async_computation.1 | async-start | bytes 655360 | tf_op jit(solution)/shard_map/all_to_all | solution.py:524
  49.8 4.9 %collective-permute-done.10 = bf16[2,96,768]{2,1,0:T(8,128)(2,1)S(1)} collective-permute-done((bf16[2,96,768]{2,1,0:T(8,128)(2,1)S(1)}, bf16[2,96,768]{2,1,0:T(8,128)(2,1)S(1)}, u32[]{:S(2)}, u32[]{:S(2)}) %collective-permute-start.10) | collective-permute-done | bytes 294944 | tf_op jit(solution)/shard_map/last_swap/ppermute | solution.py:53
  56.2 2.4 %collective-permute-start.14 = (bf16[4,96,768]{2,1,0:T(8,128)(2,1)S(1)}, bf16[4,96,768]{2,1,0:T(8,128)(2,1)}, u32[]{:S(2)}, u32[]{:S(2)}) collective-permute-start(bf16[4,96,768]{2,1,0:T(8,128)(2,1)S(1)} %pad_maximum_fusion.1.refs_0_), channel_id=1, source_target_pairs={{0,24},{2,26},{4,28},{6,30},{8,0},{10,2},{12,4},{14,6},{16,8},{18,... | collective-permute-start | bytes 1769480 | tf_op jit(solution)/shard_map/ring_by_3/ppermute | solution.py:44
  58.7 4.3 %collective-permute-done.18.refs_1_ = bf16[4,48,1536]{2,1,0:T(8,128)(2,1)S(1)} collective-permute-done((bf16[4,48,1536]{2,1,0:T(8,128)(2,1)S(1)}, bf16[4,48,1536]{2,1,0:T(8,128)(2,1)S(1)}, u32[]{:S(2)}, u32[]{:S(2)}) %collective-permute-start.18) | collective-permute-done | bytes 589856 | tf_op jit(solution)/shard_map/first_swap/ppermute | solution.py:53
  63.9 6.7 %collective-permute-done.8.refs_2_ = bf16[8,48,1536]{2,1,0:T(8,128)(2,1)} collective-permute-done((bf16[8,48,1536]{2,1,0:T(8,128)(2,1)}, bf16[8,48,1536]{2,1,0:T(8,128)(2,1)}, u32[]{:S(2)}, u32[]{:S(2)}) %collective-permute-start.8) | collective-permute-done | bytes 1179680 | tf_op jit(solution)/shard_map/last_swap/ppermute | solution.py:53
  76.4 2.4 %attention.1 = (bf16[256,768]{1,0:T(8,128)(2,1)S(1)}, bf16[256,1152]{1,0:T(8,128)(2,1)S(1)}, bf16[256,384]{1,0:T(8,128)(2,1)S(1)}, f32[256,128]{1,0:T(8,128)S(1)}) custom-call(bf16[256,768]{1,0:T(8,128)(2,1)S(1)} %get-tuple-element.265.x_ref, f32[6,768]{1,0:T(8,128)S(1)} %reshape.250.mod_ref, bf16[768,1152]{1,0:T(8,128)(2,1)S(1)} %bitcast.104, ...), custom_call_target="tpu_custom_call" | custom-call | bytes 3494912 | tf_op jit(solution)/shard_map/attention/pallas_call | solution.py:148
  82.0 5.1 %collective-permute-done.19.refs_2_ = bf16[8,48,1536]{2,1,0:T(8,128)(2,1)} collective-permute-done((bf16[8,48,1536]{2,1,0:T(8,128)(2,1)}, bf16[8,48,1536]{2,1,0:T(8,128)(2,1)}, u32[]{:S(2)}, u32[]{:S(2)}) %collective-permute-start.19) | collective-permute-done | bytes 1179680 | tf_op jit(solution)/shard_map/last_swap/ppermute | solution.py:53
  88.6 3.4 %mlp.1 = (f32[256,768]{1,0:T(8,128)S(1)}, f32[128,768]{1,0:T(8,128)S(1)}, bf16[256,768]{1,0:T(8,128)(2,1)S(1)}, bf16[256,1536]{1,0:T(8,128)(2,1)S(1)}, f32[256,1...) custom-call(bf16[256,768]{1,0:T(8,128)(2,1)S(1)} %get-tuple-element.265.x_ref, ...), custom_call_target="tpu_custom_call" | custom-call | bytes 11430912 | tf_op jit(solution)/shard_map/mlp/pallas_call | solution.py:148
  92.2 6.3 %collective-permute-done.20.refs_2_ = bf16[4,96,768]{2,1,0:T(8,128)(2,1)S(1)} collective-permute-done((bf16[4,96,768]{2,1,0:T(8,128)(2,1)}, bf16[4,96,768]{2,1,0:T(8,128)(2,1)S(1)}, u32[]{:S(2)}, u32[]{:S(2)}) %collective-permute-start.20) | collective-permute-done | bytes 589856 | tf_op jit(solution)/shard_map/ring_by_1/ppermute | solution.py:44
  110.0 4.7 %collective-permute-done.22.got_ref = bf16[8,96,768]{2,1,0:T(8,128)(2,1)S(1)} collective-permute-done((bf16[8,96,768]{2,1,0:T(8,128)(2,1)S(1)}, bf16[8,96,768]{2,1,0:T(8,128)(2,1)S(1)}, u32[]{:S(2)}, u32[]{:S(2)}) %collective-permute-start.22) | collective-permute-done | bytes 1179680 | tf_op jit(solution)/shard_map/last_swap/ppermute | solution.py:53
  114.9 3.4 %attention_back.1 = (bf16[256,1152]{1,0:T(8,128)(2,1)S(1)}, f32[1,1152]{1,0:T(1,128)S(1)}, f32[128,768]{1,0:T(8,128)S(1)}, f32[128,768]{1,0:T(8,128)S(1)}) custom-call(bf16[256,1152]{1,0:T(8,128)(2,1)S(1)} %get-tuple-element.145.qkv_ref, bf16[256,384]{1,0:T(8,128)(2,1)S(1)} %get-tuple-element.151.att_ref, bf16[256,384]{1,0:T(8,128)(2,1)S(1)} %get-tuple-element.184.d_att_ref, ...), custom_call_target="tpu_custom_call" | custom-call | bytes 4264448 | tf_op jit(solution)/shard_map/attention_back/pallas_call | solution.py:148
  127.1 8.0 %collective-permute-done.27.got_ref = bf16[4,96,768]{2,1,0:T(8,128)(2,1)S(1)} collective-permute-done((bf16[4,96,768]{2,1,0:T(8,128)(2,1)S(1)}, bf16[4,96,768]{2,1,0:T(8,128)(2,1)S(1)}, u32[]{:S(2)}, u32[]{:S(2)}) %collective-permute-start.27) | collective-permute-done | bytes 589856 | tf_op jit(solution)/shard_map/first_swap/ppermute | solution.py:53
  136.2 3.6 %all-to-all-start.2 = ((bf16[16,16,768]{2,1,0:T(8,128)(2,1)}), bf16[16,16,768]{2,1,0:T(8,128)(2,1)S(1)}, u32[]{:S(2)}, u32[]{:S(2)}) async-start(bf16[16,16,768]{2,1,0:T(8,128)(2,1)} %broadcast_in_dim.39), calls=%async_computation.2 | async-start | bytes 786432 | tf_op jit(solution)/shard_map/all_to_all | solution.py:629
  145.2 3.3 %collective-permute-start.31 = (bf16[96,768]{1,0:T(8,128)(2,1)}, bf16[96,768]{1,0:T(8,128)(2,1)}, u32[]{:S(2)}, u32[]{:S(2)}) collective-permute-start(bf16[96,768]{1,0:T(8,128)(2,1)} %bitcast.119), channel_id=1, source_target_pairs={{0,24},{2,26},{4,28},{6,30},{8,0},{10,2},{12,4},{14,6},{16,8},{18,... | collective-permute-start | bytes 442376 | tf_op jit(solution)/shard_map/ring_by_3/ppermute | solution.py:44
  149.7 5.7 %collective-permute-done.30.got_ref = bf16[4,48,1536]{2,1,0:T(8,128)(2,1)} collective-permute-done((bf16[4,48,1536]{2,1,0:T(8,128)(2,1)}, bf16[4,48,1536]{2,1,0:T(8,128)(2,1)}, u32[]{:S(2)}, u32[]{:S(2)}) %collective-permute-start.30) | collective-permute-done | bytes 589856 | tf_op jit(solution)/shard_map/first_swap/ppermute | solution.py:53
  162.1 2.9 %collective-permute-start.38 = (bf16[48,1536]{1,0:T(8,128)(2,1)}, bf16[48,1536]{1,0:T(8,128)(2,1)S(1)}, u32[]{:S(2)}, u32[]{:S(2)}) collective-permute-start(bf16[48,1536]{1,0:T(8,128)(2,1)} %bitcast.120), channel_id=1, source_target_pairs={{0,24},{2,26},{4,28},{6,30},{8,0},{10,2},{12,4},{14,6},{16,8},{18,... | collective-permute-start | bytes 442376 | tf_op jit(solution)/shard_map/ring_by_3/ppermute | solution.py:44
  173.7 4.1 %all-to-all-start.3 = ((f32[32,1,384]{2,1,0:T(1,128)}), f32[32,1,384]{2,1,0:T(1,128)S(1)}, u32[]{:S(2)}, u32[]{:S(2)}) async-start(f32[32,1,384]{2,1,0:T(1,128)} %reshape.296), calls=%async_computation.3 | async-start | bytes 98304 | tf_op jit(solution)/shard_map/all_to_all | solution.py:642
  177.8 3.7 %collective-permute-start.35 = (bf16[48,1536]{1,0:T(8,128)(2,1)S(1)}, bf16[48,1536]{1,0:T(8,128)(2,1)S(1)}, u32[]{:S(2)}, u32[]{:S(2)}) collective-permute-start(bf16[48,1536]{1,0:T(8,128)(2,1)S(1)} %bitcast.123), channel_id=1, source_target_pairs={{0,24},{2,26},{4,28},{6,30},{8,0},{10,2},{12,4},{14,6},{16,8},{18,... | collective-permute-start | bytes 442376 | tf_op jit(solution)/shard_map/ring_by_3/ppermute | solution.py:44
  187.1 8.2 %collective-permute-done.36 = bf16[48,1536]{1,0:T(8,128)(2,1)S(1)} collective-permute-done((bf16[48,1536]{1,0:T(8,128)(2,1)S(1)}, bf16[48,1536]{1,0:T(8,128)(2,1)S(1)}, u32[]{:S(2)}, u32[]{:S(2)}) %collective-permute-start.36) | collective-permute-done | bytes 147488 | tf_op jit(solution)/shard_map/ring_by_2/ppermute | solution.py:44
  (302 shorter events, 94.1 us)
Async XLA Ops:
  4.8 70.3 %collective-permute-start = (bf16[2,128,768]{2,1,0:T(8,128)(2,1)}, bf16[2,128,768]{2,1,0:T(8,128)(2,1)}, u32[]{:S(2)}, u32[]{:S(2)}) collective-permute-start(bf16[2,128,768]{2,1,0:T(8,128)(2,1)} %constant_dynamic-update-slice_fusion), channel_id=1, source_target_pairs={{0,1},{1,0},{2,3},{3,2},{4,5},{5,4},{6,7},{7,6},{8,9},{9,8},{10,11... | collective-permute-start | bytes 1179656 | tf_op jit(solution)/shard_map/ppermute | solution.py:410
  14.8 18.1 %collective-permute-start.9 = (bf16[1,96,768]{2,1,0:T(8,128)(2,1)S(1)}, bf16[1,96,768]{2,1,0:T(8,128)(2,1)S(1)}, u32[]{:S(2)}, u32[]{:S(2)}) collective-permute-start(bf16[1,96,768]{2,1,0:T(8,128)(2,1)S(1)} %bitcast.134), channel_id=1, source_target_pairs={{0,2},{1,5},{2,0},{3,7},{4,6},{5,1},{6,4},{7,3},{8,10},{9,13},{10,... | collective-permute-start | bytes 442376 | tf_op jit(solution)/shard_map/first_swap/ppermute | solution.py:53
  17.2 17.9 %all-to-all-start = ((bf16[32,2,1056]{2,1,0:T(2,128)(2,1)}), bf16[32,2,1056]{2,1,0:T(2,128)(2,1)S(1)}, u32[]{:S(2)}, u32[]{:S(2)}) async-start(bf16[32,2,1056]{2,1,0:T(2,128)(2,1)} %reshape.294), calls=%async_computation | async-start | bytes 294912 | tf_op jit(solution)/shard_map/all_to_all | solution.py:479
  23.9 21.4 %collective-permute-start.11 = (bf16[1,48,1536]{2,1,0:T(8,128)(2,1)S(1)}, bf16[1,48,1536]{2,1,0:T(8,128)(2,1)S(1)}, u32[]{:S(2)}, u32[]{:S(2)}) collective-permute-start(bf16[1,48,1536]{2,1,0:T(8,128)(2,1)S(1)} %bitcast.124), channel_id=1, source_target_pairs={{0,8},{2,10},{4,12},{6,14},{8,16},{10,18},{12,20},{14,22},{16,24},... | collective-permute-start | bytes 442376 | tf_op jit(solution)/shard_map/ring_by_1/ppermute | solution.py:44
  29.2 16.5 %collective-permute-start.12 = (bf16[1,48,1536]{2,1,0:T(8,128)(2,1)S(1)}, bf16[1,48,1536]{2,1,0:T(8,128)(2,1)S(1)}, u32[]{:S(2)}, u32[]{:S(2)}) collective-permute-start(bf16[1,48,1536]{2,1,0:T(8,128)(2,1)S(1)} %bitcast.125), channel_id=1, source_target_pairs={{0,16},{2,18},{4,20},{6,22},{8,24},{10,26},{12,28},{14,30},{16,0},... | collective-permute-start | bytes 442376 | tf_op jit(solution)/shard_map/ring_by_2/ppermute | solution.py:44
  31.1 14.5 %collective-permute-start.13 = (bf16[1,48,1536]{2,1,0:T(8,128)(2,1)S(1)}, bf16[1,48,1536]{2,1,0:T(8,128)(2,1)S(1)}, u32[]{:S(2)}, u32[]{:S(2)}) collective-permute-start(bf16[1,48,1536]{2,1,0:T(8,128)(2,1)S(1)} %bitcast.126), channel_id=1, source_target_pairs={{0,24},{2,26},{4,28},{6,30},{8,0},{10,2},{12,4},{14,6},{16,8},{18,... | collective-permute-start | bytes 442376 | tf_op jit(solution)/shard_map/ring_by_3/ppermute | solution.py:44
  37.2 21.4 %all-to-all-start.1 = ((f32[16,36,128]{2,1,0:T(8,128)}), f32[16,36,128]{2,1,0:T(8,128)S(1)}, u32[]{:S(2)}, u32[]{:S(2)}) async-start(f32[16,36,128]{2,1,0:T(8,128)} %reshape.233), calls=%async_computation.1 | async-start | bytes 655360 | tf_op jit(solution)/shard_map/all_to_all | solution.py:524
  45.2 25.3 %collective-permute-start.8 = (bf16[8,48,1536]{2,1,0:T(8,128)(2,1)}, bf16[8,48,1536]{2,1,0:T(8,128)(2,1)}, u32[]{:S(2)}, u32[]{:S(2)}) collective-permute-start(bf16[8,48,1536]{2,1,0:T(8,128)(2,1)} %constant_dynamic-update-slice_fusion.2), channel_id=1, source_target_pairs={{0,4},{1,3},{2,6},{3,1},{4,0},{5,7},{6,2},{7,5},{8,12},{9,11},{10,... | collective-permute-start | bytes 3538952 | tf_op jit(solution)/shard_map/last_swap/ppermute | solution.py:53
  45.8 17.2 %collective-permute-start.18 = (bf16[4,48,1536]{2,1,0:T(8,128)(2,1)S(1)}, bf16[4,48,1536]{2,1,0:T(8,128)(2,1)S(1)}, u32[]{:S(2)}, u32[]{:S(2)}) collective-permute-start(bf16[4,48,1536]{2,1,0:T(8,128)(2,1)S(1)} %pad_maximum_fusion.2.refs_0_), channel_id=1, source_target_pairs={{0,2},{1,5},{2,0},{3,7},{4,6},{5,1},{6,4},{7,3},{8,10},{9,13},{10,... | collective-permute-start | bytes 1769480 | tf_op jit(solution)/shard_map/first_swap/ppermute | solution.py:53
  54.7 24.0 %collective-permute-start.15 = (bf16[4,96,768]{2,1,0:T(8,128)(2,1)S(1)}, bf16[4,96,768]{2,1,0:T(8,128)(2,1)}, u32[]{:S(2)}, u32[]{:S(2)}) collective-permute-start(bf16[4,96,768]{2,1,0:T(8,128)(2,1)S(1)} %pad_maximum_fusion.1.refs_0_), channel_id=1, source_target_pairs={{0,8},{2,10},{4,12},{6,14},{8,16},{10,18},{12,20},{14,22},{16,24},... | collective-permute-start | bytes 1769480 | tf_op jit(solution)/shard_map/ring_by_1/ppermute | solution.py:44
  56.2 23.1 %collective-permute-start.14 = (bf16[4,96,768]{2,1,0:T(8,128)(2,1)S(1)}, bf16[4,96,768]{2,1,0:T(8,128)(2,1)}, u32[]{:S(2)}, u32[]{:S(2)}) collective-permute-start(bf16[4,96,768]{2,1,0:T(8,128)(2,1)S(1)} %pad_maximum_fusion.1.refs_0_), channel_id=1, source_target_pairs={{0,24},{2,26},{4,28},{6,30},{8,0},{10,2},{12,4},{14,6},{16,8},{18,... | collective-permute-start | bytes 1769480 | tf_op jit(solution)/shard_map/ring_by_3/ppermute | solution.py:44
  70.6 16.5 %collective-permute-start.19 = (bf16[8,48,1536]{2,1,0:T(8,128)(2,1)}, bf16[8,48,1536]{2,1,0:T(8,128)(2,1)}, u32[]{:S(2)}, u32[]{:S(2)}) collective-permute-start(bf16[8,48,1536]{2,1,0:T(8,128)(2,1)} %constant_dynamic-update-slice_fusion.7), channel_id=1, source_target_pairs={{0,4},{1,3},{2,6},{3,1},{4,0},{5,7},{6,2},{7,5},{8,12},{9,11},{10,... | collective-permute-start | bytes 3538952 | tf_op jit(solution)/shard_map/last_swap/ppermute | solution.py:53
  80.7 17.7 %collective-permute-start.20 = (bf16[4,96,768]{2,1,0:T(8,128)(2,1)}, bf16[4,96,768]{2,1,0:T(8,128)(2,1)S(1)}, u32[]{:S(2)}, u32[]{:S(2)}) collective-permute-start(bf16[4,96,768]{2,1,0:T(8,128)(2,1)} %collective-permute-done.15.refs_1_), channel_id=1, source_target_pairs={{0,8},{2,10},{4,12},{6,14},{8,16},{10,18},{12,20},{14,22},{16,24},... | collective-permute-start | bytes 1769480 | tf_op jit(solution)/shard_map/ring_by_1/ppermute | solution.py:44
  98.5 16.2 %collective-permute-start.22 = (bf16[8,96,768]{2,1,0:T(8,128)(2,1)S(1)}, bf16[8,96,768]{2,1,0:T(8,128)(2,1)S(1)}, u32[]{:S(2)}, u32[]{:S(2)}) collective-permute-start(bf16[8,96,768]{2,1,0:T(8,128)(2,1)S(1)} %get-tuple-element.181), channel_id=1, source_target_pairs={{0,4},{1,3},{2,6},{3,1},{4,0},{5,7},{6,2},{7,5},{8,12},{9,11},{10,... | collective-permute-start | bytes 3538952 | tf_op jit(solution)/shard_map/last_swap/ppermute | solution.py:53
  108.4 31.4 %collective-permute-start.29 = (bf16[8,48,1536]{2,1,0:T(8,128)(2,1)}, bf16[8,48,1536]{2,1,0:T(8,128)(2,1)}, u32[]{:S(2)}, u32[]{:S(2)}) collective-permute-start(bf16[8,48,1536]{2,1,0:T(8,128)(2,1)} %get-tuple-element.219), channel_id=1, source_target_pairs={{0,4},{1,3},{2,6},{3,1},{4,0},{5,7},{6,2},{7,5},{8,12},{9,11},{10,... | collective-permute-start | bytes 3538952 | tf_op jit(solution)/shard_map/last_swap/ppermute | solution.py:53
  118.9 16.3 %collective-permute-start.27 = (bf16[4,96,768]{2,1,0:T(8,128)(2,1)S(1)}, bf16[4,96,768]{2,1,0:T(8,128)(2,1)S(1)}, u32[]{:S(2)}, u32[]{:S(2)}) collective-permute-start(bf16[4,96,768]{2,1,0:T(8,128)(2,1)S(1)} %get-tuple-element.208), channel_id=1, source_target_pairs={{0,2},{1,5},{2,0},{3,7},{4,6},{5,1},{6,4},{7,3},{8,10},{9,13},{10,... | collective-permute-start | bytes 1769480 | tf_op jit(solution)/shard_map/first_swap/ppermute | solution.py:53
  123.0 35.5 %collective-permute-start.28 = (bf16[8,48,1536]{2,1,0:T(8,128)(2,1)}, bf16[8,48,1536]{2,1,0:T(8,128)(2,1)S(1)}, u32[]{:S(2)}, u32[]{:S(2)}) collective-permute-start(bf16[8,48,1536]{2,1,0:T(8,128)(2,1)} %get-tuple-element.215), channel_id=1, source_target_pairs={{0,4},{1,3},{2,6},{3,1},{4,0},{5,7},{6,2},{7,5},{8,12},{9,11},{10,... | collective-permute-start | bytes 3538952 | tf_op jit(solution)/shard_map/last_swap/ppermute | solution.py:53
  136.2 24.7 %all-to-all-start.2 = ((bf16[16,16,768]{2,1,0:T(8,128)(2,1)}), bf16[16,16,768]{2,1,0:T(8,128)(2,1)S(1)}, u32[]{:S(2)}, u32[]{:S(2)}) async-start(bf16[16,16,768]{2,1,0:T(8,128)(2,1)} %broadcast_in_dim.39), calls=%async_computation.2 | async-start | bytes 786432 | tf_op jit(solution)/shard_map/all_to_all | solution.py:629
  145.2 15.7 %collective-permute-start.31 = (bf16[96,768]{1,0:T(8,128)(2,1)}, bf16[96,768]{1,0:T(8,128)(2,1)}, u32[]{:S(2)}, u32[]{:S(2)}) collective-permute-start(bf16[96,768]{1,0:T(8,128)(2,1)} %bitcast.119), channel_id=1, source_target_pairs={{0,24},{2,26},{4,28},{6,30},{8,0},{10,2},{12,4},{14,6},{16,8},{18,... | collective-permute-start | bytes 442376 | tf_op jit(solution)/shard_map/ring_by_3/ppermute | solution.py:44
  148.6 24.1 %collective-permute-start.33 = (bf16[96,768]{1,0:T(8,128)(2,1)}, bf16[96,768]{1,0:T(8,128)(2,1)}, u32[]{:S(2)}, u32[]{:S(2)}) collective-permute-start(bf16[96,768]{1,0:T(8,128)(2,1)} %bitcast.116), channel_id=1, source_target_pairs={{0,16},{2,18},{4,20},{6,22},{8,24},{10,26},{12,28},{14,30},{16,0},... | collective-permute-start | bytes 442376 | tf_op jit(solution)/shard_map/ring_by_2/ppermute | solution.py:44
  148.6 24.1 %collective-permute-start.34 = (bf16[96,768]{1,0:T(8,128)(2,1)}, bf16[96,768]{1,0:T(8,128)(2,1)}, u32[]{:S(2)}, u32[]{:S(2)}) collective-permute-start(bf16[96,768]{1,0:T(8,128)(2,1)} %bitcast.115), channel_id=1, source_target_pairs={{0,8},{2,10},{4,12},{6,14},{8,16},{10,18},{12,20},{14,22},{16,24},... | collective-permute-start | bytes 442376 | tf_op jit(solution)/shard_map/ring_by_1/ppermute | solution.py:44
  162.1 19.4 %collective-permute-start.38 = (bf16[48,1536]{1,0:T(8,128)(2,1)}, bf16[48,1536]{1,0:T(8,128)(2,1)S(1)}, u32[]{:S(2)}, u32[]{:S(2)}) collective-permute-start(bf16[48,1536]{1,0:T(8,128)(2,1)} %bitcast.120), channel_id=1, source_target_pairs={{0,24},{2,26},{4,28},{6,30},{8,0},{10,2},{12,4},{14,6},{16,8},{18,... | collective-permute-start | bytes 442376 | tf_op jit(solution)/shard_map/ring_by_3/ppermute | solution.py:44
  165.1 22.0 %collective-permute-start.39 = (bf16[48,1536]{1,0:T(8,128)(2,1)S(1)}, bf16[48,1536]{1,0:T(8,128)(2,1)S(1)}, u32[]{:S(2)}, u32[]{:S(2)}) collective-permute-start(bf16[48,1536]{1,0:T(8,128)(2,1)S(1)} %bitcast.118), channel_id=1, source_target_pairs={{0,16},{2,18},{4,20},{6,22},{8,24},{10,26},{12,28},{14,30},{16,0},... | collective-permute-start | bytes 442376 | tf_op jit(solution)/shard_map/ring_by_2/ppermute | solution.py:44
  171.0 16.0 %collective-permute-start.40 = (bf16[48,1536]{1,0:T(8,128)(2,1)S(1)}, bf16[48,1536]{1,0:T(8,128)(2,1)S(1)}, u32[]{:S(2)}, u32[]{:S(2)}) collective-permute-start(bf16[48,1536]{1,0:T(8,128)(2,1)S(1)} %bitcast.117), channel_id=1, source_target_pairs={{0,8},{2,10},{4,12},{6,14},{8,16},{10,18},{12,20},{14,22},{16,24},... | collective-permute-start | bytes 442376 | tf_op jit(solution)/shard_map/ring_by_1/ppermute | solution.py:44
  (63 other events, 376.6 us)
